TPU v7x, 32 devices: a whole 2x2x4 slice. The times are simulated.
32 devices in a mesh: replica: 4 (over y, x), shard: 8 (over z, core).
Axes of the slice: x: 2, y: 2, z: 4, core: 2. Of those that a mesh axis runs over, the one named last changes fastest.
Arguments:
- table: float32 [2048, 1024], P('shard'), may hold values from -6 to 6
- accum: float32 [2048], P('shard'), may hold values from 0.0001 to 0.01
- owner: int32 [8192, 1], P(('replica', 'shard')), may hold values from 0 to 7; in each aligned block of 256 rows (0 to 255, 256 to 511, ...) at most 64 rows name the same one
- local_row: int32 [8192], P(('replica', 'shard')), may hold values from 0 to 255
- lengths: int32 [32, 4], P(('replica', 'shard')), may hold values from 1 to 128, 256 in all within a row
- queries: bfloat16 [8192, 512], P(('replica', 'shard')), may hold values from -6 to 6
- keys: bfloat16 [8192, 512], P(('replica', 'shard')), may hold values from -6 to 6
- cotangent: bfloat16 [8192, 1024], P(('replica', 'shard')), may hold values from -6 to 6
- out_weight: bfloat16 [1024, 1024], P('shard'), may hold values from -0.1875 to 0.1875
Outputs:
- new_table: float32 [2048, 1024], P('shard')
- new_accum: float32 [2048], P('shard')
- weight_grad: bfloat16 [1024, 1024], P('shard')
Inputs may be any that keep to these rules, and one draw needn't show every extreme that they name: Among the 256 tokens of one device no owner is named more than 64 times; in every draw some owner is named exactly 64 times by some device's tokens. Each row holds positive lengths that sum to 256; the largest of each row is 128.
All inputs are finite; a program needn't handle non-finite values.
Results may differ from a plain program's by a relative error of at most 0.0064.
Values may be sent and summed in bfloat16 or wider, within the bound.
No kernel may reach another device: no remote copies, remote signals or barrier semaphores. Data moves between devices by JAX's collectives and lax.ppermute only.
A program may use at most 64 MiB of HBM per device.

v0:
```python
import jax
import jax.numpy as jnp
from jax import lax
from jax.sharding import PartitionSpec as P

HEADS = 8
MAXLEN = 128


def adagrad(table_rows, accum_rows, grad_rows):
    new_accum = accum_rows + jnp.mean(grad_rows * grad_rows, axis=1)
    new_table = table_rows - 1.0 * grad_rows / (jnp.sqrt(new_accum)[:, None] + 1e-08)
    return (new_table, new_accum)


def body(table, accum, owner, local_row, lengths, queries, keys, cotangent, out_weight):
    shards = lax.axis_size("shard")
    tok = owner.shape[0]
    rows_dev = table.shape[0]
    width = table.shape[1]
    heads = HEADS
    dqk = queries.shape[1] // heads
    dval = width // heads
    slots = 2 * tok // shards
    dest = owner[:, 0]
    onehot = (dest[:, None] == jnp.arange(shards)[None, :]).astype(jnp.bfloat16)
    pos = jnp.arange(tok)
    lower = (pos[None, :] < pos[:, None]).astype(jnp.bfloat16)
    before = jnp.dot(lower, onehot, preferred_element_type=jnp.float32)
    rank = jnp.sum(before * onehot.astype(jnp.float32), axis=1).astype(jnp.int32)
    slot = dest * slots + rank
    send_idx = (
        jnp.full((shards * slots,), -1, jnp.int32).at[slot].set(local_row).reshape(shards, slots)
    )
    recv_idx = lax.all_to_all(send_idx, "shard", split_axis=0, concat_axis=0, tiled=True).reshape(
        -1
    )
    valid = recv_idx >= 0
    picked = jnp.take(table, jnp.clip(recv_idx, 0, rows_dev - 1), axis=0)
    picked = (
        jnp.where(valid[:, None], picked, 0.0).astype(jnp.bfloat16).reshape(shards, slots, width)
    )
    ends = jnp.cumsum(lengths[0])
    seg = jnp.sum((pos[:, None] >= ends[None, :]).astype(jnp.int32), axis=1)
    mask = ((seg[:, None] == seg[None, :]) & (pos[None, :] <= pos[:, None])).astype(jnp.float32)
    q3 = queries.reshape(tok, heads, dqk)
    k3 = keys.reshape(tok, heads, dqk)
    scores = jnp.einsum("ihd,jhd->hij", q3, k3, preferred_element_type=jnp.float32) * dqk ** (-0.5)
    weights = (jax.nn.silu(scores) / MAXLEN * mask[None]).astype(jnp.bfloat16)
    fetched = lax.all_to_all(picked, "shard", split_axis=0, concat_axis=0, tiled=True).reshape(
        shards * slots, width
    )
    embedded = fetched[slot]
    vals = embedded.reshape(tok, heads, dval)
    mixed = (
        jnp.einsum("hij,jhd->ihd", weights, vals, preferred_element_type=jnp.float32)
        .reshape(tok, width)
        .astype(jnp.bfloat16)
    )
    back = lax.dot_general(
        cotangent,
        lax.all_gather(out_weight, "shard", axis=0, tiled=True),
        (((1,), (1,)), ((), ())),
        preferred_element_type=jnp.float32,
    ).astype(jnp.bfloat16)
    grad_share = lax.psum_scatter(
        lax.dot_general(
            mixed, cotangent, (((0,), (0,)), ((), ())), preferred_element_type=jnp.float32
        ),
        "shard",
        scatter_dimension=0,
        tiled=True,
    )
    weight_grad = lax.psum(grad_share, "replica").astype(jnp.bfloat16)
    b3 = back.reshape(tok, heads, dval)
    token_grad = jnp.einsum(
        "hij,ihd->jhd", weights, b3, preferred_element_type=jnp.float32
    ).reshape(tok, width)
    send_grad = (
        jnp.zeros((shards * slots, width), jnp.float32)
        .at[slot]
        .set(token_grad)
        .reshape(shards, slots, width)
    )
    arrived = (
        lax.all_to_all(
            send_grad.astype(jnp.bfloat16), "shard", split_axis=0, concat_axis=0, tiled=True
        )
        .astype(send_grad.dtype)
        .reshape(shards * slots, width)
    )
    select = (recv_idx[:, None] == jnp.arange(rows_dev)[None, :]).astype(jnp.float32)
    grad_rows = lax.dot_general(
        select,
        arrived,
        (((0,), (0,)), ((), ())),
        precision=lax.Precision.HIGHEST,
        preferred_element_type=jnp.float32,
    )
    share = lax.psum_scatter(
        grad_rows.astype(jnp.bfloat16), "replica", scatter_dimension=0, tiled=True
    ).astype(jnp.float32)
    quarter = share.shape[0]
    first = lax.axis_index("replica") * quarter
    part_table = lax.dynamic_slice_in_dim(table, first, quarter, 0)
    part_accum = lax.dynamic_slice_in_dim(accum, first, quarter, 0)
    upd_table, upd_accum = adagrad(part_table, part_accum, share)
    new_table, new_accum = (
        lax.all_gather(upd_table, "replica", axis=0, tiled=True),
        lax.all_gather(upd_accum, "replica", axis=0, tiled=True),
    )
    return (new_table, new_accum, weight_grad)


def solution(mesh):
    placed = (
        P("shard", None),
        P("shard"),
        P(("replica", "shard"), None),
        P(("replica", "shard")),
        P(("replica", "shard"), None),
        P(("replica", "shard"), None),
        P(("replica", "shard"), None),
        P(("replica", "shard"), None),
        P("shard", None),
    )
    return jax.shard_map(
        body,
        mesh=mesh,
        in_specs=placed,
        out_specs=(P("shard", None), P("shard"), P("shard", None)),
        check_vma=False,
    )
```

profile of v0, /device:TPU:0, one launch (start us, length us, event | category | flops | bytes accessed | tf_op | source)
XLA Modules:
  0.0 222.2 jit_solution(11168392712295051595)
XLA Ops:
  7.2 0.0 all-gather.3.cloned.1.call-start
  7.2 0.7 all-gather.3.cloned.1.call-update
  7.9 0.9 fusion
  8.9 0.7 compare_select_fusion.2
  9.6 1.6 scatter_custom_fusion
  11.1 0.7 all_to_all.12
  11.8 6.3 %all-to-all-start = ((s32[8,1,64]{2,1,0:T(1,128)}), s32[8,1,64]{2,1,0:T(1,128)S(1)}, u32[]{:S(2)}, u32[]{:S(2)}) async-start(s32[8,1,64]{2,1,0:T(1,128)} %all_to_all.12), calls=%async_computation | async-start | bytes 8192 | tf_op jit(solution)/shard_map/all_to_all | solution.py:35
  18.1 1.1 copy.33
  19.2 1.1 copy.34
  20.3 0.8 reduce-window.8
  21.2 0.1 convert_reduce_fusion
  21.2 0.1 fusion.7
  21.3 0.8 multiply_convert_fusion
  22.2 19.3 %all-gather.3.cloned.1.call-done = bf16[1024,1024]{1,0:T(8,128)(2,1)} async-done(((bf16[128,1024]{1,0:T(8,128)(2,1)}), bf16[1024,1024]{1,0:T(8,128)(2,1)}) %all-gather.3.cloned.1.call-update) | async-done | bytes 2097168 | tf_op jit(solution)/shard_map/all_gather | solution.py:62
  41.5 2.3 %convolution_convert_fusion.2 = bf16[256,1024]{1,0:T(8,128)(2,1)S(1)} fusion(bf16[256,1024]{1,0:T(8,128)(2,1)S(1)} %copy-done, bf16[1024,1024]{1,0:T(8,128)(2,1)} %all-gather.3.cloned.1.call-done), kind=kOutput, calls=%fused_computation.8 | convolution fusion | flops 537133056 | bytes 3145728 | tf_op jit(solution)/shard_map/dot_general | solution.py:60
  43.8 0.2 copy.40
  44.1 0.3 fusion.13
  44.4 1.3 copy.36
  45.7 2.6 %scatter_custom_fusion.1 = f32[512,1024]{1,0:T(8,128)S(1)} fusion(s32[256]{0:T(256)S(1)} %bitcast.57, f32[256,1024]{1,0:T(8,128)} %copy.36, f32[]{:T(128)} %constant.19.clone.1), kind=kCustom, calls=%fused_computation.11 | custom fusion | bytes 2097664 | tf_op jit(solution)/shard_map/scatter | solution.py:82
  48.3 1.1 convert_element_type.71
  49.4 3.7 %all-to-all-start.1 = ((bf16[8,64,1024]{2,1,0:T(8,128)(2,1)}), bf16[8,64,1024]{2,1,0:T(8,128)(2,1)S(1)}, u32[]{:S(2)}, u32[]{:S(2)}) async-start(bf16[8,64,1024]{2,1,0:T(8,128)(2,1)} %bitcast.44), calls=%async_computation.1 | async-start | bytes 2097152 | tf_op jit(solution)/shard_map/all_to_all | solution.py:86
  53.1 0.0 reduce-scatter.3.cloned.1.call-start
  53.2 0.5 broadcast.129
  53.7 0.7 reduce.3
  54.4 0.1 eq.51
  54.4 0.1 min.18
  54.5 25.1 %all-to-all-done.1 = bf16[8,64,1024]{2,1,0:T(8,128)(2,1)S(1)} async-done(((bf16[8,64,1024]{2,1,0:T(8,128)(2,1)}), bf16[8,64,1024]{2,1,0:T(8,128)(2,1)S(1)}, u32[]{:S(2)}, u32[]{:S(2)}) %all-to-all-start.1) | async-done | bytes 1048608 | tf_op jit(solution)/shard_map/all_to_all | solution.py:86
  79.6 1.4 convolution_convert_fusion
  81.0 0.0 reduce-scatter.3.cloned.1.call-update
  81.1 1.8 gather_fusion
  82.9 1.3 select_convert_fusion
  84.2 3.6 %all-to-all-start.2 = ((bf16[8,64,1024]{2,1,0:T(8,128)(2,1)}), bf16[8,64,1024]{2,1,0:T(8,128)(2,1)S(1)}, u32[]{:S(2)}, u32[]{:S(2)}) async-start(bf16[8,64,1024]{2,1,0:T(8,128)(2,1)} %select_convert_fusion), calls=%async_computation.3 | async-start | bytes 2097152 | tf_op jit(solution)/shard_map/all_to_all | solution.py:50
  87.8 0.0 all-gather.5.cloned.1.call-start
  87.9 0.6 dynamic-slice
  89.1 15.7 %reduce-scatter.3.cloned.1.call-done = bf16[64,1024]{1,0:T(8,128)(2,1)} async-done(((bf16[256,1024]{1,0:T(8,128)(2,1)}), bf16[64,1024]{1,0:T(8,128)(2,1)}) %reduce-scatter.3.cloned.1.call-update) | async-done | bytes 131088 | tf_op jit(solution)/shard_map/reduce_scatter | solution.py:100
  104.8 1.0 fusion.3
  105.8 0.2 fusion.12
  106.0 1.7 fusion.4
  107.7 0.0 reduce-scatter.5.cloned.1.call-start
  107.8 6.5 %all-to-all-done.2 = bf16[8,64,1024]{2,1,0:T(8,128)(2,1)S(1)} async-done(((bf16[8,64,1024]{2,1,0:T(8,128)(2,1)}), bf16[8,64,1024]{2,1,0:T(8,128)(2,1)S(1)}, u32[]{:S(2)}, u32[]{:S(2)}) %all-to-all-start.2) | async-done | bytes 1048608 | tf_op jit(solution)/shard_map/all_to_all | solution.py:50
  114.3 1.2 gather_fusion.1
  115.5 0.2 copy.41
  115.7 0.5 convolution_convert_fusion.1
  116.2 2.6 %fusion.14 = f32[1024,1024]{1,0:T(8,128)} fusion(bf16[256,1024]{0,1:T(8,128)(2,1)S(1)} %bitcast.47, bf16[256,1024]{1,0:T(8,128)(2,1)S(1)} %copy-done), kind=kOutput, calls=%fused_computation.42 | convolution fusion | flops 536870912 | bytes 5242880 | tf_op jit(solution)/shard_map/dot_general | solution.py:67
  118.9 15.7 %all-gather.5.cloned.1.call-done = f32[256,1024]{1,0:T(8,128)} async-done(((f32[64,1024]{1,0:T(8,128)}), f32[256,1024]{1,0:T(8,128)}) %all-gather.5.cloned.1.call-update) | async-done | bytes 1048592 | tf_op jit(solution)/shard_map/all_gather | solution.py:109
  134.5 52.3 %reduce-scatter.5.cloned.1.call-done = f32[128,1024]{1,0:T(8,128)} async-done(((f32[1024,1024]{1,0:T(8,128)}), f32[128,1024]{1,0:T(8,128)}) %reduce-scatter.5.cloned.1.call-update) | async-done | bytes 524304 | tf_op jit(solution)/shard_map/reduce_scatter | solution.py:66
  186.8 26.6 %all-reduce.3 = (f32[256]{0:T(256)}, bf16[128,1024]{1,0:T(8,128)(2,1)}) all-reduce(f32[256]{0:T(256)S(1)} %get-tuple-element.5, f32[128,1024]{1,0:T(8,128)} %reduce-scatter.5.cloned.1.call-done), channel_id=1, replica_groups=mesh['replica'=4,'shard'=8] {'replica'}, use_global_device_ids=true, to_apply=%add | all-reduce | flops 131328 | bytes 788480
  213.4 2.3 %copy.47 = f32[256,1024]{1,0:T(8,128)} copy(f32[256,1024]{1,0:T(8,128)} %all-gather.5.cloned.1.call-done) | data formatting | bytes 2097152
  (23 shorter events, 0.1 us)
Async XLA Ops:
  7.2 34.3 %copy-start = (bf16[256,1024]{1,0:T(8,128)(2,1)S(1)}, bf16[256,1024]{1,0:T(8,128)(2,1)}, u32[]{:S(2)}) copy-start(bf16[256,1024]{1,0:T(8,128)(2,1)} %param.16) | copy-start | bytes 1572868
  7.2 34.3 %all-gather.3.cloned.1.call-start = ((), (), s32[]{:S(2)}) async-start(), calls=%async_computation.5 | async-start | bytes 2359296 | tf_op jit(solution)/shard_map/all_gather | solution.py:62
  11.8 37.6 %all-to-all-start = ((s32[8,1,64]{2,1,0:T(1,128)}), s32[8,1,64]{2,1,0:T(1,128)S(1)}, u32[]{:S(2)}, u32[]{:S(2)}) async-start(s32[8,1,64]{2,1,0:T(1,128)} %all_to_all.12), calls=%async_computation | async-start | bytes 8192 | tf_op jit(solution)/shard_map/all_to_all | solution.py:35
  22.2 21.8 %copy-start.2 = (bf16[8,256,256]{2,1,0:T(8,128)(2,1)}, bf16[8,256,256]{2,1,0:T(8,128)(2,1)S(1)}, u32[]{:S(2)}) copy-start(bf16[8,256,256]{2,1,0:T(8,128)(2,1)S(1)} %multiply_convert_fusion) | copy-start | bytes 3145732
  49.4 31.6 %copy-start.1 = (f32[256,1024]{1,0:T(8,128)S(1)}, f32[256,1024]{1,0:T(8,128)}, u32[]{:S(2)}) copy-start(f32[256,1024]{1,0:T(8,128)} %param.9) | copy-start | bytes 3145732
  49.4 30.2 %all-to-all-start.1 = ((bf16[8,64,1024]{2,1,0:T(8,128)(2,1)}), bf16[8,64,1024]{2,1,0:T(8,128)(2,1)S(1)}, u32[]{:S(2)}, u32[]{:S(2)}) async-start(bf16[8,64,1024]{2,1,0:T(8,128)(2,1)} %bitcast.44), calls=%async_computation.1 | async-start | bytes 2097152 | tf_op jit(solution)/shard_map/all_to_all | solution.py:86
  53.1 51.7 %reduce-scatter.3.cloned.1.call-start = ((), (), s32[]{:S(2)}) async-start(), calls=%async_computation.6 | async-start | bytes 655360 | tf_op jit(solution)/shard_map/reduce_scatter | solution.py:100
  82.9 5.0 %copy-start.5 = (u32[32]{0:T(128)S(1)}, u32[32]{0:T(128)}, u32[]{:S(2)}) copy-start(u32[32]{0:T(128)} %constant.56) | copy-start | bytes 388
  82.9 22.9 %copy-start.4 = (f32[256]{0:T(256)S(1)}, f32[256]{0:T(256)}, u32[]{:S(2)}) copy-start(f32[256]{0:T(256)} %param.10) | copy-start | bytes 3076
  84.2 30.1 %all-to-all-start.2 = ((bf16[8,64,1024]{2,1,0:T(8,128)(2,1)}), bf16[8,64,1024]{2,1,0:T(8,128)(2,1)S(1)}, u32[]{:S(2)}, u32[]{:S(2)}) async-start(bf16[8,64,1024]{2,1,0:T(8,128)(2,1)} %select_convert_fusion), calls=%async_computation.3 | async-start | bytes 2097152 | tf_op jit(solution)/shard_map/all_to_all | solution.py:50
  87.8 46.7 %all-gather.5.cloned.1.call-start = ((), (), s32[]{:S(2)}) async-start(), calls=%async_computation.7 | async-start | bytes 1310720 | tf_op jit(solution)/shard_map/all_gather | solution.py:109
  107.7 79.1 %reduce-scatter.5.cloned.1.call-start = ((), (), s32[]{:S(2)}) async-start(), calls=%async_computation.8 | async-start | bytes 4718592 | tf_op jit(solution)/shard_map/reduce_scatter | solution.py:66
  114.3 1.4 copy-start.3
Sparse Core Ops, SparseCore 0:
  9.6 31.8 all-gather.2
  81.2 23.5 reduce-scatter.2
  107.9 26.6 all-gather.4
  136.8 49.9 reduce-scatter.4
where the time goes:
time: 223 us; the launch traced here: 222 us
  waiting for transfers between devices  135 us (61%)
  blocking collectives  26.6 us (12%)
  local copies, waits for them, and re-layouts  15.3 us (7%)
  between operations  14.7 us (7%)
  starting transfers between devices  13.7 us (6%)
  matrix products  8.92 us (4%)
  other arithmetic  7.75 us (3%)
    reduce_scatter x1, waiting for transfers between devices, body(): lax.psum_scatter(lax.dot_general(mixed, cotangent, (((0,), (0,)), ((), ()...  52.3 us
    unnamed x1, blocking collectives  26.6 us
    all_to_all x1, waiting for transfers between devices, body(): lax.all_to_all(send_grad.astype(jnp.bfloat16), 'shard', split_axis=0, con...  25.1 us
    all_gather x1, waiting for transfers between devices, body(): lax.all_gather(out_weight, 'shard', axis=0, tiled=True)  19.3 us
    reduce_scatter x1, waiting for transfers between devices, body(): lax.psum_scatter(grad_rows.astype(jnp.bfloat16), 'replica', scatter_dimen...  15.7 us
    all_gather x1, waiting for transfers between devices, body(): lax.all_gather(upd_table, 'replica', axis=0, tiled=True)  15.7 us
    all_to_all x1, waiting for transfers between devices, body(): lax.all_to_all(picked, 'shard', split_axis=0, concat_axis=0, tiled=True)  6.52 us
    all_to_all x1, starting transfers between devices, body(): lax.all_to_all(send_idx, 'shard', split_axis=0, concat_axis=0, tiled=True)  6.33 us
  transfers between devices with their start and end apart: 7, of which 6 were waited for; matrix products, arithmetic and copies ran while one was open for 12% of the time, Pallas kernels for 0%

commit v1 on v0

--- a/solution.py
+++ b/solution.py
@@ -1,10 +1,19 @@
+import functools
+
 import jax
 import jax.numpy as jnp
 from jax import lax
+from jax.experimental import pallas as pl
+from jax.experimental.pallas import tpu as pltpu
 from jax.sharding import PartitionSpec as P
 
 HEADS = 8
 MAXLEN = 128
+EXTRA = 16
+VMEM = pl.BlockSpec(memory_space=pltpu.VMEM)
+SMEM = pl.BlockSpec(memory_space=pltpu.SMEM)
+F32 = jnp.float32
+BF16 = jnp.bfloat16
 
 
 def adagrad(table_rows, accum_rows, grad_rows):
@@ -13,7 +22,9 @@
     return (new_table, new_accum)
 
 
-def body(table, accum, owner, local_row, lengths, queries, keys, cotangent, out_weight):
+def general_body(
+    table, accum, owner, local_row, lengths, queries, keys, cotangent, out_weight
+):
     shards = lax.axis_size("shard")
     tok = owner.shape[0]
     rows_dev = table.shape[0]
@@ -112,6 +123,348 @@
     return (new_table, new_accum, weight_grad)
 
 
+def iota(shape, axis):
+    return lax.broadcasted_iota(jnp.int32, shape, axis)
+
+
+def nt(a, b):
+    return lax.dot_general(a, b, (((1,), (1,)), ((), ())), preferred_element_type=F32)
+
+
+def nn(a, b):
+    return lax.dot_general(a, b, (((1,), (0,)), ((), ())), preferred_element_type=F32)
+
+
+def call(kernel, name, out, n_in, smem=1, scratch=(), flops=0, nbytes=0):
+    return pl.pallas_call(
+        kernel,
+        out_shape=out,
+        in_specs=[SMEM] * smem + [VMEM] * n_in,
+        out_specs=[VMEM] * len(out) if isinstance(out, (list, tuple)) else VMEM,
+        scratch_shapes=list(scratch),
+        name=name,
+        cost_estimate=pl.CostEstimate(flops=flops, bytes_accessed=nbytes, transcendentals=0),
+        compiler_params=pltpu.CompilerParams(vmem_limit_bytes=32 * 1024 * 1024),
+    )
+
+
+def sds(shape, dtype=BF16):
+    return jax.ShapeDtypeStruct(shape, dtype)
+
+
+def pack_kernel(me, lens, q, k, owner, local, *out):
+    tok = q.shape[0]
+    pw = q.shape[1] // len(out)
+    lane = iota((EXTRA, tok), 1)
+    row = iota((EXTRA, tok), 0)
+    seg = jnp.zeros((EXTRA, tok), F32)
+    end = jnp.int32(0)
+    for n in range(lens.shape[1]):
+        end = end + lens[0, n]
+        seg = seg + jnp.where(lane >= end, 1.0, 0.0)
+    own = jnp.broadcast_to(owner[...].astype(F32), (EXTRA, tok))
+    loc = jnp.broadcast_to(local[...].astype(F32), (EXTRA, tok))
+    ids = jnp.where(row == 0, own, jnp.where(row == 1, loc, jnp.where(row == 2, seg, 0.0)))
+    ids = ids.astype(BF16)
+    for n, o in enumerate(out):
+        at = pl.ds(pl.multiple_of((me[0] ^ n) * pw, pw), pw)
+        o[0:tok, 0:pw] = q[:, at]
+        o[0:tok, pw : 2 * pw] = k[:, at]
+        o[tok : tok + EXTRA, :] = ids
+
+
+def rows_kernel(me, table, weight, out_t, out_z):
+    rows, width = table.shape
+    cols = out_t.shape[0]
+    at = pl.ds(pl.multiple_of(me[0] * cols, cols), cols)
+    t = table[:, at].T.astype(BF16)
+    out_t[...] = t
+    out_z[0:cols, :] = t
+    part = weight.shape[0] * cols // width
+    w = weight[pl.ds(pl.multiple_of(me[0] * part, part), part), :]
+    for n in range(width // rows):
+        out_z[cols + n * part : cols + (n + 1) * part, :] = w[:, n * rows : (n + 1) * rows]
+
+
+def weights_kernel(*refs):
+    *packs, out = refs
+    tok = packs[0].shape[0] - EXTRA
+    pw = packs[0].shape[1] // 2
+    heads = out.shape[1]
+    dqk = pw // heads
+    down, across = iota((tok, tok), 0), iota((tok, tok), 1)
+    lane = iota((tok, pw), 1)
+    for r, p in enumerate(packs):
+        q = p[0:tok, 0:pw]
+        k = p[0:tok, pw : 2 * pw]
+        seg = p[tok : tok + EXTRA, :].astype(F32)[2:3, :]
+        seg_down = jnp.sum(jnp.where(down == across, seg, 0.0), axis=1, keepdims=True)
+        mask = (seg == seg_down) & (down <= across)
+        for j in range(heads):
+            kj = jnp.where(lane // dqk == j, k, jnp.zeros_like(k))
+            s = nt(kj, q) * dqk ** (-0.5)
+            w = s / (1.0 + jnp.exp(-s)) * (1.0 / MAXLEN)
+            out[r, j] = jnp.where(mask, w, 0.0).astype(BF16)
+
+
+def choose_kernel(me, *refs):
+    n = len(refs) // 2
+    parts, out = refs[:n], refs[n : 2 * n]
+    held = refs[2 * n]
+    first = held.shape[1]
+    first = parts[0].shape[0] - first
+    for m in range(n):
+        held[m] = parts[m][first:, :]
+    for m in range(n):
+        out[m][...] = held[me[1] ^ me[0] ^ m]
+
+
+def pick_kernel(me, *refs):
+    n = (len(refs) - 1) // 2
+    held = refs[2 * n]
+    for m in range(n):
+        held[m] = refs[m][...]
+    for m in range(n):
+        refs[n + m][...] = held[me[1] ^ me[0] ^ m]
+
+
+def one_hot(ids, rows):
+    tok = ids.shape[1]
+    own = ids[0:1, :]
+    loc = ids[1:2, :]
+    at = iota((rows, tok), 0).astype(F32)
+    return jnp.broadcast_to(own, (rows, tok)), at == loc
+
+
+def mix_kernel(n, me, *refs):
+    mine, other = refs[:n], refs[n : 2 * n]
+    packs = refs[2 * n : 3 * n]
+    w, out = refs[3 * n], refs[3 * n + 1]
+    cols = other[0].shape[0]
+    rows = other[0].shape[1]
+    tok = packs[0].shape[0] - EXTRA
+    heads = w.shape[1]
+    dv = cols // heads
+    for r in range(n):
+        ids = packs[r][tok : tok + EXTRA, :].astype(F32)
+        own, hit = one_hot(ids, rows)
+        vals = jnp.zeros((cols, tok), F32)
+        for m in range(n):
+            for cc in range(2):
+                shard = (2 * (me[1] ^ m) + (me[2] ^ cc)).astype(F32)
+                pickm = jnp.where(hit & (own == shard), 1.0, 0.0).astype(BF16)
+                block = mine[m][0:cols, :] if cc == 0 else other[m][...]
+                vals = vals + nn(block, pickm)
+        vals = vals.astype(BF16)
+        for j in range(heads):
+            out[j * dv : (j + 1) * dv, r * tok : (r + 1) * tok] = nn(
+                vals[j * dv : (j + 1) * dv, :], w[r, j]
+            ).astype(BF16)
+
+
+def back_kernel(n, me, *refs):
+    cots, packs = refs[:n], refs[n : 2 * n]
+    ow_mine, ow_other, w = refs[2 * n : 2 * n + 3]
+    keep, send = refs[2 * n + 3 : 2 * n + 5]
+    ow, grad = refs[2 * n + 5 :]
+    tok = cots[0].shape[0]
+    heads = w.shape[1]
+    head_rows = ow_mine.shape[0]
+    part = head_rows // n
+    rows = send.shape[1]
+    for cc, src in enumerate((ow_mine, ow_other)):
+        for m in range(n):
+            at = (me[2] ^ cc) * head_rows + (me[0] ^ m) * part
+            ow[pl.ds(pl.multiple_of(at, part), part), :] = src[m * part : (m + 1) * part, :]
+    for r in range(n):
+        back = nt(cots[r][...], ow[...]).astype(BF16)
+        for j in range(heads):
+            at = slice(j * head_rows, (j + 1) * head_rows)
+            grad[r * tok : (r + 1) * tok, at] = nn(w[r, j], back[:, at]).astype(BF16)
+    for m in range(n):
+        for cc in range(2):
+            shard = (2 * (me[1] ^ m) + (me[2] ^ cc)).astype(F32)
+            total = jnp.zeros((rows, heads * head_rows), F32)
+            for r in range(n):
+                ids = packs[r][tok : tok + EXTRA, :].astype(F32)
+                own, hit = one_hot(ids, rows)
+                pickm = jnp.where(hit & (own == shard), 1.0, 0.0).astype(BF16)
+                total = total + nn(pickm, grad[r * tok : (r + 1) * tok, :])
+            if cc == 0:
+                keep[m] = total
+            else:
+                send[m] = total.astype(BF16)
+
+
+def wgrad_kernel(n, me, mixed, *refs):
+    cots, (keep, send) = refs[:n], refs[n:]
+    tok = cots[0].shape[0]
+    rows = keep.shape[0]
+    for cc, out in ((1, send), (0, keep)):
+        at = pl.ds(pl.multiple_of((me[2] ^ cc) * rows, rows), rows)
+        total = jnp.zeros(keep.shape, F32)
+        for r in range(n):
+            total = total + nn(mixed[at, r * tok : (r + 1) * tok], cots[r][...])
+        out[...] = total.astype(out.dtype)
+
+
+def add_kernel(keep, got, *out):
+    for m, o in enumerate(out):
+        o[...] = (keep[m] + got[m].astype(F32)).astype(o.dtype)
+
+
+def add_parts_kernel(me, keep, got, *out):
+    n = len(out)
+    part = keep.shape[0] // n
+    for m, o in enumerate(out):
+        at = pl.ds(pl.multiple_of((me[0] ^ m) * part, part), part)
+        o[...] = (keep[at, :] + got[at, :].astype(F32)).astype(o.dtype)
+
+
+def sum_kernel(*refs):
+    *parts, out = refs
+    total = parts[0][...].astype(F32)
+    for p in parts[1:]:
+        total = total + p[...].astype(F32)
+    out[...] = total.astype(out.dtype)
+
+
+def place_kernel(me, *refs):
+    *parts, out = refs
+    rows = parts[0].shape[0]
+    for m, p in enumerate(parts):
+        out[pl.ds(pl.multiple_of((me[0] ^ m) * rows, rows), rows), :] = p[...]
+
+
+def update_kernel(n, me, *refs):
+    parts = refs[:n]
+    table, accum, new_table, new_accum, grad = refs[n:]
+    rows, width = table.shape
+    cols = width // n
+    for m in range(n):
+        at = pl.ds(pl.multiple_of((me[0] ^ m) * cols, cols), cols)
+        grad[:, at] = parts[m][...].astype(F32)
+    mean = jnp.sum(grad[...] * grad[...], axis=1, keepdims=True) * (1.0 / width)
+    same = iota((rows, rows), 0) == iota((rows, rows), 1)
+    old = jnp.sum(jnp.where(same, accum[...], 0.0), axis=1, keepdims=True)
+    fresh = old + mean
+    new_accum[...] = jnp.sum(jnp.where(same, fresh, 0.0), axis=0, keepdims=True)
+    new_table[...] = table[...] - grad[...] / (jnp.sqrt(fresh) + 1e-08)
+
+
+def body(table, accum, owner, local_row, lengths, queries, keys, cotangent, out_weight):
+    n = lax.axis_size("replica")
+    shards = lax.axis_size("shard")
+    tok = owner.shape[0]
+    rows, width = table.shape
+    cols = width // n
+    heads = HEADS // n
+    part = out_weight.shape[0] // n
+    shard = lax.axis_index("shard")
+    me = jnp.stack([lax.axis_index("replica"), shard // 2, shard % 2]).astype(jnp.int32)
+
+    def column(x, m):
+        return lax.ppermute(x, "replica", [(i, i ^ m) for i in range(n)]) if m else x
+
+    def along(x, m):
+        return lax.ppermute(x, "shard", [(i, i ^ (2 * m)) for i in range(shards)]) if m else x
+
+    def core(x):
+        return lax.ppermute(x, "shard", [(i, i ^ 1) for i in range(shards)])
+
+    packs = call(
+        pack_kernel,
+        "pack",
+        [sds((tok + EXTRA, 2 * queries.shape[1] // n))] * n,
+        4,
+        smem=2,
+    )(me, lengths, queries, keys, owner.reshape(1, tok), local_row.reshape(1, tok))
+    packs = [column(p, m) for m, p in enumerate(packs)]
+    cots = [column(cotangent, m) for m in range(n)]
+
+    zrows = cols + part * width // rows
+    turned, zpay = call(
+        rows_kernel, "rows", [sds((cols, rows)), sds((zrows, rows))], 2
+    )(me, table, out_weight)
+    mine = [along(zpay, m) for m in range(n)]
+    other = [core(turned if m == 0 else mine[m][0:cols]) for m in range(n)]
+
+    w = call(
+        weights_kernel, "weights", sds((n, heads, tok, tok)), n, smem=0, flops=n * heads * tok * tok * 512
+    )(*packs)
+
+    owp = call(
+        choose_kernel,
+        "choose",
+        [sds((zrows - cols, rows))] * n,
+        n,
+        scratch=[pltpu.VMEM((n, zrows - cols, rows), BF16)],
+    )(me, *mine)
+    owp = [column(p, m) for m, p in enumerate(owp)]
+    owp = [
+        jnp.concatenate([p[i * part : (i + 1) * part] for i in range(width // rows)], axis=1)
+        for p in owp
+    ]
+    ow_mine = jnp.concatenate(owp, axis=0)
+    ow_other = core(ow_mine)
+
+    mixed = call(
+        functools.partial(mix_kernel, n), "mix", sds((cols, n * tok)), 3 * n + 1, flops=2 * n * tok * cols * rows * shards
+    )(me, *mine, *other, *packs, w)
+
+    keep, send = call(
+        functools.partial(back_kernel, n),
+        "back",
+        [sds((n, rows, cols), F32), sds((n, rows, cols))],
+        2 * n + 3,
+        scratch=[pltpu.VMEM((cols, width), BF16), pltpu.VMEM((n * tok, cols), BF16)],
+        flops=4 * n * tok * cols * width,
+    )(me, *cots, *packs, ow_mine, ow_other, w)
+    got = core(send)
+    sums = call(
+        add_kernel, "add", [sds((rows, cols), F32)] + [sds((rows, cols))] * (n - 1), 2, smem=0
+    )(keep, got)
+    sums = [along(s, m) for m, s in enumerate(sums)]
+    grad = call(sum_kernel, "sum_rows", sds((rows, cols)), n, smem=0)(*sums)
+    grads = [column(grad, m) for m in range(n)]
+    new_table, new_accum = call(
+        functools.partial(update_kernel, n),
+        "update",
+        [sds((rows, width), F32), sds((1, rows), F32)],
+        n + 2,
+        scratch=[pltpu.VMEM((rows, width), F32)],
+    )(me, *grads, table, accum.reshape(1, rows))
+
+    wkeep, wsend = call(
+        functools.partial(wgrad_kernel, n),
+        "wgrad",
+        [sds((n * part, width), F32), sds((n * part, width))],
+        n + 1,
+        flops=2 * n * tok * cols * width,
+    )(me, mixed, *cots)
+    wparts = call(add_parts_kernel, "add_parts", [sds((part, width))] * n, 2)(
+        me, wkeep, core(wsend)
+    )
+    wparts = [column(p, m) for m, p in enumerate(wparts)]
+    wparts = call(
+        pick_kernel,
+        "pick",
+        [sds((part, width))] * n,
+        n,
+        scratch=[pltpu.VMEM((n, part, width), BF16)],
+    )(me, *wparts)
+    wparts = [along(p, m) for m, p in enumerate(wparts)]
+    wsum = call(sum_kernel, "sum_parts", sds((part, width)), n, smem=0)(*wparts)
+    wsums = [column(wsum, m) for m in range(n)]
+    weight_grad = call(place_kernel, "place", sds((n * part, width)), n)(me, *wsums)
+    return (new_table, new_accum.reshape(rows), weight_grad)
+
+
+def fits(mesh):
+    n, shards = mesh.shape["replica"], mesh.shape["shard"]
+    return n & (n - 1) == 0 and shards == HEADS and 2 * n == HEADS
+
+
 def solution(mesh):
     placed = (
         P("shard", None),
@@ -125,7 +478,7 @@
         P("shard", None),
     )
     return jax.shard_map(
-        body,
+        body if fits(mesh) else general_body,
         mesh=mesh,
         in_specs=placed,
         out_specs=(P("shard", None), P("shard"), P("shard", None)),

time: 223 us -> 117 us (0.52)
  waiting for transfers between devices: 135 us -> 53.4 us
  starting transfers between devices: 13.7 us -> 43.2 us
  blocking collectives: 26.6 us -> 0 us
  Pallas kernels: 0 us -> 15.5 us
  between operations: 14.7 us -> 0.88 us
  local copies, waits for them, and re-layouts: 15.3 us -> 3.56 us
  matrix products: 8.92 us -> 0 us
  other arithmetic: 7.75 us -> 0.09 us
    reduce_scatter x2 -> x0, waiting for transfers between devices: 68 us -> none  [the longest x1 52.3 us: body(): lax.psum_scatter(lax.dot_general(mixed, cotangent, (((0,), (0,)), ((), ()...]
    ppermute x0 -> x34, waiting for transfers between devices: none -> 53.4 us  [the longest x18 32.6 us: column(): lax.ppermute(x, 'replica', [(i, i ^ m) for i in range(n)])]
    ppermute x0 -> x34, starting transfers between devices: none -> 43.2 us  [the longest x18 27.1 us: column(): lax.ppermute(x, 'replica', [(i, i ^ m) for i in range(n)])]
    all_gather x2 -> x0, waiting for transfers between devices: 34.9 us -> none  [the longest x1 19.3 us: body(): lax.all_gather(out_weight, 'shard', axis=0, tiled=True)]
    all_to_all x3 -> x0, waiting for transfers between devices: 31.6 us -> none  [the longest x1 25.1 us: body(): lax.all_to_all(send_grad.astype(jnp.bfloat16), 'shard', split_axis=0, con...]
    unnamed x1 -> x0, blocking collectives: 26.6 us -> none
    pallas_call x0 -> x14, Pallas kernels: none -> 15.5 us  [the longest x1 3.75 us: body(): call(functools.partial(back_kernel, n), 'back', [sds((n, rows, cols), F32...]
    all_to_all x3 -> x0, starting transfers between devices: 13.6 us -> none  [the longest x1 6.33 us: body(): lax.all_to_all(send_idx, 'shard', split_axis=0, concat_axis=0, tiled=True)]
  transfers between devices with their start and end apart: 7 -> 34, of which waited for: 6 -> 15; matrix products, arithmetic and copies ran while one was open for 12% -> 0% of each run, Pallas kernels for 0% -> 11%
where the time goes in v1:
time: 117 us
  waiting for transfers between devices  53.4 us (46%)
  starting transfers between devices  43.2 us (37%)
  Pallas kernels  15.5 us (13%)
  local copies, waits for them, and re-layouts  3.56 us (3%)
    ppermute x18, waiting for transfers between devices, column(): lax.ppermute(x, 'replica', [(i, i ^ m) for i in range(n)])  32.6 us
    ppermute x18, starting transfers between devices, column(): lax.ppermute(x, 'replica', [(i, i ^ m) for i in range(n)])  27.1 us
    ppermute x9, waiting for transfers between devices, along(): lax.ppermute(x, 'shard', [(i, i ^ 2 * m) for i in range(shards)])  19.6 us
    ppermute x9, starting transfers between devices, along(): lax.ppermute(x, 'shard', [(i, i ^ 2 * m) for i in range(shards)])  14.3 us
    pallas_call x1, Pallas kernels, body(): call(functools.partial(back_kernel, n), 'back', [sds((n, rows, cols), F32...  3.75 us
    unnamed x20, local copies, waits for them, and re-layouts  3.51 us
    pallas_call x1, Pallas kernels, body(): call(functools.partial(mix_kernel, n), 'mix', sds((cols, n * tok)), 3 * n...  3.34 us
  transfers between devices with their start and end apart: 34, of which 15 were waited for; matrix products, arithmetic and copies ran while one was open for 0% of the time, Pallas kernels for 11%

profile of v1, /device:TPU:0, one launch (start us, length us, event | category | flops | bytes accessed | tf_op | source)
XLA Modules:
  0.0 116.6 jit_solution(14391619885404846046)
XLA Ops:
  0.7 1.2 %copy-done = f32[256,1024]{1,0:T(8,128)S(1)} copy-done((f32[256,1024]{1,0:T(8,128)S(1)}, f32[256,1024]{1,0:T(8,128)}, u32[]{:S(2)}) %copy-start) | copy-done | bytes 1048600
  2.0 0.9 copy-done.3
  2.9 0.6 rows.1
  3.6 3.1 %collective-permute-start.6 = (bf16[384,256]{1,0:T(8,128)(2,1)S(1)}, bf16[384,256]{1,0:T(8,128)(2,1)S(1)}, u32[]{:S(2)}, u32[]{:S(2)}) collective-permute-start(bf16[384,256]{1,0:T(8,128)(2,1)S(1)} %get-tuple-element.35.refs_0_), channel_id=1, source_target_pairs={{0,2},{1,3},{2,0},{3,1},{4,6},{5,7},{6,4},{7,5},{8,10},{9,11},{10,... | collective-permute-start | bytes 589832 | tf_op jit(solution)/shard_map/ppermute | solution.py:370
  6.7 2.6 %collective-permute-start.7 = (bf16[384,256]{1,0:T(8,128)(2,1)S(1)}, bf16[384,256]{1,0:T(8,128)(2,1)S(1)}, u32[]{:S(2)}, u32[]{:S(2)}) collective-permute-start(bf16[384,256]{1,0:T(8,128)(2,1)S(1)} %get-tuple-element.35.refs_0_), channel_id=1, source_target_pairs={{0,4},{1,5},{2,6},{3,7},{4,0},{5,1},{6,2},{7,3},{8,12},{9,13},{10,... | collective-permute-start | bytes 589832 | tf_op jit(solution)/shard_map/ppermute | solution.py:370
  9.3 1.7 %collective-permute-start = (bf16[256,1024]{1,0:T(8,128)(2,1)S(1)}, bf16[256,1024]{1,0:T(8,128)(2,1)S(1)}, u32[]{:S(2)}, u32[]{:S(2)}) collective-permute-start(bf16[256,1024]{1,0:T(8,128)(2,1)S(1)} %copy-done.2), channel_id=1, source_target_pairs={{0,8},{8,0},{16,24},{24,16},{1,9},{9,1},{17,25},{25,17},{2,10},{10... | collective-permute-start | bytes 1572872 | tf_op jit(solution)/shard_map/ppermute | solution.py:367
  11.0 1.5 %collective-permute-start.1 = (bf16[256,1024]{1,0:T(8,128)(2,1)S(1)}, bf16[256,1024]{1,0:T(8,128)(2,1)S(1)}, u32[]{:S(2)}, u32[]{:S(2)}) collective-permute-start(bf16[256,1024]{1,0:T(8,128)(2,1)S(1)} %copy-done.2), channel_id=1, source_target_pairs={{0,16},{8,24},{16,0},{24,8},{1,17},{9,25},{17,1},{25,9},{2,18},{10... | collective-permute-start | bytes 1572872 | tf_op jit(solution)/shard_map/ppermute | solution.py:367
  12.5 0.7 copy-done.6
  13.2 0.6 pack.1
  13.8 1.2 %collective-permute-done.6.refs_1_ = bf16[384,256]{1,0:T(8,128)(2,1)S(1)} collective-permute-done((bf16[384,256]{1,0:T(8,128)(2,1)S(1)}, bf16[384,256]{1,0:T(8,128)(2,1)S(1)}, u32[]{:S(2)}, u32[]{:S(2)}) %collective-permute-start.6) | collective-permute-done | bytes 196640 | tf_op jit(solution)/shard_map/ppermute | solution.py:370
  15.0 2.6 %collective-permute-start.2 = (bf16[256,1024]{1,0:T(8,128)(2,1)S(1)}, bf16[256,1024]{1,0:T(8,128)(2,1)S(1)}, u32[]{:S(2)}, u32[]{:S(2)}) collective-permute-start(bf16[256,1024]{1,0:T(8,128)(2,1)S(1)} %copy-done.2), channel_id=1, source_target_pairs={{0,24},{8,16},{16,8},{24,0},{1,25},{9,17},{17,9},{25,1},{2,26},{10... | collective-permute-start | bytes 1572872 | tf_op jit(solution)/shard_map/ppermute | solution.py:367
  17.6 6.2 %collective-permute-done.7.refs_2_ = bf16[384,256]{1,0:T(8,128)(2,1)S(1)} collective-permute-done((bf16[384,256]{1,0:T(8,128)(2,1)S(1)}, bf16[384,256]{1,0:T(8,128)(2,1)S(1)}, u32[]{:S(2)}, u32[]{:S(2)}) %collective-permute-start.7) | collective-permute-done | bytes 196640 | tf_op jit(solution)/shard_map/ppermute | solution.py:370
  23.8 1.5 %collective-permute-start.3 = (bf16[272,256]{1,0:T(8,128)(2,1)S(1)}, bf16[272,256]{1,0:T(8,128)(2,1)S(1)}, u32[]{:S(2)}, u32[]{:S(2)}) collective-permute-start(bf16[272,256]{1,0:T(8,128)(2,1)S(1)} %get-tuple-element.32), channel_id=1, source_target_pairs={{0,8},{8,0},{16,24},{24,16},{1,9},{9,1},{17,25},{25,17},{2,10},{10... | collective-permute-start | bytes 417800 | tf_op jit(solution)/shard_map/ppermute | solution.py:367
  26.5 11.5 %collective-permute-done.9 = bf16[128,256]{1,0:T(8,128)(2,1)S(1)} collective-permute-done((bf16[128,256]{1,0:T(8,128)(2,1)S(1)}, bf16[128,256]{1,0:T(8,128)(2,1)S(1)}, u32[]{:S(2)}, u32[]{:S(2)}) %collective-permute-start.9) | collective-permute-done | bytes 65568 | tf_op jit(solution)/shard_map/ppermute | solution.py:367
  38.0 1.5 %collective-permute-start.10 = (bf16[128,256]{1,0:T(8,128)(2,1)S(1)}, bf16[128,256]{1,0:T(8,128)(2,1)S(1)}, u32[]{:S(2)}, u32[]{:S(2)}) collective-permute-start(bf16[128,256]{1,0:T(8,128)(2,1)S(1)} %get-tuple-element.38), channel_id=1, source_target_pairs={{0,16},{8,24},{16,0},{24,8},{1,17},{9,25},{17,1},{25,9},{2,18},{10... | collective-permute-start | bytes 196616 | tf_op jit(solution)/shard_map/ppermute | solution.py:367
  39.6 2.7 %collective-permute-done.10 = bf16[128,256]{1,0:T(8,128)(2,1)S(1)} collective-permute-done((bf16[128,256]{1,0:T(8,128)(2,1)S(1)}, bf16[128,256]{1,0:T(8,128)(2,1)S(1)}, u32[]{:S(2)}, u32[]{:S(2)}) %collective-permute-start.10) | collective-permute-done | bytes 65568 | tf_op jit(solution)/shard_map/ppermute | solution.py:367
  42.3 2.4 %collective-permute-start.11 = (bf16[128,256]{1,0:T(8,128)(2,1)S(1)}, bf16[128,256]{1,0:T(8,128)(2,1)S(1)}, u32[]{:S(2)}, u32[]{:S(2)}) collective-permute-start(bf16[128,256]{1,0:T(8,128)(2,1)S(1)} %get-tuple-element.39), channel_id=1, source_target_pairs={{0,24},{8,16},{16,8},{24,0},{1,25},{9,17},{17,9},{25,1},{2,26},{10... | collective-permute-start | bytes 196616 | tf_op jit(solution)/shard_map/ppermute | solution.py:367
  44.7 2.9 %collective-permute-done.11 = bf16[128,256]{1,0:T(8,128)(2,1)S(1)} collective-permute-done((bf16[128,256]{1,0:T(8,128)(2,1)S(1)}, bf16[128,256]{1,0:T(8,128)(2,1)S(1)}, u32[]{:S(2)}, u32[]{:S(2)}) %collective-permute-start.11) | collective-permute-done | bytes 65568 | tf_op jit(solution)/shard_map/ppermute | solution.py:367
  47.6 1.5 %collective-permute-start.4 = (bf16[272,256]{1,0:T(8,128)(2,1)S(1)}, bf16[272,256]{1,0:T(8,128)(2,1)S(1)}, u32[]{:S(2)}, u32[]{:S(2)}) collective-permute-start(bf16[272,256]{1,0:T(8,128)(2,1)S(1)} %get-tuple-element.33), channel_id=1, source_target_pairs={{0,16},{8,24},{16,0},{24,8},{1,17},{9,25},{17,1},{25,9},{2,18},{10... | collective-permute-start | bytes 417800 | tf_op jit(solution)/shard_map/ppermute | solution.py:367
  49.2 4.0 %collective-permute-done.4.refs_2_.refs_6_.refs_10_ = bf16[272,256]{1,0:T(8,128)(2,1)S(1)} collective-permute-done((bf16[272,256]{1,0:T(8,128)(2,1)S(1)}, bf16[272,256]{1,0:T(8,128)(2,1)S(1)}, u32[]{:S(2)}, u32[]{:S(2)}) %collective-permute-start.4) | collective-permute-done | bytes 139296 | tf_op jit(solution)/shard_map/ppermute | solution.py:367
  53.2 3.3 %collective-permute-start.5 = (bf16[272,256]{1,0:T(8,128)(2,1)S(1)}, bf16[272,256]{1,0:T(8,128)(2,1)S(1)}, u32[]{:S(2)}, u32[]{:S(2)}) collective-permute-start(bf16[272,256]{1,0:T(8,128)(2,1)S(1)} %get-tuple-element.34), channel_id=1, source_target_pairs={{0,24},{8,16},{16,8},{24,0},{1,25},{9,17},{17,9},{25,1},{2,26},{10... | collective-permute-start | bytes 417800 | tf_op jit(solution)/shard_map/ppermute | solution.py:367
  56.5 3.0 %collective-permute-done.5.refs_3_.refs_7_.refs_11_ = bf16[272,256]{1,0:T(8,128)(2,1)S(1)} collective-permute-done((bf16[272,256]{1,0:T(8,128)(2,1)S(1)}, bf16[272,256]{1,0:T(8,128)(2,1)S(1)}, u32[]{:S(2)}, u32[]{:S(2)}) %collective-permute-start.5) | collective-permute-done | bytes 139296 | tf_op jit(solution)/shard_map/ppermute | solution.py:367
  59.6 0.8 weights.1.refs_10_.refs_12_
  61.6 3.8 %back.1 = (f32[4,256,256]{2,1,0:T(8,128)S(1)}, bf16[4,256,256]{2,1,0:T(8,128)(2,1)S(1)}) custom-call(s32[3]{0:T(128)S(1)} %pad_add_fusion.me, bf16[256,1024]{1,0:T(8,128)(2,1)S(1)} %copy-done.2, bf16[256,1024]{1,0:T(8,128)(2,1)S(1)} %collective-permute-done.refs_1_, bf16[256,1024]{1,0:T(8,128)(2,1)S(1)} %collective-permute-done.1.refs_2_, ...), custom_call_target="tpu_custom_call" | custom-call | flops 1073741824 | tf_op jit(solution)/shard_map/back/pallas_call | solution.py:415
  65.5 3.3 %mix.1.mixed = bf16[256,1024]{1,0:T(8,128)(2,1)S(1)} custom-call(s32[3]{0:T(128)S(1)} %pad_add_fusion.me, bf16[384,256]{1,0:T(8,128)(2,1)S(1)} %get-tuple-element.35.refs_0_, bf16[384,256]{1,0:T(8,128)(2,1)S(1)} %collective-permute-done.6.refs_1_, bf16[384,256]{1,0:T(8,128)(2,1)S(1)} %collective-permute-done.7.refs_2_, ...), custom_call_target="tpu_custom_call" | custom-call | flops 1073741824 | tf_op jit(solution)/shard_map/mix/pallas_call | solution.py:411
  68.8 1.3 %wgrad.1 = (f32[128,1024]{1,0:T(8,128)S(1)}, bf16[128,1024]{1,0:T(8,128)(2,1)S(1)}) custom-call(s32[3]{0:T(128)S(1)} %pad_add_fusion.me, bf16[256,1024]{1,0:T(8,128)(2,1)S(1)} %mix.1.mixed, bf16[256,1024]{1,0:T(8,128)(2,1)S(1)} %copy-done.2, bf16[256,1024]{1,0:T(8,128)(2,1)S(1)} %collective-permute-done.refs_1_, ...), custom_call_target="tpu_custom_call" | custom-call | flops 536870912 | tf_op jit(solution)/shard_map/wgrad/pallas_call | solution.py:438
  70.6 1.2 collective-permute-done.24.got
  72.3 1.1 collective-permute-start.25
  73.5 2.4 %collective-permute-start.26 = (bf16[32,1024]{1,0:T(8,128)(2,1)S(1)}, bf16[32,1024]{1,0:T(8,128)(2,1)S(1)}, u32[]{:S(2)}, u32[]{:S(2)}) collective-permute-start(bf16[32,1024]{1,0:T(8,128)(2,1)S(1)} %get-tuple-element.53), channel_id=1, source_target_pairs={{0,16},{8,24},{16,0},{24,8},{1,17},{9,25},{17,1},{25,9},{2,18},{10... | collective-permute-start | bytes 196616 | tf_op jit(solution)/shard_map/ppermute | solution.py:367
  75.9 0.9 collective-permute-done.25.refs_1_
  76.8 2.4 %collective-permute-done.26.refs_2_ = bf16[32,1024]{1,0:T(8,128)(2,1)S(1)} collective-permute-done((bf16[32,1024]{1,0:T(8,128)(2,1)S(1)}, bf16[32,1024]{1,0:T(8,128)(2,1)S(1)}, u32[]{:S(2)}, u32[]{:S(2)}) %collective-permute-start.26) | collective-permute-done | bytes 65568 | tf_op jit(solution)/shard_map/ppermute | solution.py:367
  79.1 1.9 %collective-permute-done.27.refs_3_ = bf16[32,1024]{1,0:T(8,128)(2,1)S(1)} collective-permute-done((bf16[32,1024]{1,0:T(8,128)(2,1)S(1)}, bf16[32,1024]{1,0:T(8,128)(2,1)S(1)}, u32[]{:S(2)}, u32[]{:S(2)}) %collective-permute-start.27) | collective-permute-done | bytes 65568 | tf_op jit(solution)/shard_map/ppermute | solution.py:367
  81.7 0.7 collective-permute-start.28
  82.5 1.5 %collective-permute-start.14 = (bf16[256,256]{1,0:T(8,128)(2,1)S(1)}, bf16[256,256]{1,0:T(8,128)(2,1)S(1)}, u32[]{:S(2)}, u32[]{:S(2)}) collective-permute-start(bf16[256,256]{1,0:T(8,128)(2,1)S(1)} %get-tuple-element.43), channel_id=1, source_target_pairs={{0,2},{1,3},{2,0},{3,1},{4,6},{5,7},{6,4},{7,5},{8,10},{9,11},{10,... | collective-permute-start | bytes 393224 | tf_op jit(solution)/shard_map/ppermute | solution.py:370
  83.9 2.2 %collective-permute-start.15 = (bf16[256,256]{1,0:T(8,128)(2,1)S(1)}, bf16[256,256]{1,0:T(8,128)(2,1)S(1)}, u32[]{:S(2)}, u32[]{:S(2)}) collective-permute-start(bf16[256,256]{1,0:T(8,128)(2,1)S(1)} %get-tuple-element.44), channel_id=1, source_target_pairs={{0,4},{1,5},{2,6},{3,7},{4,0},{5,1},{6,2},{7,3},{8,12},{9,13},{10,... | collective-permute-start | bytes 393224 | tf_op jit(solution)/shard_map/ppermute | solution.py:370
  86.1 1.4 %collective-permute-start.16 = (bf16[256,256]{1,0:T(8,128)(2,1)S(1)}, bf16[256,256]{1,0:T(8,128)(2,1)S(1)}, u32[]{:S(2)}, u32[]{:S(2)}) collective-permute-start(bf16[256,256]{1,0:T(8,128)(2,1)S(1)} %get-tuple-element.45), channel_id=1, source_target_pairs={{0,6},{1,7},{2,4},{3,5},{4,2},{5,3},{6,0},{7,1},{8,14},{9,15},{10,... | collective-permute-start | bytes 393224 | tf_op jit(solution)/shard_map/ppermute | solution.py:370
  87.5 2.0 %collective-permute-start.29 = (bf16[32,1024]{1,0:T(8,128)(2,1)S(1)}, bf16[32,1024]{1,0:T(8,128)(2,1)S(1)}, u32[]{:S(2)}, u32[]{:S(2)}) collective-permute-start(bf16[32,1024]{1,0:T(8,128)(2,1)S(1)} %get-tuple-element.57), channel_id=1, source_target_pairs={{0,4},{1,5},{2,6},{3,7},{4,0},{5,1},{6,2},{7,3},{8,12},{9,13},{10,... | collective-permute-start | bytes 196616 | tf_op jit(solution)/shard_map/ppermute | solution.py:370
  89.5 0.9 collective-permute-start.30
  90.4 12.2 %collective-permute-done.29.refs_2_ = bf16[32,1024]{1,0:T(8,128)(2,1)S(1)} collective-permute-done((bf16[32,1024]{1,0:T(8,128)(2,1)S(1)}, bf16[32,1024]{1,0:T(8,128)(2,1)S(1)}, u32[]{:S(2)}, u32[]{:S(2)}) %collective-permute-start.29) | collective-permute-done | bytes 65568 | tf_op jit(solution)/shard_map/ppermute | solution.py:370
  102.7 0.6 collective-permute-start.31
  103.4 1.5 %collective-permute-start.17 = (bf16[256,256]{1,0:T(8,128)(2,1)S(1)}, bf16[256,256]{1,0:T(8,128)(2,1)S(1)}, u32[]{:S(2)}, u32[]{:S(2)}) collective-permute-start(bf16[256,256]{1,0:T(8,128)(2,1)S(1)} %sum_rows.1.refs_0_), channel_id=1, source_target_pairs={{0,8},{8,0},{16,24},{24,16},{1,9},{9,1},{17,25},{25,17},{2,10},{10... | collective-permute-start | bytes 393224 | tf_op jit(solution)/shard_map/ppermute | solution.py:367
  105.3 1.6 %collective-permute-start.19 = (bf16[256,256]{1,0:T(8,128)(2,1)S(1)}, bf16[256,256]{1,0:T(8,128)(2,1)S(1)}, u32[]{:S(2)}, u32[]{:S(2)}) collective-permute-start(bf16[256,256]{1,0:T(8,128)(2,1)S(1)} %sum_rows.1.refs_0_), channel_id=1, source_target_pairs={{0,24},{8,16},{16,8},{24,0},{1,25},{9,17},{17,9},{25,1},{2,26},{10... | collective-permute-start | bytes 393224 | tf_op jit(solution)/shard_map/ppermute | solution.py:367
  107.7 2.2 %collective-permute-start.33 = (bf16[32,1024]{1,0:T(8,128)(2,1)S(1)}, bf16[32,1024]{1,0:T(8,128)(2,1)S(1)}, u32[]{:S(2)}, u32[]{:S(2)}) collective-permute-start(bf16[32,1024]{1,0:T(8,128)(2,1)S(1)} %sum_parts.1.refs_0_), channel_id=1, source_target_pairs={{0,24},{8,16},{16,8},{24,0},{1,25},{9,17},{17,9},{25,1},{2,26},{10... | collective-permute-start | bytes 196616 | tf_op jit(solution)/shard_map/ppermute | solution.py:367
  109.8 2.1 %collective-permute-done.32.refs_2_ = bf16[32,1024]{1,0:T(8,128)(2,1)S(1)} collective-permute-done((bf16[32,1024]{1,0:T(8,128)(2,1)S(1)}, bf16[32,1024]{1,0:T(8,128)(2,1)S(1)}, u32[]{:S(2)}, u32[]{:S(2)}) %collective-permute-start.32) | collective-permute-done | bytes 65568 | tf_op jit(solution)/shard_map/ppermute | solution.py:367
  112.0 0.9 collective-permute-done.33.refs_3_
  112.8 1.3 %place.1 = bf16[128,1024]{1,0:T(8,128)(2,1)} custom-call(s32[3]{0:T(128)S(1)} %pad_add_fusion.me, bf16[32,1024]{1,0:T(8,128)(2,1)S(1)} %sum_parts.1.refs_0_, bf16[32,1024]{1,0:T(8,128)(2,1)S(1)} %collective-permute-done.31.refs_1_, bf16[32,1024]{1,0:T(8,128)(2,1)S(1)} %collective-permute-done.32.refs_2_, bf16[32,1024]{1,0:T(8,128)(2,1)S(1)} %collective-permute-done.33.refs_3_), custom_call_target="tpu_custom_call" | custom-call | tf_op jit(solution)/shard_map/place/pallas_call | solution.py:459
  114.1 0.6 copy-done.8
  114.8 1.8 %update.1 = (f32[256,1024]{1,0:T(8,128)}, f32[1,256]{1,0:T(1,128)}) custom-call(s32[3]{0:T(128)S(1)} %pad_add_fusion.me, bf16[256,256]{1,0:T(8,128)(2,1)S(1)} %sum_rows.1.refs_0_, bf16[256,256]{1,0:T(8,128)(2,1)S(1)} %collective-permute-done.17.refs_1_, bf16[256,256]{1,0:T(8,128)(2,1)S(1)} %collective-permute-done.18.refs_2_, ...), custom_call_target="tpu_custom_call" | custom-call | tf_op jit(solution)/shard_map/update/pallas_call | solution.py:430
  (63 shorter events, 5.7 us)
Async XLA Ops:
  0.7 1.2 %copy-start = (f32[256,1024]{1,0:T(8,128)S(1)}, f32[256,1024]{1,0:T(8,128)}, u32[]{:S(2)}) copy-start(f32[256,1024]{1,0:T(8,128)} %refs_4_.1) | copy-start | bytes 3145732
  2.0 0.9 copy-start.3
  2.9 6.3 %copy-start.2 = (bf16[256,1024]{1,0:T(8,128)(2,1)S(1)}, bf16[256,1024]{1,0:T(8,128)(2,1)}, u32[]{:S(2)}) copy-start(bf16[256,1024]{1,0:T(8,128)(2,1)} %refs_0_.3) | copy-start | bytes 1572868
  2.9 9.6 %copy-start.4 = (bf16[256,512]{1,0:T(8,128)(2,1)S(1)}, bf16[256,512]{1,0:T(8,128)(2,1)}, u32[]{:S(2)}) copy-start(bf16[256,512]{1,0:T(8,128)(2,1)} %q.1) | copy-start | bytes 786436
  2.9 9.6 %copy-start.5 = (bf16[256,512]{1,0:T(8,128)(2,1)S(1)}, bf16[256,512]{1,0:T(8,128)(2,1)}, u32[]{:S(2)}) copy-start(bf16[256,512]{1,0:T(8,128)(2,1)} %k.1) | copy-start | bytes 786436
  2.9 9.6 %copy-start.7 = (s32[256]{0:T(256)S(1)}, s32[256]{0:T(256)}, u32[]{:S(2)}) copy-start(s32[256]{0:T(256)} %param.12) | copy-start | bytes 3076
  3.6 11.4 %collective-permute-start.6 = (bf16[384,256]{1,0:T(8,128)(2,1)S(1)}, bf16[384,256]{1,0:T(8,128)(2,1)S(1)}, u32[]{:S(2)}, u32[]{:S(2)}) collective-permute-start(bf16[384,256]{1,0:T(8,128)(2,1)S(1)} %get-tuple-element.35.refs_0_), channel_id=1, source_target_pairs={{0,2},{1,3},{2,0},{3,1},{4,6},{5,7},{6,4},{7,5},{8,10},{9,11},{10,... | collective-permute-start | bytes 589832 | tf_op jit(solution)/shard_map/ppermute | solution.py:370
  6.7 17.2 %collective-permute-start.7 = (bf16[384,256]{1,0:T(8,128)(2,1)S(1)}, bf16[384,256]{1,0:T(8,128)(2,1)S(1)}, u32[]{:S(2)}, u32[]{:S(2)}) collective-permute-start(bf16[384,256]{1,0:T(8,128)(2,1)S(1)} %get-tuple-element.35.refs_0_), channel_id=1, source_target_pairs={{0,4},{1,5},{2,6},{3,7},{4,0},{5,1},{6,2},{7,3},{8,12},{9,13},{10,... | collective-permute-start | bytes 589832 | tf_op jit(solution)/shard_map/ppermute | solution.py:370
  9.2 16.1 %collective-permute-start.8 = (bf16[384,256]{1,0:T(8,128)(2,1)S(1)}, bf16[384,256]{1,0:T(8,128)(2,1)S(1)}, u32[]{:S(2)}, u32[]{:S(2)}) collective-permute-start(bf16[384,256]{1,0:T(8,128)(2,1)S(1)} %get-tuple-element.35.refs_0_), channel_id=1, source_target_pairs={{0,6},{1,7},{2,4},{3,5},{4,2},{5,3},{6,0},{7,1},{8,14},{9,15},{10,... | collective-permute-start | bytes 589832 | tf_op jit(solution)/shard_map/ppermute | solution.py:370
  9.3 51.2 %collective-permute-start = (bf16[256,1024]{1,0:T(8,128)(2,1)S(1)}, bf16[256,1024]{1,0:T(8,128)(2,1)S(1)}, u32[]{:S(2)}, u32[]{:S(2)}) collective-permute-start(bf16[256,1024]{1,0:T(8,128)(2,1)S(1)} %copy-done.2), channel_id=1, source_target_pairs={{0,8},{8,0},{16,24},{24,16},{1,9},{9,1},{17,25},{25,17},{2,10},{10... | collective-permute-start | bytes 1572872 | tf_op jit(solution)/shard_map/ppermute | solution.py:367
  11.0 50.1 %collective-permute-start.1 = (bf16[256,1024]{1,0:T(8,128)(2,1)S(1)}, bf16[256,1024]{1,0:T(8,128)(2,1)S(1)}, u32[]{:S(2)}, u32[]{:S(2)}) collective-permute-start(bf16[256,1024]{1,0:T(8,128)(2,1)S(1)} %copy-done.2), channel_id=1, source_target_pairs={{0,16},{8,24},{16,0},{24,8},{1,17},{9,25},{17,1},{25,9},{2,18},{10... | collective-permute-start | bytes 1572872 | tf_op jit(solution)/shard_map/ppermute | solution.py:367
  12.5 0.7 copy-start.6
  12.5 0.7 copy-start.9
  15.0 46.1 %collective-permute-start.2 = (bf16[256,1024]{1,0:T(8,128)(2,1)S(1)}, bf16[256,1024]{1,0:T(8,128)(2,1)S(1)}, u32[]{:S(2)}, u32[]{:S(2)}) collective-permute-start(bf16[256,1024]{1,0:T(8,128)(2,1)S(1)} %copy-done.2), channel_id=1, source_target_pairs={{0,24},{8,16},{16,8},{24,0},{1,25},{9,17},{17,9},{25,1},{2,26},{10... | collective-permute-start | bytes 1572872 | tf_op jit(solution)/shard_map/ppermute | solution.py:367
  23.8 25.3 %collective-permute-start.3 = (bf16[272,256]{1,0:T(8,128)(2,1)S(1)}, bf16[272,256]{1,0:T(8,128)(2,1)S(1)}, u32[]{:S(2)}, u32[]{:S(2)}) collective-permute-start(bf16[272,256]{1,0:T(8,128)(2,1)S(1)} %get-tuple-element.32), channel_id=1, source_target_pairs={{0,8},{8,0},{16,24},{24,16},{1,9},{9,1},{17,25},{25,17},{2,10},{10... | collective-permute-start | bytes 417800 | tf_op jit(solution)/shard_map/ppermute | solution.py:367
  25.9 12.1 %collective-permute-start.9 = (bf16[128,256]{1,0:T(8,128)(2,1)S(1)}, bf16[128,256]{1,0:T(8,128)(2,1)S(1)}, u32[]{:S(2)}, u32[]{:S(2)}) collective-permute-start(bf16[128,256]{1,0:T(8,128)(2,1)S(1)} %get-tuple-element.37), channel_id=1, source_target_pairs={{0,8},{8,0},{16,24},{24,16},{1,9},{9,1},{17,25},{25,17},{2,10},{10... | collective-permute-start | bytes 196616 | tf_op jit(solution)/shard_map/ppermute | solution.py:367
  38.0 4.3 %collective-permute-start.10 = (bf16[128,256]{1,0:T(8,128)(2,1)S(1)}, bf16[128,256]{1,0:T(8,128)(2,1)S(1)}, u32[]{:S(2)}, u32[]{:S(2)}) collective-permute-start(bf16[128,256]{1,0:T(8,128)(2,1)S(1)} %get-tuple-element.38), channel_id=1, source_target_pairs={{0,16},{8,24},{16,0},{24,8},{1,17},{9,25},{17,1},{25,9},{2,18},{10... | collective-permute-start | bytes 196616 | tf_op jit(solution)/shard_map/ppermute | solution.py:367
  42.3 5.3 %collective-permute-start.11 = (bf16[128,256]{1,0:T(8,128)(2,1)S(1)}, bf16[128,256]{1,0:T(8,128)(2,1)S(1)}, u32[]{:S(2)}, u32[]{:S(2)}) collective-permute-start(bf16[128,256]{1,0:T(8,128)(2,1)S(1)} %get-tuple-element.39), channel_id=1, source_target_pairs={{0,24},{8,16},{16,8},{24,0},{1,25},{9,17},{17,9},{25,1},{2,26},{10... | collective-permute-start | bytes 196616 | tf_op jit(solution)/shard_map/ppermute | solution.py:367
  47.6 5.6 %collective-permute-start.4 = (bf16[272,256]{1,0:T(8,128)(2,1)S(1)}, bf16[272,256]{1,0:T(8,128)(2,1)S(1)}, u32[]{:S(2)}, u32[]{:S(2)}) collective-permute-start(bf16[272,256]{1,0:T(8,128)(2,1)S(1)} %get-tuple-element.33), channel_id=1, source_target_pairs={{0,16},{8,24},{16,0},{24,8},{1,17},{9,25},{17,1},{25,9},{2,18},{10... | collective-permute-start | bytes 417800 | tf_op jit(solution)/shard_map/ppermute | solution.py:367
  49.1 12.4 %collective-permute-start.12 = (bf16[128,1024]{1,0:T(8,128)(2,1)S(1)}, bf16[128,1024]{1,0:T(8,128)(2,1)S(1)}, u32[]{:S(2)}, u32[]{:S(2)}) collective-permute-start(bf16[128,1024]{1,0:T(8,128)(2,1)S(1)} %maximum_maximum_fusion.refs_8_), channel_id=1, source_target_pairs={{0,1},{1,0},{2,3},{3,2},{4,5},{5,4},{6,7},{7,6},{8,9},{9,8},{10,11... | collective-permute-start | bytes 786440 | tf_op jit(solution)/shard_map/ppermute | solution.py:373
  53.2 6.4 %collective-permute-start.5 = (bf16[272,256]{1,0:T(8,128)(2,1)S(1)}, bf16[272,256]{1,0:T(8,128)(2,1)S(1)}, u32[]{:S(2)}, u32[]{:S(2)}) collective-permute-start(bf16[272,256]{1,0:T(8,128)(2,1)S(1)} %get-tuple-element.34), channel_id=1, source_target_pairs={{0,24},{8,16},{16,8},{24,0},{1,25},{9,17},{17,9},{25,1},{2,26},{10... | collective-permute-start | bytes 417800 | tf_op jit(solution)/shard_map/ppermute | solution.py:367
  59.6 5.9 %collective-permute-start.20 = (bf16[256,256]{1,0:T(8,128)(2,1)S(1)}, bf16[256,256]{1,0:T(8,128)(2,1)S(1)}, u32[]{:S(2)}, u32[]{:S(2)}) collective-permute-start(bf16[256,256]{1,0:T(8,128)(2,1)S(1)} %get-tuple-element.48), channel_id=1, source_target_pairs={{0,1},{1,0},{2,3},{3,2},{4,5},{5,4},{6,7},{7,6},{8,9},{9,8},{10,11... | collective-permute-start | bytes 393224 | tf_op jit(solution)/shard_map/ppermute | solution.py:373
  60.5 5.0 %collective-permute-start.21 = (bf16[256,256]{1,0:T(8,128)(2,1)S(1)}, bf16[256,256]{1,0:T(8,128)(2,1)S(1)}, u32[]{:S(2)}, u32[]{:S(2)}) collective-permute-start(bf16[256,256]{1,0:T(8,128)(2,1)S(1)} %slice.88), channel_id=1, source_target_pairs={{0,1},{1,0},{2,3},{3,2},{4,5},{5,4},{6,7},{7,6},{8,9},{9,8},{10,11... | collective-permute-start | bytes 393224 | tf_op jit(solution)/shard_map/ppermute | solution.py:373
  61.0 4.4 %collective-permute-start.22 = (bf16[256,256]{1,0:T(8,128)(2,1)S(1)}, bf16[256,256]{1,0:T(8,128)(2,1)S(1)}, u32[]{:S(2)}, u32[]{:S(2)}) collective-permute-start(bf16[256,256]{1,0:T(8,128)(2,1)S(1)} %slice.89), channel_id=1, source_target_pairs={{0,1},{1,0},{2,3},{3,2},{4,5},{5,4},{6,7},{7,6},{8,9},{9,8},{10,11... | collective-permute-start | bytes 393224 | tf_op jit(solution)/shard_map/ppermute | solution.py:373
  61.1 4.3 %collective-permute-start.23 = (bf16[256,256]{1,0:T(8,128)(2,1)S(1)}, bf16[256,256]{1,0:T(8,128)(2,1)S(1)}, u32[]{:S(2)}, u32[]{:S(2)}) collective-permute-start(bf16[256,256]{1,0:T(8,128)(2,1)S(1)} %slice.90), channel_id=1, source_target_pairs={{0,1},{1,0},{2,3},{3,2},{4,5},{5,4},{6,7},{7,6},{8,9},{9,8},{10,11... | collective-permute-start | bytes 393224 | tf_op jit(solution)/shard_map/ppermute | solution.py:373
  65.3 17.0 %collective-permute-start.13 = (bf16[4,256,256]{2,1,0:T(8,128)(2,1)S(1)}, bf16[4,256,256]{2,1,0:T(8,128)(2,1)S(1)}, u32[]{:S(2)}, u32[]{:S(2)}) collective-permute-start(bf16[4,256,256]{2,1,0:T(8,128)(2,1)S(1)} %get-tuple-element.41), channel_id=1, source_target_pairs={{0,1},{1,0},{2,3},{3,2},{4,5},{5,4},{6,7},{7,6},{8,9},{9,8},{10,11... | collective-permute-start | bytes 1572872 | tf_op jit(solution)/shard_map/ppermute | solution.py:373
  70.1 1.7 %collective-permute-start.24 = (bf16[128,1024]{1,0:T(8,128)(2,1)S(1)}, bf16[128,1024]{1,0:T(8,128)(2,1)S(1)}, u32[]{:S(2)}, u32[]{:S(2)}) collective-permute-start(bf16[128,1024]{1,0:T(8,128)(2,1)S(1)} %get-tuple-element.50), channel_id=1, source_target_pairs={{0,1},{1,0},{2,3},{3,2},{4,5},{5,4},{6,7},{7,6},{8,9},{9,8},{10,11... | collective-permute-start | bytes 786440 | tf_op jit(solution)/shard_map/ppermute | solution.py:373
  72.3 4.4 %collective-permute-start.25 = (bf16[32,1024]{1,0:T(8,128)(2,1)S(1)}, bf16[32,1024]{1,0:T(8,128)(2,1)S(1)}, u32[]{:S(2)}, u32[]{:S(2)}) collective-permute-start(bf16[32,1024]{1,0:T(8,128)(2,1)S(1)} %get-tuple-element.52), channel_id=1, source_target_pairs={{0,8},{8,0},{16,24},{24,16},{1,9},{9,1},{17,25},{25,17},{2,10},{10... | collective-permute-start | bytes 196616 | tf_op jit(solution)/shard_map/ppermute | solution.py:367
  73.5 5.7 %collective-permute-start.26 = (bf16[32,1024]{1,0:T(8,128)(2,1)S(1)}, bf16[32,1024]{1,0:T(8,128)(2,1)S(1)}, u32[]{:S(2)}, u32[]{:S(2)}) collective-permute-start(bf16[32,1024]{1,0:T(8,128)(2,1)S(1)} %get-tuple-element.53), channel_id=1, source_target_pairs={{0,16},{8,24},{16,0},{24,8},{1,17},{9,25},{17,1},{25,9},{2,18},{10... | collective-permute-start | bytes 196616 | tf_op jit(solution)/shard_map/ppermute | solution.py:367
  75.9 5.2 %collective-permute-start.27 = (bf16[32,1024]{1,0:T(8,128)(2,1)S(1)}, bf16[32,1024]{1,0:T(8,128)(2,1)S(1)}, u32[]{:S(2)}, u32[]{:S(2)}) collective-permute-start(bf16[32,1024]{1,0:T(8,128)(2,1)S(1)} %get-tuple-element.54), channel_id=1, source_target_pairs={{0,24},{8,16},{16,8},{24,0},{1,25},{9,17},{17,9},{25,1},{2,26},{10... | collective-permute-start | bytes 196616 | tf_op jit(solution)/shard_map/ppermute | solution.py:367
  81.7 7.8 %collective-permute-start.28 = (bf16[32,1024]{1,0:T(8,128)(2,1)S(1)}, bf16[32,1024]{1,0:T(8,128)(2,1)S(1)}, u32[]{:S(2)}, u32[]{:S(2)}) collective-permute-start(bf16[32,1024]{1,0:T(8,128)(2,1)S(1)} %get-tuple-element.56), channel_id=1, source_target_pairs={{0,2},{1,3},{2,0},{3,1},{4,6},{5,7},{6,4},{7,5},{8,10},{9,11},{10,... | collective-permute-start | bytes 196616 | tf_op jit(solution)/shard_map/ppermute | solution.py:370
  82.4 31.7 %copy-start.1 = (f32[256,1024]{1,0:T(8,128)S(1)}, f32[256,1024]{1,0:T(8,128)}, u32[]{:S(2)}) copy-start(f32[256,1024]{1,0:T(8,128)} %refs_4_.1) | copy-start | bytes 3145732
  82.5 20.9 %collective-permute-start.14 = (bf16[256,256]{1,0:T(8,128)(2,1)S(1)}, bf16[256,256]{1,0:T(8,128)(2,1)S(1)}, u32[]{:S(2)}, u32[]{:S(2)}) collective-permute-start(bf16[256,256]{1,0:T(8,128)(2,1)S(1)} %get-tuple-element.43), channel_id=1, source_target_pairs={{0,2},{1,3},{2,0},{3,1},{4,6},{5,7},{6,4},{7,5},{8,10},{9,11},{10,... | collective-permute-start | bytes 393224 | tf_op jit(solution)/shard_map/ppermute | solution.py:370
  83.9 19.4 %collective-permute-start.15 = (bf16[256,256]{1,0:T(8,128)(2,1)S(1)}, bf16[256,256]{1,0:T(8,128)(2,1)S(1)}, u32[]{:S(2)}, u32[]{:S(2)}) collective-permute-start(bf16[256,256]{1,0:T(8,128)(2,1)S(1)} %get-tuple-element.44), channel_id=1, source_target_pairs={{0,4},{1,5},{2,6},{3,7},{4,0},{5,1},{6,2},{7,3},{8,12},{9,13},{10,... | collective-permute-start | bytes 393224 | tf_op jit(solution)/shard_map/ppermute | solution.py:370
  86.1 17.2 %collective-permute-start.16 = (bf16[256,256]{1,0:T(8,128)(2,1)S(1)}, bf16[256,256]{1,0:T(8,128)(2,1)S(1)}, u32[]{:S(2)}, u32[]{:S(2)}) collective-permute-start(bf16[256,256]{1,0:T(8,128)(2,1)S(1)} %get-tuple-element.45), channel_id=1, source_target_pairs={{0,6},{1,7},{2,4},{3,5},{4,2},{5,3},{6,0},{7,1},{8,14},{9,15},{10,... | collective-permute-start | bytes 393224 | tf_op jit(solution)/shard_map/ppermute | solution.py:370
  87.5 15.1 %collective-permute-start.29 = (bf16[32,1024]{1,0:T(8,128)(2,1)S(1)}, bf16[32,1024]{1,0:T(8,128)(2,1)S(1)}, u32[]{:S(2)}, u32[]{:S(2)}) collective-permute-start(bf16[32,1024]{1,0:T(8,128)(2,1)S(1)} %get-tuple-element.57), channel_id=1, source_target_pairs={{0,4},{1,5},{2,6},{3,7},{4,0},{5,1},{6,2},{7,3},{8,12},{9,13},{10,... | collective-permute-start | bytes 196616 | tf_op jit(solution)/shard_map/ppermute | solution.py:370
  89.5 13.1 %collective-permute-start.30 = (bf16[32,1024]{1,0:T(8,128)(2,1)S(1)}, bf16[32,1024]{1,0:T(8,128)(2,1)S(1)}, u32[]{:S(2)}, u32[]{:S(2)}) collective-permute-start(bf16[32,1024]{1,0:T(8,128)(2,1)S(1)} %get-tuple-element.58), channel_id=1, source_target_pairs={{0,6},{1,7},{2,4},{3,5},{4,2},{5,3},{6,0},{7,1},{8,14},{9,15},{10,... | collective-permute-start | bytes 196616 | tf_op jit(solution)/shard_map/ppermute | solution.py:370
  102.7 5.0 %collective-permute-start.31 = (bf16[32,1024]{1,0:T(8,128)(2,1)S(1)}, bf16[32,1024]{1,0:T(8,128)(2,1)S(1)}, u32[]{:S(2)}, u32[]{:S(2)}) collective-permute-start(bf16[32,1024]{1,0:T(8,128)(2,1)S(1)} %sum_parts.1.refs_0_), channel_id=1, source_target_pairs={{0,8},{8,0},{16,24},{24,16},{1,9},{9,1},{17,25},{25,17},{2,10},{10... | collective-permute-start | bytes 196616 | tf_op jit(solution)/shard_map/ppermute | solution.py:367
  103.4 10.7 %collective-permute-start.17 = (bf16[256,256]{1,0:T(8,128)(2,1)S(1)}, bf16[256,256]{1,0:T(8,128)(2,1)S(1)}, u32[]{:S(2)}, u32[]{:S(2)}) collective-permute-start(bf16[256,256]{1,0:T(8,128)(2,1)S(1)} %sum_rows.1.refs_0_), channel_id=1, source_target_pairs={{0,8},{8,0},{16,24},{24,16},{1,9},{9,1},{17,25},{25,17},{2,10},{10... | collective-permute-start | bytes 393224 | tf_op jit(solution)/shard_map/ppermute | solution.py:367
  104.9 9.2 %collective-permute-start.18 = (bf16[256,256]{1,0:T(8,128)(2,1)S(1)}, bf16[256,256]{1,0:T(8,128)(2,1)S(1)}, u32[]{:S(2)}, u32[]{:S(2)}) collective-permute-start(bf16[256,256]{1,0:T(8,128)(2,1)S(1)} %sum_rows.1.refs_0_), channel_id=1, source_target_pairs={{0,16},{8,24},{16,0},{24,8},{1,17},{9,25},{17,1},{25,9},{2,18},{10... | collective-permute-start | bytes 393224 | tf_op jit(solution)/shard_map/ppermute | solution.py:367
  105.3 8.8 %collective-permute-start.19 = (bf16[256,256]{1,0:T(8,128)(2,1)S(1)}, bf16[256,256]{1,0:T(8,128)(2,1)S(1)}, u32[]{:S(2)}, u32[]{:S(2)}) collective-permute-start(bf16[256,256]{1,0:T(8,128)(2,1)S(1)} %sum_rows.1.refs_0_), channel_id=1, source_target_pairs={{0,24},{8,16},{16,8},{24,0},{1,25},{9,17},{17,9},{25,1},{2,26},{10... | collective-permute-start | bytes 393224 | tf_op jit(solution)/shard_map/ppermute | solution.py:367
  106.9 5.0 %collective-permute-start.32 = (bf16[32,1024]{1,0:T(8,128)(2,1)S(1)}, bf16[32,1024]{1,0:T(8,128)(2,1)S(1)}, u32[]{:S(2)}, u32[]{:S(2)}) collective-permute-start(bf16[32,1024]{1,0:T(8,128)(2,1)S(1)} %sum_parts.1.refs_0_), channel_id=1, source_target_pairs={{0,16},{8,24},{16,0},{24,8},{1,17},{9,25},{17,1},{25,9},{2,18},{10... | collective-permute-start | bytes 196616 | tf_op jit(solution)/shard_map/ppermute | solution.py:367
  107.7 5.2 %collective-permute-start.33 = (bf16[32,1024]{1,0:T(8,128)(2,1)S(1)}, bf16[32,1024]{1,0:T(8,128)(2,1)S(1)}, u32[]{:S(2)}, u32[]{:S(2)}) collective-permute-start(bf16[32,1024]{1,0:T(8,128)(2,1)S(1)} %sum_parts.1.refs_0_), channel_id=1, source_target_pairs={{0,24},{8,16},{16,8},{24,0},{1,25},{9,17},{17,9},{25,1},{2,26},{10... | collective-permute-start | bytes 196616 | tf_op jit(solution)/shard_map/ppermute | solution.py:367
  114.1 0.7 copy-start.8

commit v2 on v0

--- a/solution.py
+++ b/solution.py
@@ -1,10 +1,23 @@
+import functools
+
 import jax
 import jax.numpy as jnp
 from jax import lax
+from jax.experimental import pallas as pl
+from jax.experimental.pallas import tpu as pltpu
 from jax.sharding import PartitionSpec as P
 
 HEADS = 8
 MAXLEN = 128
+PASS_COST = 12 * 10**9
+GATE_COST = 8 * 10**9
+EXTRA = 16
+VMEM = pl.BlockSpec(memory_space=pltpu.VMEM)
+ANY = pl.BlockSpec(memory_space=pl.ANY)
+HBM = pl.BlockSpec(memory_space=pltpu.HBM)
+SMEM = pl.BlockSpec(memory_space=pltpu.SMEM)
+F32 = jnp.float32
+BF16 = jnp.bfloat16
 
 
 def adagrad(table_rows, accum_rows, grad_rows):
@@ -13,7 +26,9 @@
     return (new_table, new_accum)
 
 
-def body(table, accum, owner, local_row, lengths, queries, keys, cotangent, out_weight):
+def general_body(
+    table, accum, owner, local_row, lengths, queries, keys, cotangent, out_weight
+):
     shards = lax.axis_size("shard")
     tok = owner.shape[0]
     rows_dev = table.shape[0]
@@ -112,6 +127,428 @@
     return (new_table, new_accum, weight_grad)
 
 
+def iota(shape, axis):
+    return lax.broadcasted_iota(jnp.int32, shape, axis)
+
+
+def nt(a, b):
+    return lax.dot_general(a, b, (((1,), (1,)), ((), ())), preferred_element_type=F32)
+
+
+def nn(a, b):
+    return lax.dot_general(a, b, (((1,), (0,)), ((), ())), preferred_element_type=F32)
+
+
+def call(kernel, name, out, ins, smem=0, after=(), scratch=(), hbm=(), limit=32 << 20, cost=0, placed=False):
+    n_in, n_after = len(ins), len(after)
+    many = isinstance(out, (list, tuple))
+
+    def run(*refs):
+        refs = (*refs[:n_in], *refs[n_in + n_after :])
+        if placed:
+            shard = lax.axis_index("shard")
+            kernel((lax.axis_index("replica"), shard // 2, shard % 2), *refs)
+        else:
+            kernel(*refs)
+
+    return pl.pallas_call(
+        run,
+        out_shape=out,
+        in_specs=[SMEM if i < smem else HBM if i in hbm else VMEM for i in range(n_in)]
+        + [ANY] * n_after,
+        out_specs=[VMEM] * len(out) if many else VMEM,
+        scratch_shapes=list(scratch),
+        name=name,
+        cost_estimate=pl.CostEstimate(flops=cost, bytes_accessed=0, transcendentals=0),
+        compiler_params=pltpu.CompilerParams(vmem_limit_bytes=limit),
+    )(*ins, *after)
+
+
+def sds(shape, dtype=BF16):
+    return jax.ShapeDtypeStruct(shape, dtype)
+
+
+def aligned(index, size):
+    return pl.ds(pl.multiple_of(index * size, size), size)
+
+
+def start_all(pairs, sem):
+    copies = [pltpu.make_async_copy(a, b, sem.at[i]) for i, (a, b) in enumerate(pairs)]
+    for c in copies:
+        c.start()
+    return copies
+
+
+def pack_kernel(me, lens, owner, local, q, k, weight, table, out, out_z, rows_in, part_in, sem):
+    n, _, pw = out.shape
+    pw = pw // 2
+    tok = q.shape[0]
+    rows, cols = rows_in.shape
+    part = part_in.shape[0]
+    copies = start_all(
+        [
+            (table.at[:, aligned(me[0], cols)], rows_in),
+            (weight.at[aligned(me[0], part), :], part_in),
+        ]
+        + [
+            (x.at[:, i * pw : (i + 1) * pw], out.at[i, 0:tok, j * pw : (j + 1) * pw])
+            for i in range(n)
+            for j, x in enumerate((q, k))
+        ],
+        sem,
+    )
+    lane = iota((EXTRA, tok), 1)
+    row = iota((EXTRA, tok), 0)
+    seg = jnp.zeros((EXTRA, tok), F32)
+    end = jnp.int32(0)
+    for i in range(lens.shape[1]):
+        end = end + lens[0, i]
+        seg = seg + jnp.where(lane >= end, 1.0, 0.0)
+    ids = jnp.where(
+        row == 0,
+        jnp.broadcast_to(owner[...].astype(F32), (EXTRA, tok)),
+        jnp.where(
+            row == 1,
+            jnp.broadcast_to(local[...].astype(F32), (EXTRA, tok)),
+            jnp.where(row == 2, seg, 0.0),
+        ),
+    ).astype(BF16)
+    for i in range(n):
+        out[i, tok : tok + EXTRA, :] = ids
+    copies[0].wait()
+    out_z[0:cols, :] = rows_in[...].T.astype(BF16)
+    copies[1].wait()
+    for i in range((out_z.shape[0] - cols) // part):
+        out_z[cols + i * part : cols + (i + 1) * part, :] = part_in[:, i * rows : (i + 1) * rows]
+    for c in copies[2:]:
+        c.wait()
+
+
+def pass_kernel(x, y, far_y, far_x, sem):
+    half = far_x.shape[0]
+    copies = start_all([(x.at[half:, :], far_y), (y.at[0:half, :], far_x)], sem)
+    for c in copies:
+        c.wait()
+
+
+def sort_kernel(me, *refs):
+    *blocks, out_t, out_w = refs
+    _, cols, rows = out_t.shape
+    part = out_w.shape[1]
+    for m, p in enumerate(blocks):
+        z = me[1] ^ m
+        out_t[z] = p[0:cols, :]
+        for i in range((p.shape[0] - cols) // part):
+            out_w[z, :, i * rows : (i + 1) * rows] = p[cols + i * part : cols + (i + 1) * part, :]
+
+
+def gate_kernel(out):
+    out[...] = jnp.zeros_like(out)
+
+
+def choose_kernel(me, *refs):
+    n = (len(refs) - 1) // 2
+    parts, out, held = refs[:n], refs[n : 2 * n], refs[2 * n]
+    for m, p in enumerate(parts):
+        held[m] = p[...]
+    for m, o in enumerate(out):
+        o[...] = held[me[1] ^ me[0] ^ m]
+
+
+def weights_kernel(me, packs, out):
+    n, tok, pw = packs.shape
+    tok, pw = tok - EXTRA, pw // 2
+    heads = out.shape[1]
+    dqk = pw // heads
+    down, across = iota((tok, tok), 0), iota((tok, tok), 1)
+    lane = iota((tok, pw), 1)
+    for r in range(n):
+        p = packs.at[me[0] ^ r]
+        q = p[0:tok, 0:pw]
+        k = p[0:tok, pw : 2 * pw]
+        seg = ids_of(packs, me[0] ^ r)[2:3, :]
+        seg_down = jnp.sum(jnp.where(down == across, seg, 0.0), axis=1, keepdims=True)
+        mask = (seg == seg_down) & (down <= across)
+        for j in range(heads):
+            kj = jnp.where(lane // dqk == j, k, jnp.zeros_like(k))
+            s = nt(kj, q) * dqk ** (-0.5)
+            w = s / (1.0 + jnp.exp(-s)) * (1.0 / MAXLEN)
+            out[r, j] = jnp.where(mask, w, 0.0).astype(BF16)
+
+
+def ids_of(packs, r):
+    rows = packs.shape[1]
+    return packs[r, rows - EXTRA : rows, :].astype(F32)
+
+
+def one_hot(ids, rows):
+    tok = ids.shape[1]
+    own = ids[0:1, :]
+    loc = ids[1:2, :]
+    at = iota((rows, tok), 0).astype(F32)
+    return jnp.broadcast_to(own, (rows, tok)), at == loc
+
+
+def mix_kernel(me, packs, w, mine, other, out):
+    n, cols, rows = mine.shape
+    heads, tok = w.shape[1:3]
+    dv = cols // heads
+    for r in range(n):
+        own, hit = one_hot(ids_of(packs, me[0] ^ r), rows)
+        vals = jnp.zeros((cols, tok), F32)
+        for z in range(n):
+            for cc, blocks in enumerate((mine, other)):
+                shard = (2 * z + (me[2] ^ cc)).astype(F32)
+                pick = jnp.where(hit & (own == shard), 1.0, 0.0).astype(BF16)
+                vals = vals + nn(blocks[z], pick)
+        vals = vals.astype(BF16)
+        for j in range(heads):
+            out[j * dv : (j + 1) * dv, r * tok : (r + 1) * tok] = nn(
+                vals[j * dv : (j + 1) * dv, :], w[r, j]
+            ).astype(BF16)
+
+
+def back_kernel(me, packs, ow_mine, ow_other, w, *refs):
+    *cots, keep, send, ow, grad = refs
+    n = packs.shape[0]
+    heads, tok = w.shape[1:3]
+    head_rows = ow_mine.shape[0]
+    rows = send.shape[1]
+    ow[aligned(me[2], head_rows), :] = ow_mine[...]
+    ow[aligned(1 - me[2], head_rows), :] = ow_other[...]
+    first = 0
+    for cot in cots:
+        end = first + cot.shape[0]
+        grad[first:end, :] = nt(cot[...], ow[...]).astype(BF16)
+        first = end
+    for r in range(n):
+        at_r = slice(r * tok, (r + 1) * tok)
+        for j in range(heads):
+            at_j = slice(j * head_rows, (j + 1) * head_rows)
+            grad[at_r, at_j] = nn(w[r, j], grad[at_r, at_j]).astype(BF16)
+    for cc in (1, 0):
+        for z in range(n):
+            shard = (2 * z + (me[2] ^ cc)).astype(F32)
+            total = jnp.zeros((rows, heads * head_rows), F32)
+            for r in range(n):
+                own, hit = one_hot(ids_of(packs, me[0] ^ r), rows)
+                pick = jnp.where(hit & (own == shard), 1.0, 0.0).astype(BF16)
+                total = total + nn(pick, grad[r * tok : (r + 1) * tok, :])
+            if cc == 0:
+                keep[z] = total
+            else:
+                send[z] = total.astype(BF16)
+
+
+def wgrad_kernel(me, mixed, *refs):
+    *cots, keep, send = refs
+    rows = keep.shape[0]
+    for cc, out in ((1, send), (0, keep)):
+        at = aligned(me[2] ^ cc, rows)
+        total = jnp.zeros(keep.shape, F32)
+        first = 0
+        for cot in cots:
+            end = first + cot.shape[0]
+            total = total + nn(mixed[at, first:end], cot[...])
+            first = end
+        out[...] = total.astype(out.dtype)
+
+
+def add_kernel(keep, got, out):
+    out[...] = (keep[...] + got[...].astype(F32)).astype(out.dtype)
+
+
+def add_parts_kernel(me, keep, got, *out):
+    rows = out[0].shape[0]
+    for m, o in enumerate(out):
+        at = aligned(me[0] ^ m, rows)
+        o[...] = (keep[at, :] + got[at, :].astype(F32)).astype(o.dtype)
+
+
+def sum_first_kernel(parts, out):
+    total = parts[0].astype(F32)
+    for m in range(1, parts.shape[0]):
+        total = total + parts[m].astype(F32)
+    out[...] = total.astype(out.dtype)
+
+
+def sum_kernel(*refs):
+    *parts, out = refs
+    total = parts[0][...].astype(F32)
+    for p in parts[1:]:
+        total = total + p[...].astype(F32)
+    out[...] = total.astype(out.dtype)
+
+
+def place_kernel(me, *refs):
+    *parts, out = refs
+    rows = parts[0].shape[0]
+    for m, p in enumerate(parts):
+        out[aligned(me[0] ^ m, rows), :] = p[...]
+
+
+def update_kernel(me, table, accum, *refs):
+    *parts, new_table, new_accum, grad = refs
+    rows, width = table.shape
+    cols = width // len(parts)
+    for m, p in enumerate(parts):
+        grad[:, aligned(me[0] ^ m, cols)] = p[...].astype(F32)
+    mean = jnp.sum(grad[...] * grad[...], axis=1, keepdims=True) * (1.0 / width)
+    same = iota((rows, rows), 0) == iota((rows, rows), 1)
+    old = jnp.sum(jnp.where(same, accum[...], 0.0), axis=1, keepdims=True)
+    fresh = old + mean
+    new_accum[...] = jnp.sum(jnp.where(same, fresh, 0.0), axis=0, keepdims=True)
+    new_table[...] = table[...] - grad[...] / (jnp.sqrt(fresh) + 1e-08)
+
+
+def body(table, accum, owner, local_row, lengths, queries, keys, cotangent, out_weight):
+    n = lax.axis_size("replica")
+    shards = lax.axis_size("shard")
+    tok = owner.shape[0]
+    rows, width = table.shape
+    cols = width // n
+    heads = HEADS // n
+    part = out_weight.shape[0] // n
+
+    def column(x, m):
+        return lax.ppermute(x, "replica", [(i, i ^ m) for i in range(n)]) if m else x
+
+    def along(x, m):
+        return lax.ppermute(x, "shard", [(i, i ^ (2 * m)) for i in range(shards)]) if m else x
+
+    def core(x):
+        return lax.ppermute(x, "shard", [(i, i ^ 1) for i in range(shards)])
+
+    def swap_along(x):
+        groups = [list(range(c, shards, 2)) for c in range(2)]
+        return lax.all_to_all(x, "shard", 0, 0, tiled=True, axis_index_groups=groups)
+
+    def swap_columns(x):
+        return lax.all_to_all(x, "replica", 0, 0, tiled=True)
+
+    half = tok // 2
+    x, y = column(cotangent, 1), column(cotangent, 2)
+    zrows = cols + part * width // rows
+    packs, zpay = call(
+        pack_kernel,
+        "pack",
+        [sds((n, tok + EXTRA, 2 * queries.shape[1] // n)), sds((zrows, rows))],
+        (
+            lengths,
+            owner.reshape(1, tok),
+            local_row.reshape(1, tok),
+            queries,
+            keys,
+            out_weight,
+            table,
+        ),
+        smem=1,
+        hbm=(3, 4, 5, 6),
+        scratch=[
+            pltpu.VMEM((rows, cols), F32),
+            pltpu.VMEM((part, width), BF16),
+            pltpu.SemaphoreType.DMA((2 * n + 2,)),
+        ],
+        limit=None,
+        placed=True,
+    )
+    packs = swap_columns(packs)
+    blocks = [along(zpay, m) for m in range(n)]
+    far_y, far_x = call(
+        pass_kernel,
+        "pass",
+        [sds((half, width))] * 2,
+        (x, y),
+        scratch=[pltpu.SemaphoreType.DMA((2,))],
+        cost=PASS_COST,
+    )
+    w = call(
+        weights_kernel,
+        "weights",
+        sds((n, heads, tok, tok)),
+        (packs,),
+        after=(far_x,),
+        placed=True,
+    )
+    mine, owp = call(
+        sort_kernel,
+        "sort",
+        [sds((n, cols, rows)), sds((n, part, width))],
+        blocks,
+        after=(w,),
+        placed=True,
+    )
+    other = core(mine)
+    ow_mine = swap_columns(owp).reshape(n * part, width)
+    ow_other = core(ow_mine)
+    far_y, far_x = column(far_y, 2), column(far_x, 1)
+    cots = [cotangent, x, y, far_x, far_y]
+    here = call(gate_kernel, "gate", sds((8, 128), F32), (), after=(far_x, far_y), cost=GATE_COST)
+
+    keep, send = call(
+        back_kernel,
+        "back",
+        [sds((n, rows, cols), F32), sds((n, rows, cols))],
+        (packs, ow_mine, ow_other, w, *cots),
+        after=(here,),
+        scratch=[pltpu.VMEM((cols, width), BF16), pltpu.VMEM((n * tok, cols), BF16)],
+        placed=True,
+    )
+    sums = call(add_kernel, "add", sds((n, rows, cols)), (keep, core(send)))
+    mixed = call(
+        mix_kernel,
+        "mix",
+        sds((cols, n * tok)),
+        (packs, w, mine, other),
+        after=(sums,),
+        placed=True,
+    )
+    sums = swap_along(sums)
+    wkeep, wsend = call(
+        wgrad_kernel,
+        "wgrad",
+        [sds((n * part, width), F32), sds((n * part, width))],
+        (mixed, *cots),
+        placed=True,
+    )
+    wgot = core(wsend)
+
+    wparts = call(
+        add_parts_kernel, "add_parts", [sds((part, width))] * n, (wkeep, wgot), placed=True
+    )
+    wparts = [column(p, m) for m, p in enumerate(wparts)]
+    wparts = call(
+        choose_kernel,
+        "pick",
+        [sds((part, width))] * n,
+        wparts,
+        placed=True,
+        scratch=[pltpu.VMEM((n, part, width), BF16)],
+    )
+    wready = wparts[0]
+    wparts = [along(p, m) for m, p in enumerate(wparts)]
+
+    grad = call(sum_first_kernel, "sum_rows", sds((rows, cols)), (sums,), after=(wready,))
+    grads = [column(grad, m) for m in range(n)]
+    wsum = call(sum_kernel, "sum_parts", sds((part, width)), wparts, after=(grads[1],))
+    wsums = [column(wsum, m) for m in range(n)]
+    new_table, new_accum = call(
+        update_kernel,
+        "update",
+        [sds((rows, width), F32), sds((1, rows), F32)],
+        (table, accum.reshape(1, rows), *grads),
+        placed=True,
+        scratch=[pltpu.VMEM((rows, width), F32)],
+    )
+    weight_grad = call(place_kernel, "place", sds((n * part, width)), wsums, placed=True)
+    return (new_table, new_accum.reshape(rows), weight_grad)
+
+
+def fits(mesh):
+    n, shards = mesh.shape["replica"], mesh.shape["shard"]
+    return n & (n - 1) == 0 and shards == HEADS and 2 * n == HEADS
+
+
 def solution(mesh):
     placed = (
         P("shard", None),
@@ -125,7 +562,7 @@
         P("shard", None),
     )
     return jax.shard_map(
-        body,
+        body if fits(mesh) else general_body,
         mesh=mesh,
         in_specs=placed,
         out_specs=(P("shard", None), P("shard"), P("shard", None)),

time: 223 us -> 89.3 us (0.40)
  waiting for transfers between devices: 135 us -> 22.6 us
  starting transfers between devices: 13.7 us -> 36 us
  Pallas kernels: 0 us -> 19.6 us
  blocking collectives: 26.6 us -> 8.25 us
  between operations: 14.7 us -> 0.83 us
  local copies, waits for them, and re-layouts: 15.3 us -> 1.61 us
  matrix products: 8.92 us -> 0 us
  other arithmetic: 7.75 us -> 0 us
    reduce_scatter x2 -> x0, waiting for transfers between devices: 68 us -> none  [the longest x1 52.3 us: body(): lax.psum_scatter(lax.dot_general(mixed, cotangent, (((0,), (0,)), ((), ()...]
    all_gather x2 -> x0, waiting for transfers between devices: 34.9 us -> none  [the longest x1 19.3 us: body(): lax.all_gather(out_weight, 'shard', axis=0, tiled=True)]
    all_to_all x3 -> x2, waiting for transfers between devices: 31.6 us -> 2.94 us  [the longest x1 2.94 us: swap_columns(): return lax.all_to_all(x, 'replica', 0, 0, tiled=True)]
    ppermute x0 -> x23, starting transfers between devices: none -> 27.6 us  [the longest x13 18 us: column(): lax.ppermute(x, 'replica', [(i, i ^ m) for i in range(n)])]
    unnamed x1 -> x0, blocking collectives: 26.6 us -> none
    ppermute x0 -> x23, waiting for transfers between devices: none -> 19.7 us  [the longest x13 9.19 us: column(): lax.ppermute(x, 'replica', [(i, i ^ m) for i in range(n)])]
    pallas_call x0 -> x15, Pallas kernels: none -> 19.6 us  [call(): pl.pallas_call(run, out_shape=out, in_specs=[SMEM if i < smem else HBM if...]
    dot_general x7 -> x0, matrix products: 8.92 us -> none  [the longest x1 2.64 us: body(): lax.dot_general(mixed, cotangent, (((0,), (0,)), ((), ())), preferred_ele...]
  transfers between devices with their start and end apart: 7 -> 25, of which waited for: 6 -> 12; matrix products, arithmetic and copies ran while one was open for 12% -> 0% of each run, Pallas kernels for 0% -> 18%
where the time goes in v2:
time: 89.3 us; the launch traced here: 88.9 us
  starting transfers between devices  36 us (40%)
  waiting for transfers between devices  22.6 us (25%)
  Pallas kernels  19.6 us (22%)
  blocking collectives  8.25 us (9%)
  local copies, waits for them, and re-layouts  1.61 us (2%)
    pallas_call x15, Pallas kernels, call(): pl.pallas_call(run, out_shape=out, in_specs=[SMEM if i < smem else HBM if...  19.6 us
    ppermute x13, starting transfers between devices, column(): lax.ppermute(x, 'replica', [(i, i ^ m) for i in range(n)])  18 us
    ppermute x13, waiting for transfers between devices, column(): lax.ppermute(x, 'replica', [(i, i ^ m) for i in range(n)])  9.19 us
    ppermute x6, starting transfers between devices, along(): lax.ppermute(x, 'shard', [(i, i ^ 2 * m) for i in range(shards)])  8.93 us
    all_to_all x1, blocking collectives, swap_columns(): return lax.all_to_all(x, 'replica', 0, 0, tiled=True)  8.25 us
    ppermute x6, waiting for transfers between devices, along(): lax.ppermute(x, 'shard', [(i, i ^ 2 * m) for i in range(shards)])  6.06 us
    all_to_all x1, starting transfers between devices, swap_along(): lax.all_to_all(x, 'shard', 0, 0, tiled=True, axis_index_groups=groups)  4.87 us
    ppermute x4, waiting for transfers between devices, core(): return lax.ppermute(x, 'shard', [(i, i ^ 1) for i in range(shards)])  4.43 us
  transfers between devices with their start and end apart: 25, of which 12 were waited for; matrix products, arithmetic and copies ran while one was open for 0% of the time, Pallas kernels for 18%

profile of v2, /device:TPU:0, one launch (start us, length us, event | category | flops | bytes accessed | tf_op | source)
XLA Modules:
  0.0 88.9 jit_solution(3265898585615352012)
XLA Ops:
  0.6 3.0 %collective-permute-start.3 = (bf16[256,1024]{1,0:T(8,128)(2,1)}, bf16[256,1024]{1,0:T(8,128)(2,1)S(1)}, u32[]{:S(2)}, u32[]{:S(2)}) collective-permute-start(bf16[256,1024]{1,0:T(8,128)(2,1)} %refs_1_.1), channel_id=1, source_target_pairs={{0,8},{8,0},{16,24},{24,16},{1,9},{9,1},{17,25},{25,17},{2,10},{10... | collective-permute-start | bytes 1572872 | tf_op jit(solution)/shard_map/ppermute | solution.py:414
  3.6 1.5 %collective-permute-start.4 = (bf16[256,1024]{1,0:T(8,128)(2,1)}, bf16[256,1024]{1,0:T(8,128)(2,1)S(1)}, u32[]{:S(2)}, u32[]{:S(2)}) collective-permute-start(bf16[256,1024]{1,0:T(8,128)(2,1)} %refs_1_.1), channel_id=1, source_target_pairs={{0,16},{8,24},{16,0},{24,8},{1,17},{9,25},{17,1},{25,9},{2,18},{10... | collective-permute-start | bytes 1572872 | tf_op jit(solution)/shard_map/ppermute | solution.py:414
  5.2 2.8 %pack.1 = (bf16[4,272,256]{2,1,0:T(8,128)(2,1)}, bf16[384,256]{1,0:T(8,128)(2,1)}) custom-call(s32[1,4]{1,0:T(1,128)} %refs_0_.2, s32[1,256]{1,0:T(1,128)} %bitcast.8, s32[1,256]{1,0:T(1,128)} %bitcast.9, bf16[256,512]{1,0:T(8,128)(2,1)} %refs_3_.1, bf16[256,512]{1,0:T(8,128)(2,1)} %refs_4_.2, bf16[128,1024]{1,0:T(8,128)(2,1)} %refs_5_.1, f32[256,1024]{1,0:T(8,128)} %refs_0_.3), custom_call_target="tpu_custom_call" | custom-call | tf_op jit(solution)/shard_map/pack/pallas_call | solution.py:154
  8.0 1.6 %collective-permute-start = (bf16[384,256]{1,0:T(8,128)(2,1)}, bf16[384,256]{1,0:T(8,128)(2,1)S(1)}, u32[]{:S(2)}, u32[]{:S(2)}) collective-permute-start(bf16[384,256]{1,0:T(8,128)(2,1)} %get-tuple-element.24.refs_0_), channel_id=1, source_target_pairs={{0,2},{1,3},{2,0},{3,1},{4,6},{5,7},{6,4},{7,5},{8,10},{9,11},{10,... | collective-permute-start | bytes 589832 | tf_op jit(solution)/shard_map/ppermute | solution.py:417
  9.6 2.6 %collective-permute-start.1 = (bf16[384,256]{1,0:T(8,128)(2,1)}, bf16[384,256]{1,0:T(8,128)(2,1)}, u32[]{:S(2)}, u32[]{:S(2)}) collective-permute-start(bf16[384,256]{1,0:T(8,128)(2,1)} %get-tuple-element.24.refs_0_), channel_id=1, source_target_pairs={{0,4},{1,5},{2,6},{3,7},{4,0},{5,1},{6,2},{7,3},{8,12},{9,13},{10,... | collective-permute-start | bytes 589832 | tf_op jit(solution)/shard_map/ppermute | solution.py:417
  12.2 0.2 collective-permute-start.2
  12.4 3.5 %all-to-all-start = ((bf16[4,272,256]{2,1,0:T(8,128)(2,1)}), bf16[4,272,256]{2,1,0:T(8,128)(2,1)S(1)}, u32[]{:S(2)}, u32[]{:S(2)}) async-start(bf16[4,272,256]{2,1,0:T(8,128)(2,1)} %get-tuple-element.23), calls=%async_computation | async-start | bytes 1114112 | tf_op jit(solution)/shard_map/all_to_all | solution.py:427
  15.9 3.1 %collective-permute-done.4.refs_1_.refs_6_.refs_3_ = bf16[256,1024]{1,0:T(8,128)(2,1)S(1)} collective-permute-done((bf16[256,1024]{1,0:T(8,128)(2,1)}, bf16[256,1024]{1,0:T(8,128)(2,1)S(1)}, u32[]{:S(2)}, u32[]{:S(2)}) %collective-permute-start.4) | collective-permute-done | bytes 524320 | tf_op jit(solution)/shard_map/ppermute | solution.py:414
  19.0 0.9 pass.1
  19.9 2.8 %collective-permute-start.7 = (bf16[128,1024]{1,0:T(8,128)(2,1)}, bf16[128,1024]{1,0:T(8,128)(2,1)}, u32[]{:S(2)}, u32[]{:S(2)}) collective-permute-start(bf16[128,1024]{1,0:T(8,128)(2,1)} %get-tuple-element.27), channel_id=1, source_target_pairs={{0,16},{8,24},{16,0},{24,8},{1,17},{9,25},{17,1},{25,9},{2,18},{10... | collective-permute-start | bytes 786440 | tf_op jit(solution)/shard_map/ppermute | solution.py:414
  22.7 2.9 %all-to-all-done.refs_0_ = bf16[4,272,256]{2,1,0:T(8,128)(2,1)S(1)} async-done(((bf16[4,272,256]{2,1,0:T(8,128)(2,1)}), bf16[4,272,256]{2,1,0:T(8,128)(2,1)S(1)}, u32[]{:S(2)}, u32[]{:S(2)}) %all-to-all-start) | async-done | bytes 557088 | tf_op jit(solution)/shard_map/all_to_all | solution.py:427
  25.7 0.8 weights.1.refs_4_.refs_3_.refs_1_
  26.5 0.7 copy-done.3
  27.2 0.9 %copy-done.4 = bf16[384,256]{1,0:T(8,128)(2,1)S(1)} copy-done((bf16[384,256]{1,0:T(8,128)(2,1)S(1)}, bf16[384,256]{1,0:T(8,128)(2,1)}, u32[]{:S(2)}) %copy-start.4) | copy-done | bytes 196632
  28.1 1.9 %sort.1 = (bf16[4,256,256]{2,1,0:T(8,128)(2,1)}, bf16[4,32,1024]{2,1,0:T(8,128)(2,1)S(1)}) custom-call(bf16[384,256]{1,0:T(8,128)(2,1)S(1)} %copy-done.2, bf16[384,256]{1,0:T(8,128)(2,1)S(1)} %copy-done.4, bf16[384,256]{1,0:T(8,128)(2,1)} %collective-permute-done.1.refs_2_, bf16[384,256]{1,0:T(8,128)(2,1)} %collective-permute-done.2.refs_3_, ...), custom_call_target="tpu_custom_call" | custom-call | tf_op jit(solution)/shard_map/sort/pallas_call | solution.py:154
  30.0 8.2 %all_to_all.15 = bf16[4,32,1024]{2,1,0:T(8,128)(2,1)S(1)} all-to-all(bf16[4,32,1024]{2,1,0:T(8,128)(2,1)S(1)} %get-tuple-element.26), channel_id=1, replica_groups=mesh['replica'=4,'shard'=8] {'replica'}, dimensions={0} | all-to-all | bytes 524288 | tf_op jit(solution)/shard_map/all_to_all | solution.py:427
  38.3 1.5 %collective-permute-done.5.refs_2_ = bf16[128,1024]{1,0:T(8,128)(2,1)S(1)} collective-permute-done((bf16[128,1024]{1,0:T(8,128)(2,1)S(1)}, bf16[128,1024]{1,0:T(8,128)(2,1)S(1)}, u32[]{:S(2)}, u32[]{:S(2)}) %collective-permute-start.5) | collective-permute-done | bytes 262176 | tf_op jit(solution)/shard_map/ppermute | solution.py:420
  39.8 3.3 %back.1 = (f32[4,256,256]{2,1,0:T(8,128)S(1)}, bf16[4,256,256]{2,1,0:T(8,128)(2,1)S(1)}) custom-call(bf16[4,272,256]{2,1,0:T(8,128)(2,1)S(1)} %all-to-all-done.refs_0_, bf16[128,1024]{1,0:T(8,128)(2,1)S(1)} %bitcast.6, bf16[128,1024]{1,0:T(8,128)(2,1)S(1)} %collective-permute-done.5.refs_2_, bf16[4,2,256,256]{3,2,1,0:T(8,128)(2,1)S(1)} %weights.1.refs_4_.refs_3_.refs_1_, ...), custom_call_target="tpu_custom_call" | custom-call | tf_op jit(solution)/shard_map/back/pallas_call | solution.py:154
  43.1 0.2 collective-permute-start.8
  43.3 0.4 collective-permute-start.9
  43.7 1.4 %collective-permute-done.8.refs_1_ = bf16[4,256,256]{2,1,0:T(8,128)(2,1)S(1)} collective-permute-done((bf16[4,256,256]{2,1,0:T(8,128)(2,1)S(1)}, bf16[4,256,256]{2,1,0:T(8,128)(2,1)S(1)}, u32[]{:S(2)}, u32[]{:S(2)}) %collective-permute-start.8) | collective-permute-done | bytes 524320 | tf_op jit(solution)/shard_map/ppermute | solution.py:420
  45.1 0.9 %add.1.refs_4_ = bf16[4,256,256]{2,1,0:T(8,128)(2,1)} custom-call(f32[4,256,256]{2,1,0:T(8,128)S(1)} %get-tuple-element.28.refs_0_, bf16[4,256,256]{2,1,0:T(8,128)(2,1)S(1)} %collective-permute-done.8.refs_1_), custom_call_target="tpu_custom_call" | custom-call | tf_op jit(solution)/shard_map/add/pallas_call | solution.py:154
  46.0 4.9 %all-to-all-start.2 = ((bf16[4,256,256]{2,1,0:T(8,128)(2,1)}), bf16[4,256,256]{2,1,0:T(8,128)(2,1)}, u32[]{:S(2)}, u32[]{:S(2)}) async-start(bf16[4,256,256]{2,1,0:T(8,128)(2,1)} %add.1.refs_4_), calls=%async_computation.2 | async-start | bytes 1048576 | tf_op jit(solution)/shard_map/all_to_all | solution.py:424
  50.9 4.0 %mix.1.refs_0_ = bf16[256,1024]{1,0:T(8,128)(2,1)S(1)} custom-call(bf16[4,272,256]{2,1,0:T(8,128)(2,1)S(1)} %all-to-all-done.refs_0_, bf16[4,2,256,256]{3,2,1,0:T(8,128)(2,1)S(1)} %weights.1.refs_4_.refs_3_.refs_1_, bf16[4,256,256]{2,1,0:T(8,128)(2,1)} %get-tuple-element.30.refs_2_, bf16[4,256,256]{2,1,0:T(8,128)(2,1)} %collective-permute-done.9.refs_3_, ...), custom_call_target="tpu_custom_call" | custom-call | tf_op jit(solution)/shard_map/mix/pallas_call | solution.py:154
  54.9 1.8 %wgrad.1 = (f32[128,1024]{1,0:T(8,128)S(1)}, bf16[128,1024]{1,0:T(8,128)(2,1)S(1)}) custom-call(bf16[256,1024]{1,0:T(8,128)(2,1)S(1)} %mix.1.refs_0_, bf16[256,1024]{1,0:T(8,128)(2,1)S(1)} %copy-done.1, bf16[256,1024]{1,0:T(8,128)(2,1)S(1)} %collective-permute-done.3.refs_0_.refs_5_.refs_2_, ...), custom_call_target="tpu_custom_call" | custom-call | tf_op jit(solution)/shard_map/wgrad/pallas_call | solution.py:154
  56.7 0.1 collective-permute-start.10
  56.8 1.5 %collective-permute-done.10.refs_1_ = bf16[128,1024]{1,0:T(8,128)(2,1)S(1)} collective-permute-done((bf16[128,1024]{1,0:T(8,128)(2,1)S(1)}, bf16[128,1024]{1,0:T(8,128)(2,1)S(1)}, u32[]{:S(2)}, u32[]{:S(2)}) %collective-permute-start.10) | collective-permute-done | bytes 262176 | tf_op jit(solution)/shard_map/ppermute | solution.py:420
  58.3 1.0 %collective-permute-start.11 = (bf16[32,1024]{1,0:T(8,128)(2,1)S(1)}, bf16[32,1024]{1,0:T(8,128)(2,1)S(1)}, u32[]{:S(2)}, u32[]{:S(2)}) collective-permute-start(bf16[32,1024]{1,0:T(8,128)(2,1)S(1)} %get-tuple-element.34), channel_id=1, source_target_pairs={{0,8},{8,0},{16,24},{24,16},{1,9},{9,1},{17,25},{25,17},{2,10},{10... | collective-permute-start | bytes 196616 | tf_op jit(solution)/shard_map/ppermute | solution.py:414
  59.3 0.4 collective-permute-start.12
  59.7 2.2 %collective-permute-start.13 = (bf16[32,1024]{1,0:T(8,128)(2,1)S(1)}, bf16[32,1024]{1,0:T(8,128)(2,1)S(1)}, u32[]{:S(2)}, u32[]{:S(2)}) collective-permute-start(bf16[32,1024]{1,0:T(8,128)(2,1)S(1)} %get-tuple-element.36), channel_id=1, source_target_pairs={{0,24},{8,16},{16,8},{24,0},{1,25},{9,17},{17,9},{25,1},{2,26},{10... | collective-permute-start | bytes 196616 | tf_op jit(solution)/shard_map/ppermute | solution.py:414
  61.9 0.8 collective-permute-done.11.refs_1_
  62.7 1.8 %collective-permute-done.12.refs_2_ = bf16[32,1024]{1,0:T(8,128)(2,1)S(1)} collective-permute-done((bf16[32,1024]{1,0:T(8,128)(2,1)S(1)}, bf16[32,1024]{1,0:T(8,128)(2,1)S(1)}, u32[]{:S(2)}, u32[]{:S(2)}) %collective-permute-start.12) | collective-permute-done | bytes 65568 | tf_op jit(solution)/shard_map/ppermute | solution.py:414
  64.5 0.4 collective-permute-done.13.refs_3_
  64.9 2.1 %collective-permute-start.17 = (bf16[32,1024]{1,0:T(8,128)(2,1)S(1)}, bf16[32,1024]{1,0:T(8,128)(2,1)S(1)}, u32[]{:S(2)}, u32[]{:S(2)}) collective-permute-start(bf16[32,1024]{1,0:T(8,128)(2,1)S(1)} %get-tuple-element.40), channel_id=1, source_target_pairs={{0,2},{1,3},{2,0},{3,1},{4,6},{5,7},{6,4},{7,5},{8,10},{9,11},{10,... | collective-permute-start | bytes 196616 | tf_op jit(solution)/shard_map/ppermute | solution.py:417
  67.0 1.1 %sum_rows.1.refs_2_ = bf16[256,256]{1,0:T(8,128)(2,1)S(1)} custom-call(bf16[4,256,256]{2,1,0:T(8,128)(2,1)} %all-to-all-done.2.refs_0_, bf16[32,1024]{1,0:T(8,128)(2,1)S(1)} %get-tuple-element.37.refs_1_.refs_0_), custom_call_target="tpu_custom_call" | custom-call | tf_op jit(solution)/shard_map/sum_rows/pallas_call | solution.py:154
  68.1 1.7 %collective-permute-start.14 = (bf16[256,256]{1,0:T(8,128)(2,1)S(1)}, bf16[256,256]{1,0:T(8,128)(2,1)S(1)}, u32[]{:S(2)}, u32[]{:S(2)}) collective-permute-start(bf16[256,256]{1,0:T(8,128)(2,1)S(1)} %sum_rows.1.refs_2_), channel_id=1, source_target_pairs={{0,8},{8,0},{16,24},{24,16},{1,9},{9,1},{17,25},{25,17},{2,10},{10... | collective-permute-start | bytes 393224 | tf_op jit(solution)/shard_map/ppermute | solution.py:414
  69.8 2.4 %collective-permute-start.18 = (bf16[32,1024]{1,0:T(8,128)(2,1)S(1)}, bf16[32,1024]{1,0:T(8,128)(2,1)S(1)}, u32[]{:S(2)}, u32[]{:S(2)}) collective-permute-start(bf16[32,1024]{1,0:T(8,128)(2,1)S(1)} %get-tuple-element.41), channel_id=1, source_target_pairs={{0,4},{1,5},{2,6},{3,7},{4,0},{5,1},{6,2},{7,3},{8,12},{9,13},{10,... | collective-permute-start | bytes 196616 | tf_op jit(solution)/shard_map/ppermute | solution.py:417
  72.2 1.1 %collective-permute-start.15 = (bf16[256,256]{1,0:T(8,128)(2,1)S(1)}, bf16[256,256]{1,0:T(8,128)(2,1)S(1)}, u32[]{:S(2)}, u32[]{:S(2)}) collective-permute-start(bf16[256,256]{1,0:T(8,128)(2,1)S(1)} %sum_rows.1.refs_2_), channel_id=1, source_target_pairs={{0,16},{8,24},{16,0},{24,8},{1,17},{9,25},{17,1},{25,9},{2,18},{10... | collective-permute-start | bytes 393224 | tf_op jit(solution)/shard_map/ppermute | solution.py:414
  73.3 0.8 collective-permute-start.16
  74.1 1.8 %collective-permute-done.18.refs_2_ = bf16[32,1024]{1,0:T(8,128)(2,1)S(1)} collective-permute-done((bf16[32,1024]{1,0:T(8,128)(2,1)S(1)}, bf16[32,1024]{1,0:T(8,128)(2,1)S(1)}, u32[]{:S(2)}, u32[]{:S(2)}) %collective-permute-start.18) | collective-permute-done | bytes 65568 | tf_op jit(solution)/shard_map/ppermute | solution.py:417
  75.8 4.3 %collective-permute-done.19.refs_3_ = bf16[32,1024]{1,0:T(8,128)(2,1)S(1)} collective-permute-done((bf16[32,1024]{1,0:T(8,128)(2,1)S(1)}, bf16[32,1024]{1,0:T(8,128)(2,1)S(1)}, u32[]{:S(2)}, u32[]{:S(2)}) %collective-permute-start.19) | collective-permute-done | bytes 65568 | tf_op jit(solution)/shard_map/ppermute | solution.py:417
  80.2 1.7 %collective-permute-start.20 = (bf16[32,1024]{1,0:T(8,128)(2,1)S(1)}, bf16[32,1024]{1,0:T(8,128)(2,1)S(1)}, u32[]{:S(2)}, u32[]{:S(2)}) collective-permute-start(bf16[32,1024]{1,0:T(8,128)(2,1)S(1)} %sum_parts.1.refs_0_), channel_id=1, source_target_pairs={{0,8},{8,0},{16,24},{24,16},{1,9},{9,1},{17,25},{25,17},{2,10},{10... | collective-permute-start | bytes 196616 | tf_op jit(solution)/shard_map/ppermute | solution.py:414
  81.9 1.1 %collective-permute-start.21 = (bf16[32,1024]{1,0:T(8,128)(2,1)S(1)}, bf16[32,1024]{1,0:T(8,128)(2,1)S(1)}, u32[]{:S(2)}, u32[]{:S(2)}) collective-permute-start(bf16[32,1024]{1,0:T(8,128)(2,1)S(1)} %sum_parts.1.refs_0_), channel_id=1, source_target_pairs={{0,16},{8,24},{16,0},{24,8},{1,17},{9,25},{17,1},{25,9},{2,18},{10... | collective-permute-start | bytes 196616 | tf_op jit(solution)/shard_map/ppermute | solution.py:414
  83.0 0.8 collective-permute-start.22
  83.7 1.3 %update.1 = (f32[256,1024]{1,0:T(8,128)}, f32[1,256]{1,0:T(1,128)}) custom-call(f32[256,1024]{1,0:T(8,128)S(1)} %copy-done, f32[1,256]{1,0:T(1,128)S(1)} %bitcast.7, bf16[256,256]{1,0:T(8,128)(2,1)S(1)} %sum_rows.1.refs_2_, bf16[256,256]{1,0:T(8,128)(2,1)S(1)} %collective-permute-done.14.refs_3_.refs_4_, ...), custom_call_target="tpu_custom_call" | custom-call | tf_op jit(solution)/shard_map/update/pallas_call | solution.py:154
  85.0 1.1 %collective-permute-done.21.refs_2_ = bf16[32,1024]{1,0:T(8,128)(2,1)S(1)} collective-permute-done((bf16[32,1024]{1,0:T(8,128)(2,1)S(1)}, bf16[32,1024]{1,0:T(8,128)(2,1)S(1)}, u32[]{:S(2)}, u32[]{:S(2)}) %collective-permute-start.21) | collective-permute-done | bytes 65568 | tf_op jit(solution)/shard_map/ppermute | solution.py:414
  86.1 2.0 %collective-permute-done.22.refs_3_ = bf16[32,1024]{1,0:T(8,128)(2,1)S(1)} collective-permute-done((bf16[32,1024]{1,0:T(8,128)(2,1)S(1)}, bf16[32,1024]{1,0:T(8,128)(2,1)S(1)}, u32[]{:S(2)}, u32[]{:S(2)}) %collective-permute-start.22) | collective-permute-done | bytes 65568 | tf_op jit(solution)/shard_map/ppermute | solution.py:414
  88.1 0.7 place.1
  (30 shorter events, 0.3 us)
Async XLA Ops:
  0.6 15.3 %collective-permute-start.3 = (bf16[256,1024]{1,0:T(8,128)(2,1)}, bf16[256,1024]{1,0:T(8,128)(2,1)S(1)}, u32[]{:S(2)}, u32[]{:S(2)}) collective-permute-start(bf16[256,1024]{1,0:T(8,128)(2,1)} %refs_1_.1), channel_id=1, source_target_pairs={{0,8},{8,0},{16,24},{24,16},{1,9},{9,1},{17,25},{25,17},{2,10},{10... | collective-permute-start | bytes 1572872 | tf_op jit(solution)/shard_map/ppermute | solution.py:414
  3.6 15.4 %collective-permute-start.4 = (bf16[256,1024]{1,0:T(8,128)(2,1)}, bf16[256,1024]{1,0:T(8,128)(2,1)S(1)}, u32[]{:S(2)}, u32[]{:S(2)}) collective-permute-start(bf16[256,1024]{1,0:T(8,128)(2,1)} %refs_1_.1), channel_id=1, source_target_pairs={{0,16},{8,24},{16,0},{24,8},{1,17},{9,25},{17,1},{25,9},{2,18},{10... | collective-permute-start | bytes 1572872 | tf_op jit(solution)/shard_map/ppermute | solution.py:414
  8.0 18.5 %collective-permute-start = (bf16[384,256]{1,0:T(8,128)(2,1)}, bf16[384,256]{1,0:T(8,128)(2,1)S(1)}, u32[]{:S(2)}, u32[]{:S(2)}) collective-permute-start(bf16[384,256]{1,0:T(8,128)(2,1)} %get-tuple-element.24.refs_0_), channel_id=1, source_target_pairs={{0,2},{1,3},{2,0},{3,1},{4,6},{5,7},{6,4},{7,5},{8,10},{9,11},{10,... | collective-permute-start | bytes 589832 | tf_op jit(solution)/shard_map/ppermute | solution.py:417
  9.6 17.6 %collective-permute-start.1 = (bf16[384,256]{1,0:T(8,128)(2,1)}, bf16[384,256]{1,0:T(8,128)(2,1)}, u32[]{:S(2)}, u32[]{:S(2)}) collective-permute-start(bf16[384,256]{1,0:T(8,128)(2,1)} %get-tuple-element.24.refs_0_), channel_id=1, source_target_pairs={{0,4},{1,5},{2,6},{3,7},{4,0},{5,1},{6,2},{7,3},{8,12},{9,13},{10,... | collective-permute-start | bytes 589832 | tf_op jit(solution)/shard_map/ppermute | solution.py:417
  12.2 15.0 %collective-permute-start.2 = (bf16[384,256]{1,0:T(8,128)(2,1)}, bf16[384,256]{1,0:T(8,128)(2,1)}, u32[]{:S(2)}, u32[]{:S(2)}) collective-permute-start(bf16[384,256]{1,0:T(8,128)(2,1)} %get-tuple-element.24.refs_0_), channel_id=1, source_target_pairs={{0,6},{1,7},{2,4},{3,5},{4,2},{5,3},{6,0},{7,1},{8,14},{9,15},{10,... | collective-permute-start | bytes 589832 | tf_op jit(solution)/shard_map/ppermute | solution.py:417
  12.4 13.2 %all-to-all-start = ((bf16[4,272,256]{2,1,0:T(8,128)(2,1)}), bf16[4,272,256]{2,1,0:T(8,128)(2,1)S(1)}, u32[]{:S(2)}, u32[]{:S(2)}) async-start(bf16[4,272,256]{2,1,0:T(8,128)(2,1)} %get-tuple-element.23), calls=%async_computation | async-start | bytes 1114112 | tf_op jit(solution)/shard_map/all_to_all | solution.py:427
  19.9 18.4 %collective-permute-start.6 = (bf16[128,1024]{1,0:T(8,128)(2,1)}, bf16[128,1024]{1,0:T(8,128)(2,1)S(1)}, u32[]{:S(2)}, u32[]{:S(2)}) collective-permute-start(bf16[128,1024]{1,0:T(8,128)(2,1)} %get-tuple-element.25.refs_1_), channel_id=1, source_target_pairs={{0,8},{8,0},{16,24},{24,16},{1,9},{9,1},{17,25},{25,17},{2,10},{10... | collective-permute-start | bytes 786440 | tf_op jit(solution)/shard_map/ppermute | solution.py:414
  19.9 7.3 %copy-start.2 = (bf16[384,256]{1,0:T(8,128)(2,1)S(1)}, bf16[384,256]{1,0:T(8,128)(2,1)}, u32[]{:S(2)}) copy-start(bf16[384,256]{1,0:T(8,128)(2,1)} %get-tuple-element.24.refs_0_) | copy-start | bytes 589828
  19.9 18.3 %collective-permute-start.7 = (bf16[128,1024]{1,0:T(8,128)(2,1)}, bf16[128,1024]{1,0:T(8,128)(2,1)}, u32[]{:S(2)}, u32[]{:S(2)}) collective-permute-start(bf16[128,1024]{1,0:T(8,128)(2,1)} %get-tuple-element.27), channel_id=1, source_target_pairs={{0,16},{8,24},{16,0},{24,8},{1,17},{9,25},{17,1},{25,9},{2,18},{10... | collective-permute-start | bytes 786440 | tf_op jit(solution)/shard_map/ppermute | solution.py:414
  26.5 0.7 copy-start.3
  27.2 0.9 %copy-start.4 = (bf16[384,256]{1,0:T(8,128)(2,1)S(1)}, bf16[384,256]{1,0:T(8,128)(2,1)}, u32[]{:S(2)}) copy-start(bf16[384,256]{1,0:T(8,128)(2,1)} %copy-done.3) | copy-start | bytes 589828
  38.3 1.5 %copy-start.1 = (bf16[256,1024]{1,0:T(8,128)(2,1)S(1)}, bf16[256,1024]{1,0:T(8,128)(2,1)}, u32[]{:S(2)}) copy-start(bf16[256,1024]{1,0:T(8,128)(2,1)} %refs_1_.1) | copy-start | bytes 1572868
  38.3 1.5 %collective-permute-start.5 = (bf16[128,1024]{1,0:T(8,128)(2,1)S(1)}, bf16[128,1024]{1,0:T(8,128)(2,1)S(1)}, u32[]{:S(2)}, u32[]{:S(2)}) collective-permute-start(bf16[128,1024]{1,0:T(8,128)(2,1)S(1)} %bitcast.5), channel_id=1, source_target_pairs={{0,1},{1,0},{2,3},{3,2},{4,5},{5,4},{6,7},{7,6},{8,9},{9,8},{10,11... | collective-permute-start | bytes 786440 | tf_op jit(solution)/shard_map/ppermute | solution.py:420
  43.1 2.0 %collective-permute-start.8 = (bf16[4,256,256]{2,1,0:T(8,128)(2,1)S(1)}, bf16[4,256,256]{2,1,0:T(8,128)(2,1)S(1)}, u32[]{:S(2)}, u32[]{:S(2)}) collective-permute-start(bf16[4,256,256]{2,1,0:T(8,128)(2,1)S(1)} %get-tuple-element.29), channel_id=1, source_target_pairs={{0,1},{1,0},{2,3},{3,2},{4,5},{5,4},{6,7},{7,6},{8,9},{9,8},{10,11... | collective-permute-start | bytes 1572872 | tf_op jit(solution)/shard_map/ppermute | solution.py:420
  43.3 7.5 %collective-permute-start.9 = (bf16[4,256,256]{2,1,0:T(8,128)(2,1)}, bf16[4,256,256]{2,1,0:T(8,128)(2,1)}, u32[]{:S(2)}, u32[]{:S(2)}) collective-permute-start(bf16[4,256,256]{2,1,0:T(8,128)(2,1)} %get-tuple-element.30.refs_2_), channel_id=1, source_target_pairs={{0,1},{1,0},{2,3},{3,2},{4,5},{5,4},{6,7},{7,6},{8,9},{9,8},{10,11... | collective-permute-start | bytes 1572872 | tf_op jit(solution)/shard_map/ppermute | solution.py:420
  46.0 21.0 %all-to-all-start.2 = ((bf16[4,256,256]{2,1,0:T(8,128)(2,1)}), bf16[4,256,256]{2,1,0:T(8,128)(2,1)}, u32[]{:S(2)}, u32[]{:S(2)}) async-start(bf16[4,256,256]{2,1,0:T(8,128)(2,1)} %add.1.refs_4_), calls=%async_computation.2 | async-start | bytes 1048576 | tf_op jit(solution)/shard_map/all_to_all | solution.py:424
  56.7 1.6 %collective-permute-start.10 = (bf16[128,1024]{1,0:T(8,128)(2,1)S(1)}, bf16[128,1024]{1,0:T(8,128)(2,1)S(1)}, u32[]{:S(2)}, u32[]{:S(2)}) collective-permute-start(bf16[128,1024]{1,0:T(8,128)(2,1)S(1)} %get-tuple-element.32), channel_id=1, source_target_pairs={{0,1},{1,0},{2,3},{3,2},{4,5},{5,4},{6,7},{7,6},{8,9},{9,8},{10,11... | collective-permute-start | bytes 786440 | tf_op jit(solution)/shard_map/ppermute | solution.py:420
  58.3 25.5 %copy-start = (f32[256,1024]{1,0:T(8,128)S(1)}, f32[256,1024]{1,0:T(8,128)}, u32[]{:S(2)}) copy-start(f32[256,1024]{1,0:T(8,128)} %refs_0_.3) | copy-start | bytes 3145732
  58.3 4.3 %collective-permute-start.11 = (bf16[32,1024]{1,0:T(8,128)(2,1)S(1)}, bf16[32,1024]{1,0:T(8,128)(2,1)S(1)}, u32[]{:S(2)}, u32[]{:S(2)}) collective-permute-start(bf16[32,1024]{1,0:T(8,128)(2,1)S(1)} %get-tuple-element.34), channel_id=1, source_target_pairs={{0,8},{8,0},{16,24},{24,16},{1,9},{9,1},{17,25},{25,17},{2,10},{10... | collective-permute-start | bytes 196616 | tf_op jit(solution)/shard_map/ppermute | solution.py:414
  59.3 5.2 %collective-permute-start.12 = (bf16[32,1024]{1,0:T(8,128)(2,1)S(1)}, bf16[32,1024]{1,0:T(8,128)(2,1)S(1)}, u32[]{:S(2)}, u32[]{:S(2)}) collective-permute-start(bf16[32,1024]{1,0:T(8,128)(2,1)S(1)} %get-tuple-element.35), channel_id=1, source_target_pairs={{0,16},{8,24},{16,0},{24,8},{1,17},{9,25},{17,1},{25,9},{2,18},{10... | collective-permute-start | bytes 196616 | tf_op jit(solution)/shard_map/ppermute | solution.py:414
  59.7 5.2 %collective-permute-start.13 = (bf16[32,1024]{1,0:T(8,128)(2,1)S(1)}, bf16[32,1024]{1,0:T(8,128)(2,1)S(1)}, u32[]{:S(2)}, u32[]{:S(2)}) collective-permute-start(bf16[32,1024]{1,0:T(8,128)(2,1)S(1)} %get-tuple-element.36), channel_id=1, source_target_pairs={{0,24},{8,16},{16,8},{24,0},{1,25},{9,17},{17,9},{25,1},{2,26},{10... | collective-permute-start | bytes 196616 | tf_op jit(solution)/shard_map/ppermute | solution.py:414
  64.9 9.1 %collective-permute-start.17 = (bf16[32,1024]{1,0:T(8,128)(2,1)S(1)}, bf16[32,1024]{1,0:T(8,128)(2,1)S(1)}, u32[]{:S(2)}, u32[]{:S(2)}) collective-permute-start(bf16[32,1024]{1,0:T(8,128)(2,1)S(1)} %get-tuple-element.40), channel_id=1, source_target_pairs={{0,2},{1,3},{2,0},{3,1},{4,6},{5,7},{6,4},{7,5},{8,10},{9,11},{10,... | collective-permute-start | bytes 196616 | tf_op jit(solution)/shard_map/ppermute | solution.py:417
  68.1 12.0 %collective-permute-start.14 = (bf16[256,256]{1,0:T(8,128)(2,1)S(1)}, bf16[256,256]{1,0:T(8,128)(2,1)S(1)}, u32[]{:S(2)}, u32[]{:S(2)}) collective-permute-start(bf16[256,256]{1,0:T(8,128)(2,1)S(1)} %sum_rows.1.refs_2_), channel_id=1, source_target_pairs={{0,8},{8,0},{16,24},{24,16},{1,9},{9,1},{17,25},{25,17},{2,10},{10... | collective-permute-start | bytes 393224 | tf_op jit(solution)/shard_map/ppermute | solution.py:414
  69.8 6.0 %collective-permute-start.18 = (bf16[32,1024]{1,0:T(8,128)(2,1)S(1)}, bf16[32,1024]{1,0:T(8,128)(2,1)S(1)}, u32[]{:S(2)}, u32[]{:S(2)}) collective-permute-start(bf16[32,1024]{1,0:T(8,128)(2,1)S(1)} %get-tuple-element.41), channel_id=1, source_target_pairs={{0,4},{1,5},{2,6},{3,7},{4,0},{5,1},{6,2},{7,3},{8,12},{9,13},{10,... | collective-permute-start | bytes 196616 | tf_op jit(solution)/shard_map/ppermute | solution.py:417
  72.2 11.5 %collective-permute-start.15 = (bf16[256,256]{1,0:T(8,128)(2,1)S(1)}, bf16[256,256]{1,0:T(8,128)(2,1)S(1)}, u32[]{:S(2)}, u32[]{:S(2)}) collective-permute-start(bf16[256,256]{1,0:T(8,128)(2,1)S(1)} %sum_rows.1.refs_2_), channel_id=1, source_target_pairs={{0,16},{8,24},{16,0},{24,8},{1,17},{9,25},{17,1},{25,9},{2,18},{10... | collective-permute-start | bytes 393224 | tf_op jit(solution)/shard_map/ppermute | solution.py:414
  73.3 10.4 %collective-permute-start.16 = (bf16[256,256]{1,0:T(8,128)(2,1)S(1)}, bf16[256,256]{1,0:T(8,128)(2,1)S(1)}, u32[]{:S(2)}, u32[]{:S(2)}) collective-permute-start(bf16[256,256]{1,0:T(8,128)(2,1)S(1)} %sum_rows.1.refs_2_), channel_id=1, source_target_pairs={{0,24},{8,16},{16,8},{24,0},{1,25},{9,17},{17,9},{25,1},{2,26},{10... | collective-permute-start | bytes 393224 | tf_op jit(solution)/shard_map/ppermute | solution.py:414
  74.0 6.1 %collective-permute-start.19 = (bf16[32,1024]{1,0:T(8,128)(2,1)S(1)}, bf16[32,1024]{1,0:T(8,128)(2,1)S(1)}, u32[]{:S(2)}, u32[]{:S(2)}) collective-permute-start(bf16[32,1024]{1,0:T(8,128)(2,1)S(1)} %get-tuple-element.42), channel_id=1, source_target_pairs={{0,6},{1,7},{2,4},{3,5},{4,2},{5,3},{6,0},{7,1},{8,14},{9,15},{10,... | collective-permute-start | bytes 196616 | tf_op jit(solution)/shard_map/ppermute | solution.py:417
  80.2 3.6 %copy-start.5 = (f32[256]{0:T(256)S(1)}, f32[256]{0:T(256)}, u32[]{:S(2)}) copy-start(f32[256]{0:T(256)} %param.10) | copy-start | bytes 3076
  80.2 4.9 %collective-permute-start.20 = (bf16[32,1024]{1,0:T(8,128)(2,1)S(1)}, bf16[32,1024]{1,0:T(8,128)(2,1)S(1)}, u32[]{:S(2)}, u32[]{:S(2)}) collective-permute-start(bf16[32,1024]{1,0:T(8,128)(2,1)S(1)} %sum_parts.1.refs_0_), channel_id=1, source_target_pairs={{0,8},{8,0},{16,24},{24,16},{1,9},{9,1},{17,25},{25,17},{2,10},{10... | collective-permute-start | bytes 196616 | tf_op jit(solution)/shard_map/ppermute | solution.py:414
  81.9 4.3 %collective-permute-start.21 = (bf16[32,1024]{1,0:T(8,128)(2,1)S(1)}, bf16[32,1024]{1,0:T(8,128)(2,1)S(1)}, u32[]{:S(2)}, u32[]{:S(2)}) collective-permute-start(bf16[32,1024]{1,0:T(8,128)(2,1)S(1)} %sum_parts.1.refs_0_), channel_id=1, source_target_pairs={{0,16},{8,24},{16,0},{24,8},{1,17},{9,25},{17,1},{25,9},{2,18},{10... | collective-permute-start | bytes 196616 | tf_op jit(solution)/shard_map/ppermute | solution.py:414
  83.0 5.2 %collective-permute-start.22 = (bf16[32,1024]{1,0:T(8,128)(2,1)S(1)}, bf16[32,1024]{1,0:T(8,128)(2,1)S(1)}, u32[]{:S(2)}, u32[]{:S(2)}) collective-permute-start(bf16[32,1024]{1,0:T(8,128)(2,1)S(1)} %sum_parts.1.refs_0_), channel_id=1, source_target_pairs={{0,24},{8,16},{16,8},{24,0},{1,25},{9,17},{17,9},{25,1},{2,26},{10... | collective-permute-start | bytes 196616 | tf_op jit(solution)/shard_map/ppermute | solution.py:414

commit v3 on v2

--- a/solution.py
+++ b/solution.py
@@ -231,15 +231,20 @@
         c.wait()
 
 
-def sort_kernel(me, *refs):
-    *blocks, out_t, out_w = refs
-    _, cols, rows = out_t.shape
-    part = out_w.shape[1]
+def stack_kernel(me, *refs):
+    *blocks, out = refs
+    cols = out.shape[1]
     for m, p in enumerate(blocks):
-        z = me[1] ^ m
-        out_t[z] = p[0:cols, :]
-        for i in range((p.shape[0] - cols) // part):
-            out_w[z, :, i * rows : (i + 1) * rows] = p[cols + i * part : cols + (i + 1) * part, :]
+        out[me[1] ^ m] = p[0:cols, :]
+
+
+def join_kernel(me, *refs):
+    *parts, out = refs
+    part = out.shape[0] // len(parts)
+    rows = parts[0].shape[1]
+    for m, p in enumerate(parts):
+        for i in range(p.shape[0] // part):
+            out[aligned(me[0] ^ m, part), i * rows : (i + 1) * rows] = p[i * part : (i + 1) * part, :]
 
 
 def gate_kernel(out):
@@ -249,8 +254,9 @@
 def choose_kernel(me, *refs):
     n = (len(refs) - 1) // 2
     parts, out, held = refs[:n], refs[n : 2 * n], refs[2 * n]
+    first = parts[0].shape[0] - held.shape[1]
     for m, p in enumerate(parts):
-        held[m] = p[...]
+        held[m] = p[first:, :]
     for m, o in enumerate(out):
         o[...] = held[me[1] ^ me[0] ^ m]
 
@@ -281,27 +287,24 @@
     return packs[r, rows - EXTRA : rows, :].astype(F32)
 
 
-def one_hot(ids, rows):
-    tok = ids.shape[1]
-    own = ids[0:1, :]
-    loc = ids[1:2, :]
-    at = iota((rows, tok), 0).astype(F32)
-    return jnp.broadcast_to(own, (rows, tok)), at == loc
+def one_hot(ids, shard, rows):
+    own, loc = ids[0:1, :], ids[1:2, :]
+    named = jnp.where(own == shard.astype(F32), loc, -1.0)
+    at = iota((rows, ids.shape[1]), 0).astype(F32)
+    return jnp.where(at == named, 1.0, 0.0).astype(BF16)
 
 
 def mix_kernel(me, packs, w, mine, other, out):
     n, cols, rows = mine.shape
     heads, tok = w.shape[1:3]
     dv = cols // heads
+    blocks = jnp.concatenate([x[z] for z in range(n) for x in (mine, other)], axis=1)
     for r in range(n):
-        own, hit = one_hot(ids_of(packs, me[0] ^ r), rows)
-        vals = jnp.zeros((cols, tok), F32)
-        for z in range(n):
-            for cc, blocks in enumerate((mine, other)):
-                shard = (2 * z + (me[2] ^ cc)).astype(F32)
-                pick = jnp.where(hit & (own == shard), 1.0, 0.0).astype(BF16)
-                vals = vals + nn(blocks[z], pick)
-        vals = vals.astype(BF16)
+        ids = ids_of(packs, me[0] ^ r)
+        picks = jnp.concatenate(
+            [one_hot(ids, 2 * z + (me[2] ^ cc), rows) for z in range(n) for cc in range(2)], axis=0
+        )
+        vals = nn(blocks, picks).astype(BF16)
         for j in range(heads):
             out[j * dv : (j + 1) * dv, r * tok : (r + 1) * tok] = nn(
                 vals[j * dv : (j + 1) * dv, :], w[r, j]
@@ -326,14 +329,10 @@
         for j in range(heads):
             at_j = slice(j * head_rows, (j + 1) * head_rows)
             grad[at_r, at_j] = nn(w[r, j], grad[at_r, at_j]).astype(BF16)
+    ids = jnp.concatenate([ids_of(packs, me[0] ^ r) for r in range(n)], axis=1)
     for cc in (1, 0):
         for z in range(n):
-            shard = (2 * z + (me[2] ^ cc)).astype(F32)
-            total = jnp.zeros((rows, heads * head_rows), F32)
-            for r in range(n):
-                own, hit = one_hot(ids_of(packs, me[0] ^ r), rows)
-                pick = jnp.where(hit & (own == shard), 1.0, 0.0).astype(BF16)
-                total = total + nn(pick, grad[r * tok : (r + 1) * tok, :])
+            total = nn(one_hot(ids, 2 * z + (me[2] ^ cc), rows), grad[...])
             if cc == 0:
                 keep[z] = total
             else:
@@ -470,45 +469,47 @@
         after=(far_x,),
         placed=True,
     )
-    mine, owp = call(
-        sort_kernel,
-        "sort",
-        [sds((n, cols, rows)), sds((n, part, width))],
+    owp = call(
+        choose_kernel,
+        "choose",
+        [sds((zrows - cols, rows))] * n,
         blocks,
         after=(w,),
-        placed=True,
+        scratch=[pltpu.VMEM((n, zrows - cols, rows), BF16)],
+        placed=True,
+    )
+    mine = call(
+        stack_kernel, "stack", sds((n, cols, rows)), blocks, after=(owp[0],), placed=True
     )
     other = core(mine)
-    ow_mine = swap_columns(owp).reshape(n * part, width)
+    owp = [column(p, m) for m, p in enumerate(owp)]
+    ow_mine = call(join_kernel, "join", sds((n * part, width)), owp, placed=True)
     ow_other = core(ow_mine)
     far_y, far_x = column(far_y, 2), column(far_x, 1)
     cots = [cotangent, x, y, far_x, far_y]
     here = call(gate_kernel, "gate", sds((8, 128), F32), (), after=(far_x, far_y), cost=GATE_COST)
 
+    mixed = call(
+        mix_kernel, "mix", sds((cols, n * tok)), (packs, w, mine, other), placed=True
+    )
     keep, send = call(
         back_kernel,
         "back",
         [sds((n, rows, cols), F32), sds((n, rows, cols))],
         (packs, ow_mine, ow_other, w, *cots),
-        after=(here,),
+        after=(here, mixed),
         scratch=[pltpu.VMEM((cols, width), BF16), pltpu.VMEM((n * tok, cols), BF16)],
         placed=True,
     )
     sums = call(add_kernel, "add", sds((n, rows, cols)), (keep, core(send)))
-    mixed = call(
-        mix_kernel,
-        "mix",
-        sds((cols, n * tok)),
-        (packs, w, mine, other),
-        after=(sums,),
-        placed=True,
-    )
+    ready = sums
     sums = swap_along(sums)
     wkeep, wsend = call(
         wgrad_kernel,
         "wgrad",
         [sds((n * part, width), F32), sds((n * part, width))],
         (mixed, *cots),
+        after=(ready,),
         placed=True,
     )
     wgot = core(wsend)

time: 89.3 us -> 80.4 us (0.900)
  blocking collectives: 8.25 us -> 0 us
  Pallas kernels: 19.6 us -> 13.6 us
  waiting for transfers between devices: 22.6 us -> 27.8 us
  starting transfers between devices: 36 us -> 38 us
  local copies, waits for them, and re-layouts: 1.61 us -> 0.03 us
    all_to_all x1 -> x0, blocking collectives: 8.25 us -> none  [swap_columns(): return lax.all_to_all(x, 'replica', 0, 0, tiled=True)]
    pallas_call x15 -> x17, Pallas kernels: 19.6 us -> 13.6 us  [call(): pl.pallas_call(run, out_shape=out, in_specs=[SMEM if i < smem else HBM if...]
    ppermute x13 -> x16, starting transfers between devices: 18 us -> 21.3 us  [column(): lax.ppermute(x, 'replica', [(i, i ^ m) for i in range(n)])]
    all_to_all x1, waiting for transfers between devices: 0.01 us -> 2.85 us  [swap_along(): lax.all_to_all(x, 'shard', 0, 0, tiled=True, axis_index_groups=groups)]
    all_to_all x1, waiting for transfers between devices: 2.94 us -> 4.83 us  [swap_columns(): return lax.all_to_all(x, 'replica', 0, 0, tiled=True)]
    ppermute x13 -> x16, waiting for transfers between devices: 9.19 us -> 10.8 us  [column(): lax.ppermute(x, 'replica', [(i, i ^ m) for i in range(n)])]
    unnamed x12, local copies, waits for them, and re-layouts: 1.61 us -> 0.03 us
    ppermute x4, waiting for transfers between devices: 4.43 us -> 3.06 us  [core(): return lax.ppermute(x, 'shard', [(i, i ^ 1) for i in range(shards)])]
  transfers between devices with their start and end apart: 25 -> 28, of which waited for: 12 -> 18; matrix products, arithmetic and copies ran while one was open for 0% -> 0% of each run, Pallas kernels for 18% -> 12%
where the time goes in v3:
time: 80.4 us; the launch traced here: 80.2 us
  starting transfers between devices  38 us (47%)
  waiting for transfers between devices  27.8 us (35%)
  Pallas kernels  13.6 us (17%)
  between operations  0.85 us (1%)
    ppermute x16, starting transfers between devices, column(): lax.ppermute(x, 'replica', [(i, i ^ m) for i in range(n)])  21.3 us
    pallas_call x17, Pallas kernels, call(): pl.pallas_call(run, out_shape=out, in_specs=[SMEM if i < smem else HBM if...  13.6 us
    ppermute x16, waiting for transfers between devices, column(): lax.ppermute(x, 'replica', [(i, i ^ m) for i in range(n)])  10.8 us
    ppermute x6, starting transfers between devices, along(): lax.ppermute(x, 'shard', [(i, i ^ 2 * m) for i in range(shards)])  8.01 us
    ppermute x6, waiting for transfers between devices, along(): lax.ppermute(x, 'shard', [(i, i ^ 2 * m) for i in range(shards)])  6.17 us
    all_to_all x1, waiting for transfers between devices, swap_columns(): return lax.all_to_all(x, 'replica', 0, 0, tiled=True)  4.83 us
    all_to_all x1, starting transfers between devices, swap_along(): lax.all_to_all(x, 'shard', 0, 0, tiled=True, axis_index_groups=groups)  4.51 us
    all_to_all x1, starting transfers between devices, swap_columns(): return lax.all_to_all(x, 'replica', 0, 0, tiled=True)  3.47 us
  transfers between devices with their start and end apart: 28, of which 18 were waited for; matrix products, arithmetic and copies ran while one was open for 0% of the time, Pallas kernels for 12%

profile of v3, /device:TPU:0, one launch (start us, length us, event | category | flops | bytes accessed | tf_op | source)
XLA Modules:
  0.0 80.2 jit_solution(16041554433302927094)
XLA Ops:
  0.6 3.0 %collective-permute-start.4 = (bf16[256,1024]{1,0:T(8,128)(2,1)}, bf16[256,1024]{1,0:T(8,128)(2,1)S(1)}, u32[]{:S(2)}, u32[]{:S(2)}) collective-permute-start(bf16[256,1024]{1,0:T(8,128)(2,1)} %refs_1_.1), channel_id=1, source_target_pairs={{0,16},{8,24},{16,0},{24,8},{1,17},{9,25},{17,1},{25,9},{2,18},{10... | collective-permute-start | bytes 1572872 | tf_op jit(solution)/shard_map/ppermute | solution.py:413
  3.7 1.5 %collective-permute-start.3 = (bf16[256,1024]{1,0:T(8,128)(2,1)}, bf16[256,1024]{1,0:T(8,128)(2,1)S(1)}, u32[]{:S(2)}, u32[]{:S(2)}) collective-permute-start(bf16[256,1024]{1,0:T(8,128)(2,1)} %refs_1_.1), channel_id=1, source_target_pairs={{0,8},{8,0},{16,24},{24,16},{1,9},{9,1},{17,25},{25,17},{2,10},{10... | collective-permute-start | bytes 1572872 | tf_op jit(solution)/shard_map/ppermute | solution.py:413
  5.2 2.8 %pack.1 = (bf16[4,272,256]{2,1,0:T(8,128)(2,1)}, bf16[384,256]{1,0:T(8,128)(2,1)}) custom-call(s32[1,4]{1,0:T(1,128)} %refs_0_.2, s32[1,256]{1,0:T(1,128)} %bitcast.5, s32[1,256]{1,0:T(1,128)} %bitcast.6, bf16[256,512]{1,0:T(8,128)(2,1)} %refs_3_.1, bf16[256,512]{1,0:T(8,128)(2,1)} %refs_4_.2, bf16[128,1024]{1,0:T(8,128)(2,1)} %refs_5_.1, f32[256,1024]{1,0:T(8,128)} %refs_0_.3), custom_call_target="tpu_custom_call" | custom-call | tf_op jit(solution)/shard_map/pack/pallas_call | solution.py:154
  8.0 3.7 %collective-permute-start.2 = (bf16[384,256]{1,0:T(8,128)(2,1)}, bf16[384,256]{1,0:T(8,128)(2,1)S(1)}, u32[]{:S(2)}, u32[]{:S(2)}) collective-permute-start(bf16[384,256]{1,0:T(8,128)(2,1)} %get-tuple-element.26.refs_0_), channel_id=1, source_target_pairs={{0,6},{1,7},{2,4},{3,5},{4,2},{5,3},{6,0},{7,1},{8,14},{9,15},{10,... | collective-permute-start | bytes 589832 | tf_op jit(solution)/shard_map/ppermute | solution.py:416
  11.6 0.8 collective-permute-start
  12.4 3.5 %all-to-all-start = ((bf16[4,272,256]{2,1,0:T(8,128)(2,1)}), bf16[4,272,256]{2,1,0:T(8,128)(2,1)S(1)}, u32[]{:S(2)}, u32[]{:S(2)}) async-start(bf16[4,272,256]{2,1,0:T(8,128)(2,1)} %get-tuple-element.25), calls=%async_computation | async-start | bytes 1114112 | tf_op jit(solution)/shard_map/all_to_all | solution.py:426
  15.9 1.6 %collective-permute-done.3.refs_0_.refs_5_.refs_2_ = bf16[256,1024]{1,0:T(8,128)(2,1)S(1)} collective-permute-done((bf16[256,1024]{1,0:T(8,128)(2,1)}, bf16[256,1024]{1,0:T(8,128)(2,1)S(1)}, u32[]{:S(2)}, u32[]{:S(2)}) %collective-permute-start.3) | collective-permute-done | bytes 524320 | tf_op jit(solution)/shard_map/ppermute | solution.py:413
  17.5 0.8 pass.1
  18.3 0.4 collective-permute-start.10
  18.7 2.1 %collective-permute-start.9 = (bf16[128,1024]{1,0:T(8,128)(2,1)S(1)}, bf16[128,1024]{1,0:T(8,128)(2,1)S(1)}, u32[]{:S(2)}, u32[]{:S(2)}) collective-permute-start(bf16[128,1024]{1,0:T(8,128)(2,1)S(1)} %get-tuple-element.27.refs_1_), channel_id=1, source_target_pairs={{0,8},{8,0},{16,24},{24,16},{1,9},{9,1},{17,25},{25,17},{2,10},{10... | collective-permute-start | bytes 786440 | tf_op jit(solution)/shard_map/ppermute | solution.py:413
  20.8 4.8 %all-to-all-done.refs_0_ = bf16[4,272,256]{2,1,0:T(8,128)(2,1)S(1)} async-done(((bf16[4,272,256]{2,1,0:T(8,128)(2,1)}), bf16[4,272,256]{2,1,0:T(8,128)(2,1)S(1)}, u32[]{:S(2)}, u32[]{:S(2)}) %all-to-all-start) | async-done | bytes 557088 | tf_op jit(solution)/shard_map/all_to_all | solution.py:426
  25.7 0.8 %weights.1.refs_4_.refs_1_.refs_3_ = bf16[4,2,256,256]{3,2,1,0:T(8,128)(2,1)S(1)} custom-call(bf16[4,272,256]{2,1,0:T(8,128)(2,1)S(1)} %all-to-all-done.refs_0_, bf16[128,1024]{1,0:T(8,128)(2,1)S(1)} %get-tuple-element.27.refs_1_), custom_call_target="tpu_custom_call" | custom-call | tf_op jit(solution)/shard_map/weights/pallas_call | solution.py:154
  26.5 1.5 %collective-permute-done.1.refs_2_ = bf16[384,256]{1,0:T(8,128)(2,1)S(1)} collective-permute-done((bf16[384,256]{1,0:T(8,128)(2,1)}, bf16[384,256]{1,0:T(8,128)(2,1)S(1)}, u32[]{:S(2)}, u32[]{:S(2)}) %collective-permute-start.1) | collective-permute-done | bytes 196640 | tf_op jit(solution)/shard_map/ppermute | solution.py:416
  28.0 0.6 collective-permute-start.5
  28.6 0.5 collective-permute-start.6
  29.1 2.4 %collective-permute-start.7 = (bf16[128,256]{1,0:T(8,128)(2,1)S(1)}, bf16[128,256]{1,0:T(8,128)(2,1)S(1)}, u32[]{:S(2)}, u32[]{:S(2)}) collective-permute-start(bf16[128,256]{1,0:T(8,128)(2,1)S(1)} %get-tuple-element.31), channel_id=1, source_target_pairs={{0,24},{8,16},{16,8},{24,0},{1,25},{9,17},{17,9},{25,1},{2,26},{10... | collective-permute-start | bytes 196616 | tf_op jit(solution)/shard_map/ppermute | solution.py:413
  31.6 1.0 %collective-permute-done.5.refs_1_ = bf16[128,256]{1,0:T(8,128)(2,1)S(1)} collective-permute-done((bf16[128,256]{1,0:T(8,128)(2,1)S(1)}, bf16[128,256]{1,0:T(8,128)(2,1)S(1)}, u32[]{:S(2)}, u32[]{:S(2)}) %collective-permute-start.5) | collective-permute-done | bytes 65568 | tf_op jit(solution)/shard_map/ppermute | solution.py:413
  32.9 1.4 %collective-permute-done.7.refs_3_ = bf16[128,256]{1,0:T(8,128)(2,1)S(1)} collective-permute-done((bf16[128,256]{1,0:T(8,128)(2,1)S(1)}, bf16[128,256]{1,0:T(8,128)(2,1)S(1)}, u32[]{:S(2)}, u32[]{:S(2)}) %collective-permute-start.7) | collective-permute-done | bytes 65568 | tf_op jit(solution)/shard_map/ppermute | solution.py:413
  34.5 2.8 %mix.1.refs_10_.refs_0_ = bf16[256,1024]{1,0:T(8,128)(2,1)S(1)} custom-call(bf16[4,272,256]{2,1,0:T(8,128)(2,1)S(1)} %all-to-all-done.refs_0_, bf16[4,2,256,256]{3,2,1,0:T(8,128)(2,1)S(1)} %weights.1.refs_4_.refs_1_.refs_3_, bf16[4,256,256]{2,1,0:T(8,128)(2,1)S(1)} %stack.1.refs_2_, bf16[4,256,256]{2,1,0:T(8,128)(2,1)S(1)} %collective-permute-done.11.refs_3_), custom_call_target="tpu_custom_call" | custom-call | tf_op jit(solution)/shard_map/mix/pallas_call | solution.py:154
  37.4 2.4 %back.1 = (f32[4,256,256]{2,1,0:T(8,128)S(1)}, bf16[4,256,256]{2,1,0:T(8,128)(2,1)S(1)}) custom-call(bf16[4,272,256]{2,1,0:T(8,128)(2,1)S(1)} %all-to-all-done.refs_0_, bf16[128,1024]{1,0:T(8,128)(2,1)S(1)} %join.1.refs_1_, bf16[128,1024]{1,0:T(8,128)(2,1)S(1)} %collective-permute-done.8.refs_2_, ...), custom_call_target="tpu_custom_call" | custom-call | tf_op jit(solution)/shard_map/back/pallas_call | solution.py:154
  39.7 0.5 collective-permute-start.12
  40.2 1.5 %collective-permute-done.12.refs_1_ = bf16[4,256,256]{2,1,0:T(8,128)(2,1)S(1)} collective-permute-done((bf16[4,256,256]{2,1,0:T(8,128)(2,1)S(1)}, bf16[4,256,256]{2,1,0:T(8,128)(2,1)S(1)}, u32[]{:S(2)}, u32[]{:S(2)}) %collective-permute-start.12) | collective-permute-done | bytes 524320 | tf_op jit(solution)/shard_map/ppermute | solution.py:419
  41.7 0.9 %add.1.refs_6_ = bf16[4,256,256]{2,1,0:T(8,128)(2,1)} custom-call(f32[4,256,256]{2,1,0:T(8,128)S(1)} %get-tuple-element.33.refs_0_, bf16[4,256,256]{2,1,0:T(8,128)(2,1)S(1)} %collective-permute-done.12.refs_1_), custom_call_target="tpu_custom_call" | custom-call | tf_op jit(solution)/shard_map/add/pallas_call | solution.py:154
  42.6 4.5 %all-to-all-start.1 = ((bf16[4,256,256]{2,1,0:T(8,128)(2,1)}), bf16[4,256,256]{2,1,0:T(8,128)(2,1)S(1)}, u32[]{:S(2)}, u32[]{:S(2)}) async-start(bf16[4,256,256]{2,1,0:T(8,128)(2,1)} %add.1.refs_6_), calls=%async_computation.1 | async-start | bytes 1048576 | tf_op jit(solution)/shard_map/all_to_all | solution.py:423
  47.1 0.8 %wgrad.1 = (f32[128,1024]{1,0:T(8,128)S(1)}, bf16[128,1024]{1,0:T(8,128)(2,1)S(1)}) custom-call(bf16[256,1024]{1,0:T(8,128)(2,1)S(1)} %mix.1.refs_10_.refs_0_, bf16[256,1024]{1,0:T(8,128)(2,1)S(1)} %copy-done.1, bf16[256,1024]{1,0:T(8,128)(2,1)S(1)} %collective-permute-done.3.refs_0_.refs_5_.refs_2_, ...), custom_call_target="tpu_custom_call" | custom-call | tf_op jit(solution)/shard_map/wgrad/pallas_call | solution.py:154
  48.1 1.5 %collective-permute-done.13.refs_1_ = bf16[128,1024]{1,0:T(8,128)(2,1)S(1)} collective-permute-done((bf16[128,1024]{1,0:T(8,128)(2,1)S(1)}, bf16[128,1024]{1,0:T(8,128)(2,1)S(1)}, u32[]{:S(2)}, u32[]{:S(2)}) %collective-permute-start.13) | collective-permute-done | bytes 262176 | tf_op jit(solution)/shard_map/ppermute | solution.py:419
  49.6 1.6 %collective-permute-start.14 = (bf16[32,1024]{1,0:T(8,128)(2,1)S(1)}, bf16[32,1024]{1,0:T(8,128)(2,1)S(1)}, u32[]{:S(2)}, u32[]{:S(2)}) collective-permute-start(bf16[32,1024]{1,0:T(8,128)(2,1)S(1)} %get-tuple-element.38), channel_id=1, source_target_pairs={{0,8},{8,0},{16,24},{24,16},{1,9},{9,1},{17,25},{25,17},{2,10},{10... | collective-permute-start | bytes 196616 | tf_op jit(solution)/shard_map/ppermute | solution.py:413
  51.3 0.8 %collective-permute-start.15 = (bf16[32,1024]{1,0:T(8,128)(2,1)S(1)}, bf16[32,1024]{1,0:T(8,128)(2,1)S(1)}, u32[]{:S(2)}, u32[]{:S(2)}) collective-permute-start(bf16[32,1024]{1,0:T(8,128)(2,1)S(1)} %get-tuple-element.39), channel_id=1, source_target_pairs={{0,16},{8,24},{16,0},{24,8},{1,17},{9,25},{17,1},{25,9},{2,18},{10... | collective-permute-start | bytes 196616 | tf_op jit(solution)/shard_map/ppermute | solution.py:413
  52.1 1.1 %collective-permute-start.16 = (bf16[32,1024]{1,0:T(8,128)(2,1)S(1)}, bf16[32,1024]{1,0:T(8,128)(2,1)S(1)}, u32[]{:S(2)}, u32[]{:S(2)}) collective-permute-start(bf16[32,1024]{1,0:T(8,128)(2,1)S(1)} %get-tuple-element.40), channel_id=1, source_target_pairs={{0,24},{8,16},{16,8},{24,0},{1,25},{9,17},{17,9},{25,1},{2,26},{10... | collective-permute-start | bytes 196616 | tf_op jit(solution)/shard_map/ppermute | solution.py:413
  53.2 0.8 collective-permute-done.14.refs_1_
  54.0 2.2 %collective-permute-done.15.refs_2_ = bf16[32,1024]{1,0:T(8,128)(2,1)S(1)} collective-permute-done((bf16[32,1024]{1,0:T(8,128)(2,1)S(1)}, bf16[32,1024]{1,0:T(8,128)(2,1)S(1)}, u32[]{:S(2)}, u32[]{:S(2)}) %collective-permute-start.15) | collective-permute-done | bytes 65568 | tf_op jit(solution)/shard_map/ppermute | solution.py:413
  56.2 1.0 %collective-permute-done.16.refs_3_ = bf16[32,1024]{1,0:T(8,128)(2,1)S(1)} collective-permute-done((bf16[32,1024]{1,0:T(8,128)(2,1)S(1)}, bf16[32,1024]{1,0:T(8,128)(2,1)S(1)}, u32[]{:S(2)}, u32[]{:S(2)}) %collective-permute-start.16) | collective-permute-done | bytes 65568 | tf_op jit(solution)/shard_map/ppermute | solution.py:413
  57.3 2.1 %collective-permute-start.20 = (bf16[32,1024]{1,0:T(8,128)(2,1)S(1)}, bf16[32,1024]{1,0:T(8,128)(2,1)S(1)}, u32[]{:S(2)}, u32[]{:S(2)}) collective-permute-start(bf16[32,1024]{1,0:T(8,128)(2,1)S(1)} %get-tuple-element.44), channel_id=1, source_target_pairs={{0,2},{1,3},{2,0},{3,1},{4,6},{5,7},{6,4},{7,5},{8,10},{9,11},{10,... | collective-permute-start | bytes 196616 | tf_op jit(solution)/shard_map/ppermute | solution.py:416
  59.4 2.9 %all-to-all-done.1.refs_0_ = bf16[4,256,256]{2,1,0:T(8,128)(2,1)S(1)} async-done(((bf16[4,256,256]{2,1,0:T(8,128)(2,1)}), bf16[4,256,256]{2,1,0:T(8,128)(2,1)S(1)}, u32[]{:S(2)}, u32[]{:S(2)}) %all-to-all-start.1) | async-done | bytes 524320 | tf_op jit(solution)/shard_map/all_to_all | solution.py:423
  62.3 1.6 %collective-permute-start.17 = (bf16[256,256]{1,0:T(8,128)(2,1)S(1)}, bf16[256,256]{1,0:T(8,128)(2,1)S(1)}, u32[]{:S(2)}, u32[]{:S(2)}) collective-permute-start(bf16[256,256]{1,0:T(8,128)(2,1)S(1)} %sum_rows.1.refs_2_), channel_id=1, source_target_pairs={{0,8},{8,0},{16,24},{24,16},{1,9},{9,1},{17,25},{25,17},{2,10},{10... | collective-permute-start | bytes 393224 | tf_op jit(solution)/shard_map/ppermute | solution.py:413
  63.9 1.5 %collective-permute-start.19 = (bf16[256,256]{1,0:T(8,128)(2,1)S(1)}, bf16[256,256]{1,0:T(8,128)(2,1)S(1)}, u32[]{:S(2)}, u32[]{:S(2)}) collective-permute-start(bf16[256,256]{1,0:T(8,128)(2,1)S(1)} %sum_rows.1.refs_2_), channel_id=1, source_target_pairs={{0,24},{8,16},{16,8},{24,0},{1,25},{9,17},{17,9},{25,1},{2,26},{10... | collective-permute-start | bytes 393224 | tf_op jit(solution)/shard_map/ppermute | solution.py:413
  65.4 0.5 collective-permute-start.18
  65.9 1.5 %collective-permute-start.22 = (bf16[32,1024]{1,0:T(8,128)(2,1)S(1)}, bf16[32,1024]{1,0:T(8,128)(2,1)S(1)}, u32[]{:S(2)}, u32[]{:S(2)}) collective-permute-start(bf16[32,1024]{1,0:T(8,128)(2,1)S(1)} %get-tuple-element.46), channel_id=1, source_target_pairs={{0,6},{1,7},{2,4},{3,5},{4,2},{5,3},{6,0},{7,1},{8,14},{9,15},{10,... | collective-permute-start | bytes 196616 | tf_op jit(solution)/shard_map/ppermute | solution.py:416
  67.3 2.7 %collective-permute-done.21.refs_2_ = bf16[32,1024]{1,0:T(8,128)(2,1)S(1)} collective-permute-done((bf16[32,1024]{1,0:T(8,128)(2,1)S(1)}, bf16[32,1024]{1,0:T(8,128)(2,1)S(1)}, u32[]{:S(2)}, u32[]{:S(2)}) %collective-permute-start.21) | collective-permute-done | bytes 65568 | tf_op jit(solution)/shard_map/ppermute | solution.py:416
  70.1 2.0 %collective-permute-done.22.refs_3_ = bf16[32,1024]{1,0:T(8,128)(2,1)S(1)} collective-permute-done((bf16[32,1024]{1,0:T(8,128)(2,1)S(1)}, bf16[32,1024]{1,0:T(8,128)(2,1)S(1)}, u32[]{:S(2)}, u32[]{:S(2)}) %collective-permute-start.22) | collective-permute-done | bytes 65568 | tf_op jit(solution)/shard_map/ppermute | solution.py:416
  72.1 1.9 %collective-permute-start.25 = (bf16[32,1024]{1,0:T(8,128)(2,1)S(1)}, bf16[32,1024]{1,0:T(8,128)(2,1)S(1)}, u32[]{:S(2)}, u32[]{:S(2)}) collective-permute-start(bf16[32,1024]{1,0:T(8,128)(2,1)S(1)} %sum_parts.1.refs_0_), channel_id=1, source_target_pairs={{0,24},{8,16},{16,8},{24,0},{1,25},{9,17},{17,9},{25,1},{2,26},{10... | collective-permute-start | bytes 196616 | tf_op jit(solution)/shard_map/ppermute | solution.py:413
  74.0 1.2 %collective-permute-start.24 = (bf16[32,1024]{1,0:T(8,128)(2,1)S(1)}, bf16[32,1024]{1,0:T(8,128)(2,1)S(1)}, u32[]{:S(2)}, u32[]{:S(2)}) collective-permute-start(bf16[32,1024]{1,0:T(8,128)(2,1)S(1)} %sum_parts.1.refs_0_), channel_id=1, source_target_pairs={{0,16},{8,24},{16,0},{24,8},{1,17},{9,25},{17,1},{25,9},{2,18},{10... | collective-permute-start | bytes 196616 | tf_op jit(solution)/shard_map/ppermute | solution.py:413
  75.2 0.5 collective-permute-start.23
  75.7 1.3 %update.1 = (f32[256,1024]{1,0:T(8,128)}, f32[1,256]{1,0:T(1,128)}) custom-call(f32[256,1024]{1,0:T(8,128)S(1)} %copy-done, f32[1,256]{1,0:T(1,128)S(1)} %bitcast.4, bf16[256,256]{1,0:T(8,128)(2,1)S(1)} %sum_rows.1.refs_2_, bf16[256,256]{1,0:T(8,128)(2,1)S(1)} %collective-permute-done.17.refs_3_.refs_4_, ...), custom_call_target="tpu_custom_call" | custom-call | tf_op jit(solution)/shard_map/update/pallas_call | solution.py:154
  77.0 0.4 collective-permute-done.25.refs_3_
  77.3 0.9 %collective-permute-done.24.refs_2_ = bf16[32,1024]{1,0:T(8,128)(2,1)S(1)} collective-permute-done((bf16[32,1024]{1,0:T(8,128)(2,1)S(1)}, bf16[32,1024]{1,0:T(8,128)(2,1)S(1)}, u32[]{:S(2)}, u32[]{:S(2)}) %collective-permute-start.24) | collective-permute-done | bytes 65568 | tf_op jit(solution)/shard_map/ppermute | solution.py:413
  78.3 1.2 %collective-permute-done.23.refs_1_ = bf16[32,1024]{1,0:T(8,128)(2,1)S(1)} collective-permute-done((bf16[32,1024]{1,0:T(8,128)(2,1)S(1)}, bf16[32,1024]{1,0:T(8,128)(2,1)S(1)}, u32[]{:S(2)}, u32[]{:S(2)}) %collective-permute-start.23) | collective-permute-done | bytes 65568 | tf_op jit(solution)/shard_map/ppermute | solution.py:413
  79.4 0.7 place.1
  (37 shorter events, 0.9 us)
Async XLA Ops:
  0.6 15.3 %collective-permute-start.4 = (bf16[256,1024]{1,0:T(8,128)(2,1)}, bf16[256,1024]{1,0:T(8,128)(2,1)S(1)}, u32[]{:S(2)}, u32[]{:S(2)}) collective-permute-start(bf16[256,1024]{1,0:T(8,128)(2,1)} %refs_1_.1), channel_id=1, source_target_pairs={{0,16},{8,24},{16,0},{24,8},{1,17},{9,25},{17,1},{25,9},{2,18},{10... | collective-permute-start | bytes 1572872 | tf_op jit(solution)/shard_map/ppermute | solution.py:413
  3.7 13.9 %collective-permute-start.3 = (bf16[256,1024]{1,0:T(8,128)(2,1)}, bf16[256,1024]{1,0:T(8,128)(2,1)S(1)}, u32[]{:S(2)}, u32[]{:S(2)}) collective-permute-start(bf16[256,1024]{1,0:T(8,128)(2,1)} %refs_1_.1), channel_id=1, source_target_pairs={{0,8},{8,0},{16,24},{24,16},{1,9},{9,1},{17,25},{25,17},{2,10},{10... | collective-permute-start | bytes 1572872 | tf_op jit(solution)/shard_map/ppermute | solution.py:413
  8.0 18.5 %collective-permute-start.2 = (bf16[384,256]{1,0:T(8,128)(2,1)}, bf16[384,256]{1,0:T(8,128)(2,1)S(1)}, u32[]{:S(2)}, u32[]{:S(2)}) collective-permute-start(bf16[384,256]{1,0:T(8,128)(2,1)} %get-tuple-element.26.refs_0_), channel_id=1, source_target_pairs={{0,6},{1,7},{2,4},{3,5},{4,2},{5,3},{6,0},{7,1},{8,14},{9,15},{10,... | collective-permute-start | bytes 589832 | tf_op jit(solution)/shard_map/ppermute | solution.py:416
  11.6 16.3 %collective-permute-start.1 = (bf16[384,256]{1,0:T(8,128)(2,1)}, bf16[384,256]{1,0:T(8,128)(2,1)S(1)}, u32[]{:S(2)}, u32[]{:S(2)}) collective-permute-start(bf16[384,256]{1,0:T(8,128)(2,1)} %get-tuple-element.26.refs_0_), channel_id=1, source_target_pairs={{0,4},{1,5},{2,6},{3,7},{4,0},{5,1},{6,2},{7,3},{8,12},{9,13},{10,... | collective-permute-start | bytes 589832 | tf_op jit(solution)/shard_map/ppermute | solution.py:416
  11.6 16.3 %collective-permute-start = (bf16[384,256]{1,0:T(8,128)(2,1)}, bf16[384,256]{1,0:T(8,128)(2,1)S(1)}, u32[]{:S(2)}, u32[]{:S(2)}) collective-permute-start(bf16[384,256]{1,0:T(8,128)(2,1)} %get-tuple-element.26.refs_0_), channel_id=1, source_target_pairs={{0,2},{1,3},{2,0},{3,1},{4,6},{5,7},{6,4},{7,5},{8,10},{9,11},{10,... | collective-permute-start | bytes 589832 | tf_op jit(solution)/shard_map/ppermute | solution.py:416
  12.4 13.2 %all-to-all-start = ((bf16[4,272,256]{2,1,0:T(8,128)(2,1)}), bf16[4,272,256]{2,1,0:T(8,128)(2,1)S(1)}, u32[]{:S(2)}, u32[]{:S(2)}) async-start(bf16[4,272,256]{2,1,0:T(8,128)(2,1)} %get-tuple-element.25), calls=%async_computation | async-start | bytes 1114112 | tf_op jit(solution)/shard_map/all_to_all | solution.py:426
  18.3 16.1 %collective-permute-start.10 = (bf16[128,1024]{1,0:T(8,128)(2,1)}, bf16[128,1024]{1,0:T(8,128)(2,1)S(1)}, u32[]{:S(2)}, u32[]{:S(2)}) collective-permute-start(bf16[128,1024]{1,0:T(8,128)(2,1)} %get-tuple-element.32), channel_id=1, source_target_pairs={{0,16},{8,24},{16,0},{24,8},{1,17},{9,25},{17,1},{25,9},{2,18},{10... | collective-permute-start | bytes 786440 | tf_op jit(solution)/shard_map/ppermute | solution.py:413
  18.7 9.3 %copy-start.4 = (bf16[384,256]{1,0:T(8,128)(2,1)S(1)}, bf16[384,256]{1,0:T(8,128)(2,1)}, u32[]{:S(2)}) copy-start(bf16[384,256]{1,0:T(8,128)(2,1)} %get-tuple-element.26.refs_0_) | copy-start | bytes 589828
  18.7 15.7 %collective-permute-start.9 = (bf16[128,1024]{1,0:T(8,128)(2,1)S(1)}, bf16[128,1024]{1,0:T(8,128)(2,1)S(1)}, u32[]{:S(2)}, u32[]{:S(2)}) collective-permute-start(bf16[128,1024]{1,0:T(8,128)(2,1)S(1)} %get-tuple-element.27.refs_1_), channel_id=1, source_target_pairs={{0,8},{8,0},{16,24},{24,16},{1,9},{9,1},{17,25},{25,17},{2,10},{10... | collective-permute-start | bytes 786440 | tf_op jit(solution)/shard_map/ppermute | solution.py:413
  28.0 4.6 %collective-permute-start.5 = (bf16[128,256]{1,0:T(8,128)(2,1)S(1)}, bf16[128,256]{1,0:T(8,128)(2,1)S(1)}, u32[]{:S(2)}, u32[]{:S(2)}) collective-permute-start(bf16[128,256]{1,0:T(8,128)(2,1)S(1)} %get-tuple-element.29), channel_id=1, source_target_pairs={{0,8},{8,0},{16,24},{24,16},{1,9},{9,1},{17,25},{25,17},{2,10},{10... | collective-permute-start | bytes 196616 | tf_op jit(solution)/shard_map/ppermute | solution.py:413
  28.6 4.3 %collective-permute-start.6 = (bf16[128,256]{1,0:T(8,128)(2,1)S(1)}, bf16[128,256]{1,0:T(8,128)(2,1)S(1)}, u32[]{:S(2)}, u32[]{:S(2)}) collective-permute-start(bf16[128,256]{1,0:T(8,128)(2,1)S(1)} %get-tuple-element.30), channel_id=1, source_target_pairs={{0,16},{8,24},{16,0},{24,8},{1,17},{9,25},{17,1},{25,9},{2,18},{10... | collective-permute-start | bytes 196616 | tf_op jit(solution)/shard_map/ppermute | solution.py:413
  29.1 5.2 %collective-permute-start.7 = (bf16[128,256]{1,0:T(8,128)(2,1)S(1)}, bf16[128,256]{1,0:T(8,128)(2,1)S(1)}, u32[]{:S(2)}, u32[]{:S(2)}) collective-permute-start(bf16[128,256]{1,0:T(8,128)(2,1)S(1)} %get-tuple-element.31), channel_id=1, source_target_pairs={{0,24},{8,16},{16,8},{24,0},{1,25},{9,17},{17,9},{25,1},{2,26},{10... | collective-permute-start | bytes 196616 | tf_op jit(solution)/shard_map/ppermute | solution.py:413
  32.6 1.9 %collective-permute-start.11 = (bf16[4,256,256]{2,1,0:T(8,128)(2,1)S(1)}, bf16[4,256,256]{2,1,0:T(8,128)(2,1)S(1)}, u32[]{:S(2)}, u32[]{:S(2)}) collective-permute-start(bf16[4,256,256]{2,1,0:T(8,128)(2,1)S(1)} %stack.1.refs_2_), channel_id=1, source_target_pairs={{0,1},{1,0},{2,3},{3,2},{4,5},{5,4},{6,7},{7,6},{8,9},{9,8},{10,11... | collective-permute-start | bytes 1572872 | tf_op jit(solution)/shard_map/ppermute | solution.py:419
  34.3 3.0 %collective-permute-start.8 = (bf16[128,1024]{1,0:T(8,128)(2,1)S(1)}, bf16[128,1024]{1,0:T(8,128)(2,1)S(1)}, u32[]{:S(2)}, u32[]{:S(2)}) collective-permute-start(bf16[128,1024]{1,0:T(8,128)(2,1)S(1)} %join.1.refs_1_), channel_id=1, source_target_pairs={{0,1},{1,0},{2,3},{3,2},{4,5},{5,4},{6,7},{7,6},{8,9},{9,8},{10,11... | collective-permute-start | bytes 786440 | tf_op jit(solution)/shard_map/ppermute | solution.py:419
  34.4 2.9 %copy-start.2 = (bf16[128,1024]{1,0:T(8,128)(2,1)}, bf16[128,1024]{1,0:T(8,128)(2,1)S(1)}, u32[]{:S(2)}) copy-start(bf16[128,1024]{1,0:T(8,128)(2,1)S(1)} %collective-permute-done.9.refs_0_.refs_7_.refs_4_) | copy-start | bytes 786436
  34.4 2.9 %copy-start.1 = (bf16[256,1024]{1,0:T(8,128)(2,1)S(1)}, bf16[256,1024]{1,0:T(8,128)(2,1)}, u32[]{:S(2)}) copy-start(bf16[256,1024]{1,0:T(8,128)(2,1)} %refs_1_.1) | copy-start | bytes 1572868
  39.7 2.0 %collective-permute-start.12 = (bf16[4,256,256]{2,1,0:T(8,128)(2,1)S(1)}, bf16[4,256,256]{2,1,0:T(8,128)(2,1)S(1)}, u32[]{:S(2)}, u32[]{:S(2)}) collective-permute-start(bf16[4,256,256]{2,1,0:T(8,128)(2,1)S(1)} %get-tuple-element.34), channel_id=1, source_target_pairs={{0,1},{1,0},{2,3},{3,2},{4,5},{5,4},{6,7},{7,6},{8,9},{9,8},{10,11... | collective-permute-start | bytes 1572872 | tf_op jit(solution)/shard_map/ppermute | solution.py:419
  42.6 4.5 %copy-start.3 = (bf16[128,1024]{1,0:T(8,128)(2,1)S(1)}, bf16[128,1024]{1,0:T(8,128)(2,1)}, u32[]{:S(2)}) copy-start(bf16[128,1024]{1,0:T(8,128)(2,1)} %copy-done.2) | copy-start | bytes 786436
  42.6 19.6 %all-to-all-start.1 = ((bf16[4,256,256]{2,1,0:T(8,128)(2,1)}), bf16[4,256,256]{2,1,0:T(8,128)(2,1)S(1)}, u32[]{:S(2)}, u32[]{:S(2)}) async-start(bf16[4,256,256]{2,1,0:T(8,128)(2,1)} %add.1.refs_6_), calls=%async_computation.1 | async-start | bytes 1048576 | tf_op jit(solution)/shard_map/all_to_all | solution.py:423
  48.0 1.6 %collective-permute-start.13 = (bf16[128,1024]{1,0:T(8,128)(2,1)S(1)}, bf16[128,1024]{1,0:T(8,128)(2,1)S(1)}, u32[]{:S(2)}, u32[]{:S(2)}) collective-permute-start(bf16[128,1024]{1,0:T(8,128)(2,1)S(1)} %get-tuple-element.36), channel_id=1, source_target_pairs={{0,1},{1,0},{2,3},{3,2},{4,5},{5,4},{6,7},{7,6},{8,9},{9,8},{10,11... | collective-permute-start | bytes 786440 | tf_op jit(solution)/shard_map/ppermute | solution.py:419
  49.6 26.1 %copy-start = (f32[256,1024]{1,0:T(8,128)S(1)}, f32[256,1024]{1,0:T(8,128)}, u32[]{:S(2)}) copy-start(f32[256,1024]{1,0:T(8,128)} %refs_0_.3) | copy-start | bytes 3145732
  49.6 4.3 %collective-permute-start.14 = (bf16[32,1024]{1,0:T(8,128)(2,1)S(1)}, bf16[32,1024]{1,0:T(8,128)(2,1)S(1)}, u32[]{:S(2)}, u32[]{:S(2)}) collective-permute-start(bf16[32,1024]{1,0:T(8,128)(2,1)S(1)} %get-tuple-element.38), channel_id=1, source_target_pairs={{0,8},{8,0},{16,24},{24,16},{1,9},{9,1},{17,25},{25,17},{2,10},{10... | collective-permute-start | bytes 196616 | tf_op jit(solution)/shard_map/ppermute | solution.py:413
  51.3 5.0 %collective-permute-start.15 = (bf16[32,1024]{1,0:T(8,128)(2,1)S(1)}, bf16[32,1024]{1,0:T(8,128)(2,1)S(1)}, u32[]{:S(2)}, u32[]{:S(2)}) collective-permute-start(bf16[32,1024]{1,0:T(8,128)(2,1)S(1)} %get-tuple-element.39), channel_id=1, source_target_pairs={{0,16},{8,24},{16,0},{24,8},{1,17},{9,25},{17,1},{25,9},{2,18},{10... | collective-permute-start | bytes 196616 | tf_op jit(solution)/shard_map/ppermute | solution.py:413
  52.1 5.2 %collective-permute-start.16 = (bf16[32,1024]{1,0:T(8,128)(2,1)S(1)}, bf16[32,1024]{1,0:T(8,128)(2,1)S(1)}, u32[]{:S(2)}, u32[]{:S(2)}) collective-permute-start(bf16[32,1024]{1,0:T(8,128)(2,1)S(1)} %get-tuple-element.40), channel_id=1, source_target_pairs={{0,24},{8,16},{16,8},{24,0},{1,25},{9,17},{17,9},{25,1},{2,26},{10... | collective-permute-start | bytes 196616 | tf_op jit(solution)/shard_map/ppermute | solution.py:413
  57.3 8.6 %collective-permute-start.20 = (bf16[32,1024]{1,0:T(8,128)(2,1)S(1)}, bf16[32,1024]{1,0:T(8,128)(2,1)S(1)}, u32[]{:S(2)}, u32[]{:S(2)}) collective-permute-start(bf16[32,1024]{1,0:T(8,128)(2,1)S(1)} %get-tuple-element.44), channel_id=1, source_target_pairs={{0,2},{1,3},{2,0},{3,1},{4,6},{5,7},{6,4},{7,5},{8,10},{9,11},{10,... | collective-permute-start | bytes 196616 | tf_op jit(solution)/shard_map/ppermute | solution.py:416
  62.3 9.7 %collective-permute-start.17 = (bf16[256,256]{1,0:T(8,128)(2,1)S(1)}, bf16[256,256]{1,0:T(8,128)(2,1)S(1)}, u32[]{:S(2)}, u32[]{:S(2)}) collective-permute-start(bf16[256,256]{1,0:T(8,128)(2,1)S(1)} %sum_rows.1.refs_2_), channel_id=1, source_target_pairs={{0,8},{8,0},{16,24},{24,16},{1,9},{9,1},{17,25},{25,17},{2,10},{10... | collective-permute-start | bytes 393224 | tf_op jit(solution)/shard_map/ppermute | solution.py:413
  63.9 6.1 %collective-permute-start.21 = (bf16[32,1024]{1,0:T(8,128)(2,1)S(1)}, bf16[32,1024]{1,0:T(8,128)(2,1)S(1)}, u32[]{:S(2)}, u32[]{:S(2)}) collective-permute-start(bf16[32,1024]{1,0:T(8,128)(2,1)S(1)} %get-tuple-element.45), channel_id=1, source_target_pairs={{0,4},{1,5},{2,6},{3,7},{4,0},{5,1},{6,2},{7,3},{8,12},{9,13},{10,... | collective-permute-start | bytes 196616 | tf_op jit(solution)/shard_map/ppermute | solution.py:416
  63.9 11.7 %collective-permute-start.19 = (bf16[256,256]{1,0:T(8,128)(2,1)S(1)}, bf16[256,256]{1,0:T(8,128)(2,1)S(1)}, u32[]{:S(2)}, u32[]{:S(2)}) collective-permute-start(bf16[256,256]{1,0:T(8,128)(2,1)S(1)} %sum_rows.1.refs_2_), channel_id=1, source_target_pairs={{0,24},{8,16},{16,8},{24,0},{1,25},{9,17},{17,9},{25,1},{2,26},{10... | collective-permute-start | bytes 393224 | tf_op jit(solution)/shard_map/ppermute | solution.py:413
  65.4 10.3 %collective-permute-start.18 = (bf16[256,256]{1,0:T(8,128)(2,1)S(1)}, bf16[256,256]{1,0:T(8,128)(2,1)S(1)}, u32[]{:S(2)}, u32[]{:S(2)}) collective-permute-start(bf16[256,256]{1,0:T(8,128)(2,1)S(1)} %sum_rows.1.refs_2_), channel_id=1, source_target_pairs={{0,16},{8,24},{16,0},{24,8},{1,17},{9,25},{17,1},{25,9},{2,18},{10... | collective-permute-start | bytes 393224 | tf_op jit(solution)/shard_map/ppermute | solution.py:413
  65.9 6.2 %collective-permute-start.22 = (bf16[32,1024]{1,0:T(8,128)(2,1)S(1)}, bf16[32,1024]{1,0:T(8,128)(2,1)S(1)}, u32[]{:S(2)}, u32[]{:S(2)}) collective-permute-start(bf16[32,1024]{1,0:T(8,128)(2,1)S(1)} %get-tuple-element.46), channel_id=1, source_target_pairs={{0,6},{1,7},{2,4},{3,5},{4,2},{5,3},{6,0},{7,1},{8,14},{9,15},{10,... | collective-permute-start | bytes 196616 | tf_op jit(solution)/shard_map/ppermute | solution.py:416
  72.1 3.6 %copy-start.5 = (f32[256]{0:T(256)S(1)}, f32[256]{0:T(256)}, u32[]{:S(2)}) copy-start(f32[256]{0:T(256)} %param.10) | copy-start | bytes 3076
  72.1 5.2 %collective-permute-start.25 = (bf16[32,1024]{1,0:T(8,128)(2,1)S(1)}, bf16[32,1024]{1,0:T(8,128)(2,1)S(1)}, u32[]{:S(2)}, u32[]{:S(2)}) collective-permute-start(bf16[32,1024]{1,0:T(8,128)(2,1)S(1)} %sum_parts.1.refs_0_), channel_id=1, source_target_pairs={{0,24},{8,16},{16,8},{24,0},{1,25},{9,17},{17,9},{25,1},{2,26},{10... | collective-permute-start | bytes 196616 | tf_op jit(solution)/shard_map/ppermute | solution.py:413
  74.0 4.3 %collective-permute-start.24 = (bf16[32,1024]{1,0:T(8,128)(2,1)S(1)}, bf16[32,1024]{1,0:T(8,128)(2,1)S(1)}, u32[]{:S(2)}, u32[]{:S(2)}) collective-permute-start(bf16[32,1024]{1,0:T(8,128)(2,1)S(1)} %sum_parts.1.refs_0_), channel_id=1, source_target_pairs={{0,16},{8,24},{16,0},{24,8},{1,17},{9,25},{17,1},{25,9},{2,18},{10... | collective-permute-start | bytes 196616 | tf_op jit(solution)/shard_map/ppermute | solution.py:413
  75.2 4.3 %collective-permute-start.23 = (bf16[32,1024]{1,0:T(8,128)(2,1)S(1)}, bf16[32,1024]{1,0:T(8,128)(2,1)S(1)}, u32[]{:S(2)}, u32[]{:S(2)}) collective-permute-start(bf16[32,1024]{1,0:T(8,128)(2,1)S(1)} %sum_parts.1.refs_0_), channel_id=1, source_target_pairs={{0,8},{8,0},{16,24},{24,16},{1,9},{9,1},{17,25},{25,17},{2,10},{10... | collective-permute-start | bytes 196616 | tf_op jit(solution)/shard_map/ppermute | solution.py:413

commit v4 on v3

--- a/solution.py
+++ b/solution.py
@@ -139,7 +139,20 @@
     return lax.dot_general(a, b, (((1,), (0,)), ((), ())), preferred_element_type=F32)
 
 
-def call(kernel, name, out, ins, smem=0, after=(), scratch=(), hbm=(), limit=32 << 20, cost=0, placed=False):
+def call(
+    kernel,
+    name,
+    out,
+    ins,
+    smem=0,
+    after=(),
+    scratch=(),
+    hbm=(),
+    limit=16 << 20,
+    cost=0,
+    placed=False,
+    out_hbm=False,
+):
     n_in, n_after = len(ins), len(after)
     many = isinstance(out, (list, tuple))
 
@@ -156,7 +169,7 @@
         out_shape=out,
         in_specs=[SMEM if i < smem else HBM if i in hbm else VMEM for i in range(n_in)]
         + [ANY] * n_after,
-        out_specs=[VMEM] * len(out) if many else VMEM,
+        out_specs=HBM if out_hbm else [VMEM] * len(out) if many else VMEM,
         scratch_shapes=list(scratch),
         name=name,
         cost_estimate=pl.CostEstimate(flops=cost, bytes_accessed=0, transcendentals=0),
@@ -179,19 +192,30 @@
     return copies
 
 
-def pack_kernel(me, lens, owner, local, q, k, weight, table, out, out_z, rows_in, part_in, sem):
-    n, _, pw = out.shape
-    pw = pw // 2
-    tok = q.shape[0]
+def carry_kernel(me, weight, table, out, rows_in, part_in, sem):
     rows, cols = rows_in.shape
     part = part_in.shape[0]
     copies = start_all(
         [
             (table.at[:, aligned(me[0], cols)], rows_in),
             (weight.at[aligned(me[0], part), :], part_in),
-        ]
-        + [
-            (x.at[:, i * pw : (i + 1) * pw], out.at[i, 0:tok, j * pw : (j + 1) * pw])
+        ],
+        sem,
+    )
+    copies[1].wait()
+    for i in range((out.shape[0] - cols) // part):
+        out[cols + i * part : cols + (i + 1) * part, :] = part_in[:, i * rows : (i + 1) * rows]
+    copies[0].wait()
+    out[0:cols, :] = rows_in[...].T.astype(BF16)
+
+
+def pack_kernel(lens, owner, local, q, k, out, ids, sem):
+    n, rows, pw = out.shape
+    tok = q.shape[0]
+    runs = tok // pw
+    later = start_all(
+        [
+            (x.at[:, i * pw : (i + 1) * pw], out.at[i, j * tok : (j + 1) * tok, :])
             for i in range(n)
             for j, x in enumerate((q, k))
         ],
@@ -204,7 +228,7 @@
     for i in range(lens.shape[1]):
         end = end + lens[0, i]
         seg = seg + jnp.where(lane >= end, 1.0, 0.0)
-    ids = jnp.where(
+    all_ids = jnp.where(
         row == 0,
         jnp.broadcast_to(owner[...].astype(F32), (EXTRA, tok)),
         jnp.where(
@@ -213,14 +237,12 @@
             jnp.where(row == 2, seg, 0.0),
         ),
     ).astype(BF16)
-    for i in range(n):
-        out[i, tok : tok + EXTRA, :] = ids
-    copies[0].wait()
-    out_z[0:cols, :] = rows_in[...].T.astype(BF16)
-    copies[1].wait()
-    for i in range((out_z.shape[0] - cols) // part):
-        out_z[cols + i * part : cols + (i + 1) * part, :] = part_in[:, i * rows : (i + 1) * rows]
-    for c in copies[2:]:
+    for i in range(runs):
+        ids[i * EXTRA : (i + 1) * EXTRA, :] = all_ids[:, i * pw : (i + 1) * pw]
+    later = later + start_all(
+        [(ids, out.at[i, 2 * tok : rows, :]) for i in range(n)], sem.at[pl.ds(2 * n, n)]
+    )
+    for c in later:
         c.wait()
 
 
@@ -262,17 +284,16 @@
 
 
 def weights_kernel(me, packs, out):
-    n, tok, pw = packs.shape
-    tok, pw = tok - EXTRA, pw // 2
-    heads = out.shape[1]
+    n, _, pw = packs.shape
+    heads, tok = out.shape[1:3]
     dqk = pw // heads
     down, across = iota((tok, tok), 0), iota((tok, tok), 1)
     lane = iota((tok, pw), 1)
     for r in range(n):
         p = packs.at[me[0] ^ r]
-        q = p[0:tok, 0:pw]
-        k = p[0:tok, pw : 2 * pw]
-        seg = ids_of(packs, me[0] ^ r)[2:3, :]
+        q = p[0:tok, :]
+        k = p[tok : 2 * tok, :]
+        seg = ids_of(packs, me[0] ^ r, tok)[2:3, :]
         seg_down = jnp.sum(jnp.where(down == across, seg, 0.0), axis=1, keepdims=True)
         mask = (seg == seg_down) & (down <= across)
         for j in range(heads):
@@ -282,9 +303,10 @@
             out[r, j] = jnp.where(mask, w, 0.0).astype(BF16)
 
 
-def ids_of(packs, r):
-    rows = packs.shape[1]
-    return packs[r, rows - EXTRA : rows, :].astype(F32)
+def ids_of(packs, r, tok):
+    runs = tok // packs.shape[2]
+    ids = packs[r, 2 * tok : 2 * tok + runs * EXTRA, :].astype(F32)
+    return jnp.concatenate([ids[i * EXTRA : (i + 1) * EXTRA] for i in range(runs)], axis=1)
 
 
 def one_hot(ids, shard, rows):
@@ -300,7 +322,7 @@
     dv = cols // heads
     blocks = jnp.concatenate([x[z] for z in range(n) for x in (mine, other)], axis=1)
     for r in range(n):
-        ids = ids_of(packs, me[0] ^ r)
+        ids = ids_of(packs, me[0] ^ r, w.shape[2])
         picks = jnp.concatenate(
             [one_hot(ids, 2 * z + (me[2] ^ cc), rows) for z in range(n) for cc in range(2)], axis=0
         )
@@ -311,12 +333,18 @@
             ).astype(BF16)
 
 
+def by_row(me, packs, grad, core, z, rows):
+    n = packs.shape[0]
+    tok = grad.shape[0] // n
+    ids = jnp.concatenate([ids_of(packs, me[0] ^ r, tok) for r in range(n)], axis=1)
+    return nn(one_hot(ids, 2 * z + core, rows), grad[...])
+
+
 def back_kernel(me, packs, ow_mine, ow_other, w, *refs):
-    *cots, keep, send, ow, grad = refs
+    *cots, send, grad, ow = refs
     n = packs.shape[0]
     heads, tok = w.shape[1:3]
     head_rows = ow_mine.shape[0]
-    rows = send.shape[1]
     ow[aligned(me[2], head_rows), :] = ow_mine[...]
     ow[aligned(1 - me[2], head_rows), :] = ow_other[...]
     first = 0
@@ -329,14 +357,13 @@
         for j in range(heads):
             at_j = slice(j * head_rows, (j + 1) * head_rows)
             grad[at_r, at_j] = nn(w[r, j], grad[at_r, at_j]).astype(BF16)
-    ids = jnp.concatenate([ids_of(packs, me[0] ^ r) for r in range(n)], axis=1)
-    for cc in (1, 0):
-        for z in range(n):
-            total = nn(one_hot(ids, 2 * z + (me[2] ^ cc), rows), grad[...])
-            if cc == 0:
-                keep[z] = total
-            else:
-                send[z] = total.astype(BF16)
+    for z in range(n):
+        send[z] = by_row(me, packs, grad, 1 - me[2], z, send.shape[1]).astype(BF16)
+
+
+def keep_kernel(me, packs, grad, keep):
+    for z in range(keep.shape[0]):
+        keep[z] = by_row(me, packs, grad, me[2], z, keep.shape[1])
 
 
 def wgrad_kernel(me, mixed, *refs):
@@ -428,28 +455,32 @@
     half = tok // 2
     x, y = column(cotangent, 1), column(cotangent, 2)
     zrows = cols + part * width // rows
-    packs, zpay = call(
-        pack_kernel,
-        "pack",
-        [sds((n, tok + EXTRA, 2 * queries.shape[1] // n)), sds((zrows, rows))],
-        (
-            lengths,
-            owner.reshape(1, tok),
-            local_row.reshape(1, tok),
-            queries,
-            keys,
-            out_weight,
-            table,
-        ),
-        smem=1,
-        hbm=(3, 4, 5, 6),
+    zpay = call(
+        carry_kernel,
+        "carry",
+        sds((zrows, rows)),
+        (out_weight, table),
+        hbm=(0, 1),
         scratch=[
             pltpu.VMEM((rows, cols), F32),
             pltpu.VMEM((part, width), BF16),
-            pltpu.SemaphoreType.DMA((2 * n + 2,)),
+            pltpu.SemaphoreType.DMA((2,)),
         ],
         limit=None,
         placed=True,
+    )
+    pw = queries.shape[1] // n
+    packs = call(
+        pack_kernel,
+        "pack",
+        sds((n, 2 * tok + tok // pw * EXTRA, pw)),
+        (lengths, owner.reshape(1, tok), local_row.reshape(1, tok), queries, keys),
+        smem=1,
+        out_hbm=True,
+        scratch=[
+            pltpu.VMEM((tok // pw * EXTRA, pw), BF16),
+            pltpu.SemaphoreType.DMA((3 * n,)),
+        ],
     )
     packs = swap_columns(packs)
     blocks = [along(zpay, m) for m in range(n)]
@@ -474,7 +505,7 @@
         "choose",
         [sds((zrows - cols, rows))] * n,
         blocks,
-        after=(w,),
+        after=(packs,),
         scratch=[pltpu.VMEM((n, zrows - cols, rows), BF16)],
         placed=True,
     )
@@ -492,16 +523,18 @@
     mixed = call(
         mix_kernel, "mix", sds((cols, n * tok)), (packs, w, mine, other), placed=True
     )
-    keep, send = call(
+    send, grad = call(
         back_kernel,
         "back",
-        [sds((n, rows, cols), F32), sds((n, rows, cols))],
+        [sds((n, rows, cols)), sds((n * tok, cols))],
         (packs, ow_mine, ow_other, w, *cots),
         after=(here, mixed),
-        scratch=[pltpu.VMEM((cols, width), BF16), pltpu.VMEM((n * tok, cols), BF16)],
+        scratch=[pltpu.VMEM((cols, width), BF16)],
         placed=True,
     )
-    sums = call(add_kernel, "add", sds((n, rows, cols)), (keep, core(send)))
+    got = core(send)
+    keep = call(keep_kernel, "keep", sds((n, rows, cols), F32), (packs, grad), placed=True)
+    sums = call(add_kernel, "add", sds((n, rows, cols)), (keep, got))
     ready = sums
     sums = swap_along(sums)
     wkeep, wsend = call(
@@ -526,10 +559,9 @@
         placed=True,
         scratch=[pltpu.VMEM((n, part, width), BF16)],
     )
-    wready = wparts[0]
     wparts = [along(p, m) for m, p in enumerate(wparts)]
 
-    grad = call(sum_first_kernel, "sum_rows", sds((rows, cols)), (sums,), after=(wready,))
+    grad = call(sum_first_kernel, "sum_rows", sds((rows, cols)), (sums,))
     grads = [column(grad, m) for m in range(n)]
     wsum = call(sum_kernel, "sum_parts", sds((part, width)), wparts, after=(grads[1],))
     wsums = [column(wsum, m) for m in range(n)]

time: 80.4 us -> 77.9 us (0.969)
  waiting for transfers between devices: 27.8 us -> 23.5 us
  starting transfers between devices: 38 us -> 39.1 us
    all_to_all x1, waiting for transfers between devices: 4.83 us -> 0.01 us  [swap_columns(): return lax.all_to_all(x, 'replica', 0, 0, tiled=True)]
    ppermute x6, waiting for transfers between devices: 6.17 us -> 9.82 us  [along(): lax.ppermute(x, 'shard', [(i, i ^ 2 * m) for i in range(shards)])]
    ppermute x16, waiting for transfers between devices: 10.8 us -> 8.64 us  [column(): lax.ppermute(x, 'replica', [(i, i ^ m) for i in range(n)])]
    ppermute x16, starting transfers between devices: 21.3 us -> 22.1 us  [column(): lax.ppermute(x, 'replica', [(i, i ^ m) for i in range(n)])]
    pallas_call x17 -> x19, Pallas kernels: 13.6 us -> 13.5 us  [call(): pl.pallas_call(run, out_shape=out, in_specs=[SMEM if i < smem else HBM if...]
  transfers between devices with their start and end apart: 28 -> 28, of which waited for: 18 -> 15; matrix products, arithmetic and copies ran while one was open for 0% -> 0% of each run, Pallas kernels for 12% -> 13%
where the time goes in v4:
time: 77.9 us; the launch traced here: 77.7 us
  starting transfers between devices  39.1 us (50%)
  waiting for transfers between devices  23.5 us (30%)
  Pallas kernels  13.5 us (17%)
  between operations  0.88 us (1%)
    ppermute x16, starting transfers between devices, column(): lax.ppermute(x, 'replica', [(i, i ^ m) for i in range(n)])  22.1 us
    pallas_call x19, Pallas kernels, call(): pl.pallas_call(run, out_shape=out, in_specs=[SMEM if i < smem else HBM if...  13.5 us
    ppermute x6, waiting for transfers between devices, along(): lax.ppermute(x, 'shard', [(i, i ^ 2 * m) for i in range(shards)])  9.82 us
    ppermute x16, waiting for transfers between devices, column(): lax.ppermute(x, 'replica', [(i, i ^ m) for i in range(n)])  8.64 us
    ppermute x6, starting transfers between devices, along(): lax.ppermute(x, 'shard', [(i, i ^ 2 * m) for i in range(shards)])  8 us
    all_to_all x1, starting transfers between devices, swap_along(): lax.all_to_all(x, 'shard', 0, 0, tiled=True, axis_index_groups=groups)  4.79 us
    all_to_all x1, starting transfers between devices, swap_columns(): return lax.all_to_all(x, 'replica', 0, 0, tiled=True)  3.49 us
    all_to_all x1, waiting for transfers between devices, swap_along(): lax.all_to_all(x, 'shard', 0, 0, tiled=True, axis_index_groups=groups)  2.75 us
  transfers between devices with their start and end apart: 28, of which 15 were waited for; matrix products, arithmetic and copies ran while one was open for 0% of the time, Pallas kernels for 13%

profile of v4, /device:TPU:0, one launch (start us, length us, event | category | flops | bytes accessed | tf_op | source)
XLA Modules:
  0.0 77.7 jit_solution(7509136523605271097)
XLA Ops:
  0.7 3.0 %collective-permute-start.8 = (bf16[256,1024]{1,0:T(8,128)(2,1)}, bf16[256,1024]{1,0:T(8,128)(2,1)S(1)}, u32[]{:S(2)}, u32[]{:S(2)}) collective-permute-start(bf16[256,1024]{1,0:T(8,128)(2,1)} %refs_1_.3), channel_id=1, source_target_pairs={{0,16},{8,24},{16,0},{24,8},{1,17},{9,25},{17,1},{25,9},{2,18},{10... | collective-permute-start | bytes 1572872 | tf_op jit(solution)/shard_map/ppermute | solution.py:440
  3.7 1.5 %collective-permute-start.7 = (bf16[256,1024]{1,0:T(8,128)(2,1)}, bf16[256,1024]{1,0:T(8,128)(2,1)S(1)}, u32[]{:S(2)}, u32[]{:S(2)}) collective-permute-start(bf16[256,1024]{1,0:T(8,128)(2,1)} %refs_1_.3), channel_id=1, source_target_pairs={{0,8},{8,0},{16,24},{24,16},{1,9},{9,1},{17,25},{25,17},{2,10},{10... | collective-permute-start | bytes 1572872 | tf_op jit(solution)/shard_map/ppermute | solution.py:440
  5.2 1.8 %carry.1.refs_0_ = bf16[384,256]{1,0:T(8,128)(2,1)} custom-call(bf16[128,1024]{1,0:T(8,128)(2,1)} %refs_0_.4, f32[256,1024]{1,0:T(8,128)} %refs_0_.5), custom_call_target="tpu_custom_call" | custom-call | tf_op jit(solution)/shard_map/carry/pallas_call | solution.py:167
  6.9 3.7 %collective-permute-start.2 = (bf16[384,256]{1,0:T(8,128)(2,1)}, bf16[384,256]{1,0:T(8,128)(2,1)S(1)}, u32[]{:S(2)}, u32[]{:S(2)}) collective-permute-start(bf16[384,256]{1,0:T(8,128)(2,1)} %carry.1.refs_0_), channel_id=1, source_target_pairs={{0,6},{1,7},{2,4},{3,5},{4,2},{5,3},{6,0},{7,1},{8,14},{9,15},{10,... | collective-permute-start | bytes 589832 | tf_op jit(solution)/shard_map/ppermute | solution.py:443
  10.6 0.8 %collective-permute-start = (bf16[384,256]{1,0:T(8,128)(2,1)}, bf16[384,256]{1,0:T(8,128)(2,1)S(1)}, u32[]{:S(2)}, u32[]{:S(2)}) collective-permute-start(bf16[384,256]{1,0:T(8,128)(2,1)} %carry.1.refs_0_), channel_id=1, source_target_pairs={{0,2},{1,3},{2,0},{3,1},{4,6},{5,7},{6,4},{7,5},{8,10},{9,11},{10,... | collective-permute-start | bytes 589832 | tf_op jit(solution)/shard_map/ppermute | solution.py:443
  11.4 0.7 copy-done.5
  12.1 1.4 %pack.1 = bf16[4,544,128]{2,1,0:T(8,128)(2,1)} custom-call(s32[1,4]{1,0:T(1,128)S(1)} %copy-done.8, s32[1,256]{1,0:T(1,128)S(1)} %bitcast.4, s32[1,256]{1,0:T(1,128)S(1)} %bitcast.5, bf16[256,512]{1,0:T(8,128)(2,1)S(1)} %copy-done.3, bf16[256,512]{1,0:T(8,128)(2,1)S(1)} %copy-done.4), custom_call_target="tpu_custom_call" | custom-call | tf_op jit(solution)/shard_map/pack/pallas_call | solution.py:167
  13.5 3.5 %all-to-all-start = ((bf16[4,544,128]{2,1,0:T(8,128)(2,1)}), bf16[4,544,128]{2,1,0:T(8,128)(2,1)S(1)}, u32[]{:S(2)}, u32[]{:S(2)}) async-start(bf16[4,544,128]{2,1,0:T(8,128)(2,1)} %pack.1), calls=%async_computation | async-start | bytes 1114112 | tf_op jit(solution)/shard_map/all_to_all | solution.py:453
  17.0 0.2 collective-permute-done.7.refs_0_.refs_5_.refs_2_
  17.3 1.8 %collective-permute-start.10 = (bf16[128,1024]{1,0:T(8,128)(2,1)S(1)}, bf16[128,1024]{1,0:T(8,128)(2,1)S(1)}, u32[]{:S(2)}, u32[]{:S(2)}) collective-permute-start(bf16[128,1024]{1,0:T(8,128)(2,1)S(1)} %get-tuple-element.28), channel_id=1, source_target_pairs={{0,16},{8,24},{16,0},{24,8},{1,17},{9,25},{17,1},{25,9},{2,18},{10... | collective-permute-start | bytes 786440 | tf_op jit(solution)/shard_map/ppermute | solution.py:440
  19.1 1.5 %collective-permute-start.9 = (bf16[128,1024]{1,0:T(8,128)(2,1)S(1)}, bf16[128,1024]{1,0:T(8,128)(2,1)S(1)}, u32[]{:S(2)}, u32[]{:S(2)}) collective-permute-start(bf16[128,1024]{1,0:T(8,128)(2,1)S(1)} %get-tuple-element.27.refs_1_), channel_id=1, source_target_pairs={{0,8},{8,0},{16,24},{24,16},{1,9},{9,1},{17,25},{25,17},{2,10},{10... | collective-permute-start | bytes 786440 | tf_op jit(solution)/shard_map/ppermute | solution.py:440
  20.6 6.3 %collective-permute-done.1.refs_2_ = bf16[384,256]{1,0:T(8,128)(2,1)S(1)} collective-permute-done((bf16[384,256]{1,0:T(8,128)(2,1)}, bf16[384,256]{1,0:T(8,128)(2,1)S(1)}, u32[]{:S(2)}, u32[]{:S(2)}) %collective-permute-start.1) | collective-permute-done | bytes 196640 | tf_op jit(solution)/shard_map/ppermute | solution.py:443
  27.0 1.4 %collective-permute-start.3 = (bf16[128,256]{1,0:T(8,128)(2,1)S(1)}, bf16[128,256]{1,0:T(8,128)(2,1)S(1)}, u32[]{:S(2)}, u32[]{:S(2)}) collective-permute-start(bf16[128,256]{1,0:T(8,128)(2,1)S(1)} %get-tuple-element.24), channel_id=1, source_target_pairs={{0,8},{8,0},{16,24},{24,16},{1,9},{9,1},{17,25},{25,17},{2,10},{10... | collective-permute-start | bytes 196616 | tf_op jit(solution)/shard_map/ppermute | solution.py:440
  28.4 2.1 %collective-permute-start.5 = (bf16[128,256]{1,0:T(8,128)(2,1)S(1)}, bf16[128,256]{1,0:T(8,128)(2,1)S(1)}, u32[]{:S(2)}, u32[]{:S(2)}) collective-permute-start(bf16[128,256]{1,0:T(8,128)(2,1)S(1)} %get-tuple-element.26), channel_id=1, source_target_pairs={{0,24},{8,16},{16,8},{24,0},{1,25},{9,17},{17,9},{25,1},{2,26},{10... | collective-permute-start | bytes 196616 | tf_op jit(solution)/shard_map/ppermute | solution.py:440
  30.6 1.5 %collective-permute-done.3.refs_1_ = bf16[128,256]{1,0:T(8,128)(2,1)S(1)} collective-permute-done((bf16[128,256]{1,0:T(8,128)(2,1)S(1)}, bf16[128,256]{1,0:T(8,128)(2,1)S(1)}, u32[]{:S(2)}, u32[]{:S(2)}) %collective-permute-start.3) | collective-permute-done | bytes 65568 | tf_op jit(solution)/shard_map/ppermute | solution.py:440
  32.1 0.6 collective-permute-done.4.refs_2_
  32.7 1.0 %collective-permute-done.5.refs_3_ = bf16[128,256]{1,0:T(8,128)(2,1)S(1)} collective-permute-done((bf16[128,256]{1,0:T(8,128)(2,1)S(1)}, bf16[128,256]{1,0:T(8,128)(2,1)S(1)}, u32[]{:S(2)}, u32[]{:S(2)}) %collective-permute-start.5) | collective-permute-done | bytes 65568 | tf_op jit(solution)/shard_map/ppermute | solution.py:440
  33.8 0.8 %weights.1.refs_1_.refs_3_ = bf16[4,2,256,256]{3,2,1,0:T(8,128)(2,1)S(1)} custom-call(bf16[4,544,128]{2,1,0:T(8,128)(2,1)S(1)} %all-to-all-done.refs_4_.refs_0_, bf16[128,1024]{1,0:T(8,128)(2,1)S(1)} %get-tuple-element.27.refs_1_), custom_call_target="tpu_custom_call" | custom-call | tf_op jit(solution)/shard_map/weights/pallas_call | solution.py:167
  34.7 2.8 %mix.1.refs_10_.refs_0_ = bf16[256,1024]{1,0:T(8,128)(2,1)S(1)} custom-call(bf16[4,544,128]{2,1,0:T(8,128)(2,1)S(1)} %all-to-all-done.refs_4_.refs_0_, bf16[4,2,256,256]{3,2,1,0:T(8,128)(2,1)S(1)} %weights.1.refs_1_.refs_3_, bf16[4,256,256]{2,1,0:T(8,128)(2,1)S(1)} %stack.1.refs_2_, bf16[4,256,256]{2,1,0:T(8,128)(2,1)S(1)} %collective-permute-done.11.refs_3_), custom_call_target="tpu_custom_call" | custom-call | tf_op jit(solution)/shard_map/mix/pallas_call | solution.py:167
  37.5 1.8 %back.1 = (bf16[4,256,256]{2,1,0:T(8,128)(2,1)S(1)}, bf16[1024,256]{1,0:T(8,128)(2,1)S(1)}) custom-call(bf16[4,544,128]{2,1,0:T(8,128)(2,1)S(1)} %all-to-all-done.refs_4_.refs_0_, bf16[128,1024]{1,0:T(8,128)(2,1)S(1)} %join.1.refs_1_, bf16[128,1024]{1,0:T(8,128)(2,1)S(1)} %collective-permute-done.6.refs_2_, ...), custom_call_target="tpu_custom_call" | custom-call | tf_op jit(solution)/shard_map/back/pallas_call | solution.py:167
  39.4 0.6 collective-permute-start.12
  39.9 0.7 keep.1.refs_0_
  40.6 0.8 %collective-permute-done.12.refs_1_ = bf16[4,256,256]{2,1,0:T(8,128)(2,1)S(1)} collective-permute-done((bf16[4,256,256]{2,1,0:T(8,128)(2,1)S(1)}, bf16[4,256,256]{2,1,0:T(8,128)(2,1)S(1)}, u32[]{:S(2)}, u32[]{:S(2)}) %collective-permute-start.12) | collective-permute-done | bytes 524320 | tf_op jit(solution)/shard_map/ppermute | solution.py:446
  41.5 0.9 %add.1.refs_6_ = bf16[4,256,256]{2,1,0:T(8,128)(2,1)} custom-call(f32[4,256,256]{2,1,0:T(8,128)S(1)} %keep.1.refs_0_, bf16[4,256,256]{2,1,0:T(8,128)(2,1)S(1)} %collective-permute-done.12.refs_1_), custom_call_target="tpu_custom_call" | custom-call | tf_op jit(solution)/shard_map/add/pallas_call | solution.py:167
  42.3 4.8 %all-to-all-start.1 = ((bf16[4,256,256]{2,1,0:T(8,128)(2,1)}), bf16[4,256,256]{2,1,0:T(8,128)(2,1)S(1)}, u32[]{:S(2)}, u32[]{:S(2)}) async-start(bf16[4,256,256]{2,1,0:T(8,128)(2,1)} %add.1.refs_6_), calls=%async_computation.1 | async-start | bytes 1048576 | tf_op jit(solution)/shard_map/all_to_all | solution.py:450
  47.1 0.8 %wgrad.1 = (f32[128,1024]{1,0:T(8,128)S(1)}, bf16[128,1024]{1,0:T(8,128)(2,1)S(1)}) custom-call(bf16[256,1024]{1,0:T(8,128)(2,1)S(1)} %mix.1.refs_10_.refs_0_, bf16[256,1024]{1,0:T(8,128)(2,1)S(1)} %copy-done.1, bf16[256,1024]{1,0:T(8,128)(2,1)S(1)} %collective-permute-done.7.refs_0_.refs_5_.refs_2_, ...), custom_call_target="tpu_custom_call" | custom-call | tf_op jit(solution)/shard_map/wgrad/pallas_call | solution.py:167
  48.0 0.1 collective-permute-start.16
  48.1 1.5 %collective-permute-done.16.refs_1_ = bf16[128,1024]{1,0:T(8,128)(2,1)S(1)} collective-permute-done((bf16[128,1024]{1,0:T(8,128)(2,1)S(1)}, bf16[128,1024]{1,0:T(8,128)(2,1)S(1)}, u32[]{:S(2)}, u32[]{:S(2)}) %collective-permute-start.16) | collective-permute-done | bytes 262176 | tf_op jit(solution)/shard_map/ppermute | solution.py:446
  49.6 2.0 %collective-permute-start.17 = (bf16[32,1024]{1,0:T(8,128)(2,1)S(1)}, bf16[32,1024]{1,0:T(8,128)(2,1)S(1)}, u32[]{:S(2)}, u32[]{:S(2)}) collective-permute-start(bf16[32,1024]{1,0:T(8,128)(2,1)S(1)} %get-tuple-element.36), channel_id=1, source_target_pairs={{0,8},{8,0},{16,24},{24,16},{1,9},{9,1},{17,25},{25,17},{2,10},{10... | collective-permute-start | bytes 196616 | tf_op jit(solution)/shard_map/ppermute | solution.py:440
  51.6 0.6 collective-permute-start.18
  52.2 1.0 %collective-permute-start.19 = (bf16[32,1024]{1,0:T(8,128)(2,1)S(1)}, bf16[32,1024]{1,0:T(8,128)(2,1)S(1)}, u32[]{:S(2)}, u32[]{:S(2)}) collective-permute-start(bf16[32,1024]{1,0:T(8,128)(2,1)S(1)} %get-tuple-element.38), channel_id=1, source_target_pairs={{0,24},{8,16},{16,8},{24,0},{1,25},{9,17},{17,9},{25,1},{2,26},{10... | collective-permute-start | bytes 196616 | tf_op jit(solution)/shard_map/ppermute | solution.py:440
  53.2 0.8 %collective-permute-done.17.refs_1_ = bf16[32,1024]{1,0:T(8,128)(2,1)S(1)} collective-permute-done((bf16[32,1024]{1,0:T(8,128)(2,1)S(1)}, bf16[32,1024]{1,0:T(8,128)(2,1)S(1)}, u32[]{:S(2)}, u32[]{:S(2)}) %collective-permute-start.17) | collective-permute-done | bytes 65568 | tf_op jit(solution)/shard_map/ppermute | solution.py:440
  54.0 2.6 %collective-permute-done.18.refs_2_ = bf16[32,1024]{1,0:T(8,128)(2,1)S(1)} collective-permute-done((bf16[32,1024]{1,0:T(8,128)(2,1)S(1)}, bf16[32,1024]{1,0:T(8,128)(2,1)S(1)}, u32[]{:S(2)}, u32[]{:S(2)}) %collective-permute-start.18) | collective-permute-done | bytes 65568 | tf_op jit(solution)/shard_map/ppermute | solution.py:440
  56.6 0.8 collective-permute-done.19.refs_3_
  57.4 2.1 %collective-permute-start.20 = (bf16[32,1024]{1,0:T(8,128)(2,1)S(1)}, bf16[32,1024]{1,0:T(8,128)(2,1)S(1)}, u32[]{:S(2)}, u32[]{:S(2)}) collective-permute-start(bf16[32,1024]{1,0:T(8,128)(2,1)S(1)} %get-tuple-element.40), channel_id=1, source_target_pairs={{0,2},{1,3},{2,0},{3,1},{4,6},{5,7},{6,4},{7,5},{8,10},{9,11},{10,... | collective-permute-start | bytes 196616 | tf_op jit(solution)/shard_map/ppermute | solution.py:443
  59.5 2.7 %all-to-all-done.1.refs_0_ = bf16[4,256,256]{2,1,0:T(8,128)(2,1)S(1)} async-done(((bf16[4,256,256]{2,1,0:T(8,128)(2,1)}), bf16[4,256,256]{2,1,0:T(8,128)(2,1)S(1)}, u32[]{:S(2)}, u32[]{:S(2)}) %all-to-all-start.1) | async-done | bytes 524320 | tf_op jit(solution)/shard_map/all_to_all | solution.py:450
  62.3 2.0 %collective-permute-start.13 = (bf16[256,256]{1,0:T(8,128)(2,1)S(1)}, bf16[256,256]{1,0:T(8,128)(2,1)S(1)}, u32[]{:S(2)}, u32[]{:S(2)}) collective-permute-start(bf16[256,256]{1,0:T(8,128)(2,1)S(1)} %sum_rows.1.refs_2_), channel_id=1, source_target_pairs={{0,8},{8,0},{16,24},{24,16},{1,9},{9,1},{17,25},{25,17},{2,10},{10... | collective-permute-start | bytes 393224 | tf_op jit(solution)/shard_map/ppermute | solution.py:440
  64.3 1.5 %collective-permute-start.22 = (bf16[32,1024]{1,0:T(8,128)(2,1)S(1)}, bf16[32,1024]{1,0:T(8,128)(2,1)S(1)}, u32[]{:S(2)}, u32[]{:S(2)}) collective-permute-start(bf16[32,1024]{1,0:T(8,128)(2,1)S(1)} %get-tuple-element.42), channel_id=1, source_target_pairs={{0,6},{1,7},{2,4},{3,5},{4,2},{5,3},{6,0},{7,1},{8,14},{9,15},{10,... | collective-permute-start | bytes 196616 | tf_op jit(solution)/shard_map/ppermute | solution.py:443
  65.8 1.5 %collective-permute-start.15 = (bf16[256,256]{1,0:T(8,128)(2,1)S(1)}, bf16[256,256]{1,0:T(8,128)(2,1)S(1)}, u32[]{:S(2)}, u32[]{:S(2)}) collective-permute-start(bf16[256,256]{1,0:T(8,128)(2,1)S(1)} %sum_rows.1.refs_2_), channel_id=1, source_target_pairs={{0,24},{8,16},{16,8},{24,0},{1,25},{9,17},{17,9},{25,1},{2,26},{10... | collective-permute-start | bytes 393224 | tf_op jit(solution)/shard_map/ppermute | solution.py:440
  67.3 0.2 collective-permute-start.14
  67.4 3.5 %collective-permute-done.21.refs_2_ = bf16[32,1024]{1,0:T(8,128)(2,1)S(1)} collective-permute-done((bf16[32,1024]{1,0:T(8,128)(2,1)S(1)}, bf16[32,1024]{1,0:T(8,128)(2,1)S(1)}, u32[]{:S(2)}, u32[]{:S(2)}) %collective-permute-start.21) | collective-permute-done | bytes 65568 | tf_op jit(solution)/shard_map/ppermute | solution.py:443
  70.9 1.5 %collective-permute-start.25 = (bf16[32,1024]{1,0:T(8,128)(2,1)S(1)}, bf16[32,1024]{1,0:T(8,128)(2,1)S(1)}, u32[]{:S(2)}, u32[]{:S(2)}) collective-permute-start(bf16[32,1024]{1,0:T(8,128)(2,1)S(1)} %sum_parts.1.refs_0_), channel_id=1, source_target_pairs={{0,24},{8,16},{16,8},{24,0},{1,25},{9,17},{17,9},{25,1},{2,26},{10... | collective-permute-start | bytes 196616 | tf_op jit(solution)/shard_map/ppermute | solution.py:440
  72.5 0.2 collective-permute-start.24
  72.7 1.8 %collective-permute-start.23 = (bf16[32,1024]{1,0:T(8,128)(2,1)S(1)}, bf16[32,1024]{1,0:T(8,128)(2,1)S(1)}, u32[]{:S(2)}, u32[]{:S(2)}) collective-permute-start(bf16[32,1024]{1,0:T(8,128)(2,1)S(1)} %sum_parts.1.refs_0_), channel_id=1, source_target_pairs={{0,8},{8,0},{16,24},{24,16},{1,9},{9,1},{17,25},{25,17},{2,10},{10... | collective-permute-start | bytes 196616 | tf_op jit(solution)/shard_map/ppermute | solution.py:440
  74.5 0.5 collective-permute-done.14.refs_4_
  75.0 1.3 %update.1 = (f32[256,1024]{1,0:T(8,128)}, f32[1,256]{1,0:T(1,128)}) custom-call(f32[256,1024]{1,0:T(8,128)S(1)} %copy-done, f32[1,256]{1,0:T(1,128)S(1)} %bitcast.6, bf16[256,256]{1,0:T(8,128)(2,1)S(1)} %sum_rows.1.refs_2_, bf16[256,256]{1,0:T(8,128)(2,1)S(1)} %collective-permute-done.13.refs_3_.refs_4_, ...), custom_call_target="tpu_custom_call" | custom-call | tf_op jit(solution)/shard_map/update/pallas_call | solution.py:167
  76.3 0.6 collective-permute-done.24.refs_2_
  76.9 0.7 place.1
  (45 shorter events, 0.6 us)
Async XLA Ops:
  0.6 10.8 %copy-start.4 = (bf16[256,512]{1,0:T(8,128)(2,1)S(1)}, bf16[256,512]{1,0:T(8,128)(2,1)}, u32[]{:S(2)}) copy-start(bf16[256,512]{1,0:T(8,128)(2,1)} %refs_4_.2) | copy-start | bytes 786436
  0.6 10.8 %copy-start.3 = (bf16[256,512]{1,0:T(8,128)(2,1)S(1)}, bf16[256,512]{1,0:T(8,128)(2,1)}, u32[]{:S(2)}) copy-start(bf16[256,512]{1,0:T(8,128)(2,1)} %refs_3_.1) | copy-start | bytes 786436
  0.7 16.4 %collective-permute-start.8 = (bf16[256,1024]{1,0:T(8,128)(2,1)}, bf16[256,1024]{1,0:T(8,128)(2,1)S(1)}, u32[]{:S(2)}, u32[]{:S(2)}) collective-permute-start(bf16[256,1024]{1,0:T(8,128)(2,1)} %refs_1_.3), channel_id=1, source_target_pairs={{0,16},{8,24},{16,0},{24,8},{1,17},{9,25},{17,1},{25,9},{2,18},{10... | collective-permute-start | bytes 1572872 | tf_op jit(solution)/shard_map/ppermute | solution.py:440
  3.7 13.6 %collective-permute-start.7 = (bf16[256,1024]{1,0:T(8,128)(2,1)}, bf16[256,1024]{1,0:T(8,128)(2,1)S(1)}, u32[]{:S(2)}, u32[]{:S(2)}) collective-permute-start(bf16[256,1024]{1,0:T(8,128)(2,1)} %refs_1_.3), channel_id=1, source_target_pairs={{0,8},{8,0},{16,24},{24,16},{1,9},{9,1},{17,25},{25,17},{2,10},{10... | collective-permute-start | bytes 1572872 | tf_op jit(solution)/shard_map/ppermute | solution.py:440
  5.2 6.2 %copy-start.6 = (s32[256]{0:T(256)S(1)}, s32[256]{0:T(256)}, u32[]{:S(2)}) copy-start(s32[256]{0:T(256)} %param.12) | copy-start | bytes 3076
  6.9 13.7 %collective-permute-start.2 = (bf16[384,256]{1,0:T(8,128)(2,1)}, bf16[384,256]{1,0:T(8,128)(2,1)S(1)}, u32[]{:S(2)}, u32[]{:S(2)}) collective-permute-start(bf16[384,256]{1,0:T(8,128)(2,1)} %carry.1.refs_0_), channel_id=1, source_target_pairs={{0,6},{1,7},{2,4},{3,5},{4,2},{5,3},{6,0},{7,1},{8,14},{9,15},{10,... | collective-permute-start | bytes 589832 | tf_op jit(solution)/shard_map/ppermute | solution.py:443
  10.6 16.3 %collective-permute-start.1 = (bf16[384,256]{1,0:T(8,128)(2,1)}, bf16[384,256]{1,0:T(8,128)(2,1)S(1)}, u32[]{:S(2)}, u32[]{:S(2)}) collective-permute-start(bf16[384,256]{1,0:T(8,128)(2,1)} %carry.1.refs_0_), channel_id=1, source_target_pairs={{0,4},{1,5},{2,6},{3,7},{4,0},{5,1},{6,2},{7,3},{8,12},{9,13},{10,... | collective-permute-start | bytes 589832 | tf_op jit(solution)/shard_map/ppermute | solution.py:443
  10.6 16.3 %collective-permute-start = (bf16[384,256]{1,0:T(8,128)(2,1)}, bf16[384,256]{1,0:T(8,128)(2,1)S(1)}, u32[]{:S(2)}, u32[]{:S(2)}) collective-permute-start(bf16[384,256]{1,0:T(8,128)(2,1)} %carry.1.refs_0_), channel_id=1, source_target_pairs={{0,2},{1,3},{2,0},{3,1},{4,6},{5,7},{6,4},{7,5},{8,10},{9,11},{10,... | collective-permute-start | bytes 589832 | tf_op jit(solution)/shard_map/ppermute | solution.py:443
  11.4 0.7 copy-start.5
  11.4 0.7 copy-start.8
  13.5 13.4 %all-to-all-start = ((bf16[4,544,128]{2,1,0:T(8,128)(2,1)}), bf16[4,544,128]{2,1,0:T(8,128)(2,1)S(1)}, u32[]{:S(2)}, u32[]{:S(2)}) async-start(bf16[4,544,128]{2,1,0:T(8,128)(2,1)} %pack.1), calls=%async_computation | async-start | bytes 1114112 | tf_op jit(solution)/shard_map/all_to_all | solution.py:453
  17.0 9.9 %copy-start.2 = (bf16[384,256]{1,0:T(8,128)(2,1)S(1)}, bf16[384,256]{1,0:T(8,128)(2,1)}, u32[]{:S(2)}) copy-start(bf16[384,256]{1,0:T(8,128)(2,1)} %carry.1.refs_0_) | copy-start | bytes 589828
  17.3 17.3 %collective-permute-start.10 = (bf16[128,1024]{1,0:T(8,128)(2,1)S(1)}, bf16[128,1024]{1,0:T(8,128)(2,1)S(1)}, u32[]{:S(2)}, u32[]{:S(2)}) collective-permute-start(bf16[128,1024]{1,0:T(8,128)(2,1)S(1)} %get-tuple-element.28), channel_id=1, source_target_pairs={{0,16},{8,24},{16,0},{24,8},{1,17},{9,25},{17,1},{25,9},{2,18},{10... | collective-permute-start | bytes 786440 | tf_op jit(solution)/shard_map/ppermute | solution.py:440
  19.1 15.5 %collective-permute-start.9 = (bf16[128,1024]{1,0:T(8,128)(2,1)S(1)}, bf16[128,1024]{1,0:T(8,128)(2,1)S(1)}, u32[]{:S(2)}, u32[]{:S(2)}) collective-permute-start(bf16[128,1024]{1,0:T(8,128)(2,1)S(1)} %get-tuple-element.27.refs_1_), channel_id=1, source_target_pairs={{0,8},{8,0},{16,24},{24,16},{1,9},{9,1},{17,25},{25,17},{2,10},{10... | collective-permute-start | bytes 786440 | tf_op jit(solution)/shard_map/ppermute | solution.py:440
  27.0 5.1 %collective-permute-start.3 = (bf16[128,256]{1,0:T(8,128)(2,1)S(1)}, bf16[128,256]{1,0:T(8,128)(2,1)S(1)}, u32[]{:S(2)}, u32[]{:S(2)}) collective-permute-start(bf16[128,256]{1,0:T(8,128)(2,1)S(1)} %get-tuple-element.24), channel_id=1, source_target_pairs={{0,8},{8,0},{16,24},{24,16},{1,9},{9,1},{17,25},{25,17},{2,10},{10... | collective-permute-start | bytes 196616 | tf_op jit(solution)/shard_map/ppermute | solution.py:440
  28.4 4.3 %collective-permute-start.4 = (bf16[128,256]{1,0:T(8,128)(2,1)S(1)}, bf16[128,256]{1,0:T(8,128)(2,1)S(1)}, u32[]{:S(2)}, u32[]{:S(2)}) collective-permute-start(bf16[128,256]{1,0:T(8,128)(2,1)S(1)} %get-tuple-element.25), channel_id=1, source_target_pairs={{0,16},{8,24},{16,0},{24,8},{1,17},{9,25},{17,1},{25,9},{2,18},{10... | collective-permute-start | bytes 196616 | tf_op jit(solution)/shard_map/ppermute | solution.py:440
  28.4 5.3 %collective-permute-start.5 = (bf16[128,256]{1,0:T(8,128)(2,1)S(1)}, bf16[128,256]{1,0:T(8,128)(2,1)S(1)}, u32[]{:S(2)}, u32[]{:S(2)}) collective-permute-start(bf16[128,256]{1,0:T(8,128)(2,1)S(1)} %get-tuple-element.26), channel_id=1, source_target_pairs={{0,24},{8,16},{16,8},{24,0},{1,25},{9,17},{17,9},{25,1},{2,26},{10... | collective-permute-start | bytes 196616 | tf_op jit(solution)/shard_map/ppermute | solution.py:440
  32.1 2.6 %collective-permute-start.11 = (bf16[4,256,256]{2,1,0:T(8,128)(2,1)S(1)}, bf16[4,256,256]{2,1,0:T(8,128)(2,1)S(1)}, u32[]{:S(2)}, u32[]{:S(2)}) collective-permute-start(bf16[4,256,256]{2,1,0:T(8,128)(2,1)S(1)} %stack.1.refs_2_), channel_id=1, source_target_pairs={{0,1},{1,0},{2,3},{3,2},{4,5},{5,4},{6,7},{7,6},{8,9},{9,8},{10,11... | collective-permute-start | bytes 1572872 | tf_op jit(solution)/shard_map/ppermute | solution.py:446
  33.7 3.8 %collective-permute-start.6 = (bf16[128,1024]{1,0:T(8,128)(2,1)S(1)}, bf16[128,1024]{1,0:T(8,128)(2,1)S(1)}, u32[]{:S(2)}, u32[]{:S(2)}) collective-permute-start(bf16[128,1024]{1,0:T(8,128)(2,1)S(1)} %join.1.refs_1_), channel_id=1, source_target_pairs={{0,1},{1,0},{2,3},{3,2},{4,5},{5,4},{6,7},{7,6},{8,9},{9,8},{10,11... | collective-permute-start | bytes 786440 | tf_op jit(solution)/shard_map/ppermute | solution.py:446
  34.7 2.8 %copy-start.1 = (bf16[256,1024]{1,0:T(8,128)(2,1)S(1)}, bf16[256,1024]{1,0:T(8,128)(2,1)}, u32[]{:S(2)}) copy-start(bf16[256,1024]{1,0:T(8,128)(2,1)} %refs_1_.3) | copy-start | bytes 1572868
  39.4 2.1 %collective-permute-start.12 = (bf16[4,256,256]{2,1,0:T(8,128)(2,1)S(1)}, bf16[4,256,256]{2,1,0:T(8,128)(2,1)S(1)}, u32[]{:S(2)}, u32[]{:S(2)}) collective-permute-start(bf16[4,256,256]{2,1,0:T(8,128)(2,1)S(1)} %get-tuple-element.30), channel_id=1, source_target_pairs={{0,1},{1,0},{2,3},{3,2},{4,5},{5,4},{6,7},{7,6},{8,9},{9,8},{10,11... | collective-permute-start | bytes 1572872 | tf_op jit(solution)/shard_map/ppermute | solution.py:446
  42.3 19.9 %all-to-all-start.1 = ((bf16[4,256,256]{2,1,0:T(8,128)(2,1)}), bf16[4,256,256]{2,1,0:T(8,128)(2,1)S(1)}, u32[]{:S(2)}, u32[]{:S(2)}) async-start(bf16[4,256,256]{2,1,0:T(8,128)(2,1)} %add.1.refs_6_), calls=%async_computation.1 | async-start | bytes 1048576 | tf_op jit(solution)/shard_map/all_to_all | solution.py:450
  48.0 1.6 %collective-permute-start.16 = (bf16[128,1024]{1,0:T(8,128)(2,1)S(1)}, bf16[128,1024]{1,0:T(8,128)(2,1)S(1)}, u32[]{:S(2)}, u32[]{:S(2)}) collective-permute-start(bf16[128,1024]{1,0:T(8,128)(2,1)S(1)} %get-tuple-element.34), channel_id=1, source_target_pairs={{0,1},{1,0},{2,3},{3,2},{4,5},{5,4},{6,7},{7,6},{8,9},{9,8},{10,11... | collective-permute-start | bytes 786440 | tf_op jit(solution)/shard_map/ppermute | solution.py:446
  49.6 25.4 %copy-start = (f32[256,1024]{1,0:T(8,128)S(1)}, f32[256,1024]{1,0:T(8,128)}, u32[]{:S(2)}) copy-start(f32[256,1024]{1,0:T(8,128)} %refs_0_.5) | copy-start | bytes 3145732
  49.6 4.4 %collective-permute-start.17 = (bf16[32,1024]{1,0:T(8,128)(2,1)S(1)}, bf16[32,1024]{1,0:T(8,128)(2,1)S(1)}, u32[]{:S(2)}, u32[]{:S(2)}) collective-permute-start(bf16[32,1024]{1,0:T(8,128)(2,1)S(1)} %get-tuple-element.36), channel_id=1, source_target_pairs={{0,8},{8,0},{16,24},{24,16},{1,9},{9,1},{17,25},{25,17},{2,10},{10... | collective-permute-start | bytes 196616 | tf_op jit(solution)/shard_map/ppermute | solution.py:440
  51.6 5.0 %collective-permute-start.18 = (bf16[32,1024]{1,0:T(8,128)(2,1)S(1)}, bf16[32,1024]{1,0:T(8,128)(2,1)S(1)}, u32[]{:S(2)}, u32[]{:S(2)}) collective-permute-start(bf16[32,1024]{1,0:T(8,128)(2,1)S(1)} %get-tuple-element.37), channel_id=1, source_target_pairs={{0,16},{8,24},{16,0},{24,8},{1,17},{9,25},{17,1},{25,9},{2,18},{10... | collective-permute-start | bytes 196616 | tf_op jit(solution)/shard_map/ppermute | solution.py:440
  52.2 5.2 %collective-permute-start.19 = (bf16[32,1024]{1,0:T(8,128)(2,1)S(1)}, bf16[32,1024]{1,0:T(8,128)(2,1)S(1)}, u32[]{:S(2)}, u32[]{:S(2)}) collective-permute-start(bf16[32,1024]{1,0:T(8,128)(2,1)S(1)} %get-tuple-element.38), channel_id=1, source_target_pairs={{0,24},{8,16},{16,8},{24,0},{1,25},{9,17},{17,9},{25,1},{2,26},{10... | collective-permute-start | bytes 196616 | tf_op jit(solution)/shard_map/ppermute | solution.py:440
  57.4 9.8 %collective-permute-start.20 = (bf16[32,1024]{1,0:T(8,128)(2,1)S(1)}, bf16[32,1024]{1,0:T(8,128)(2,1)S(1)}, u32[]{:S(2)}, u32[]{:S(2)}) collective-permute-start(bf16[32,1024]{1,0:T(8,128)(2,1)S(1)} %get-tuple-element.40), channel_id=1, source_target_pairs={{0,2},{1,3},{2,0},{3,1},{4,6},{5,7},{6,4},{7,5},{8,10},{9,11},{10,... | collective-permute-start | bytes 196616 | tf_op jit(solution)/shard_map/ppermute | solution.py:443
  62.3 8.6 %collective-permute-start.13 = (bf16[256,256]{1,0:T(8,128)(2,1)S(1)}, bf16[256,256]{1,0:T(8,128)(2,1)S(1)}, u32[]{:S(2)}, u32[]{:S(2)}) collective-permute-start(bf16[256,256]{1,0:T(8,128)(2,1)S(1)} %sum_rows.1.refs_2_), channel_id=1, source_target_pairs={{0,8},{8,0},{16,24},{24,16},{1,9},{9,1},{17,25},{25,17},{2,10},{10... | collective-permute-start | bytes 393224 | tf_op jit(solution)/shard_map/ppermute | solution.py:440
  64.3 6.6 %collective-permute-start.21 = (bf16[32,1024]{1,0:T(8,128)(2,1)S(1)}, bf16[32,1024]{1,0:T(8,128)(2,1)S(1)}, u32[]{:S(2)}, u32[]{:S(2)}) collective-permute-start(bf16[32,1024]{1,0:T(8,128)(2,1)S(1)} %get-tuple-element.41), channel_id=1, source_target_pairs={{0,4},{1,5},{2,6},{3,7},{4,0},{5,1},{6,2},{7,3},{8,12},{9,13},{10,... | collective-permute-start | bytes 196616 | tf_op jit(solution)/shard_map/ppermute | solution.py:443
  64.3 6.6 %collective-permute-start.22 = (bf16[32,1024]{1,0:T(8,128)(2,1)S(1)}, bf16[32,1024]{1,0:T(8,128)(2,1)S(1)}, u32[]{:S(2)}, u32[]{:S(2)}) collective-permute-start(bf16[32,1024]{1,0:T(8,128)(2,1)S(1)} %get-tuple-element.42), channel_id=1, source_target_pairs={{0,6},{1,7},{2,4},{3,5},{4,2},{5,3},{6,0},{7,1},{8,14},{9,15},{10,... | collective-permute-start | bytes 196616 | tf_op jit(solution)/shard_map/ppermute | solution.py:443
  65.8 8.7 %collective-permute-start.15 = (bf16[256,256]{1,0:T(8,128)(2,1)S(1)}, bf16[256,256]{1,0:T(8,128)(2,1)S(1)}, u32[]{:S(2)}, u32[]{:S(2)}) collective-permute-start(bf16[256,256]{1,0:T(8,128)(2,1)S(1)} %sum_rows.1.refs_2_), channel_id=1, source_target_pairs={{0,24},{8,16},{16,8},{24,0},{1,25},{9,17},{17,9},{25,1},{2,26},{10... | collective-permute-start | bytes 393224 | tf_op jit(solution)/shard_map/ppermute | solution.py:440
  67.3 7.7 %collective-permute-start.14 = (bf16[256,256]{1,0:T(8,128)(2,1)S(1)}, bf16[256,256]{1,0:T(8,128)(2,1)S(1)}, u32[]{:S(2)}, u32[]{:S(2)}) collective-permute-start(bf16[256,256]{1,0:T(8,128)(2,1)S(1)} %sum_rows.1.refs_2_), channel_id=1, source_target_pairs={{0,16},{8,24},{16,0},{24,8},{1,17},{9,25},{17,1},{25,9},{2,18},{10... | collective-permute-start | bytes 393224 | tf_op jit(solution)/shard_map/ppermute | solution.py:440
  70.9 4.1 %copy-start.7 = (f32[256]{0:T(256)S(1)}, f32[256]{0:T(256)}, u32[]{:S(2)}) copy-start(f32[256]{0:T(256)} %param.10) | copy-start | bytes 3076
  70.9 5.3 %collective-permute-start.25 = (bf16[32,1024]{1,0:T(8,128)(2,1)S(1)}, bf16[32,1024]{1,0:T(8,128)(2,1)S(1)}, u32[]{:S(2)}, u32[]{:S(2)}) collective-permute-start(bf16[32,1024]{1,0:T(8,128)(2,1)S(1)} %sum_parts.1.refs_0_), channel_id=1, source_target_pairs={{0,24},{8,16},{16,8},{24,0},{1,25},{9,17},{17,9},{25,1},{2,26},{10... | collective-permute-start | bytes 196616 | tf_op jit(solution)/shard_map/ppermute | solution.py:440
  72.5 4.4 %collective-permute-start.24 = (bf16[32,1024]{1,0:T(8,128)(2,1)S(1)}, bf16[32,1024]{1,0:T(8,128)(2,1)S(1)}, u32[]{:S(2)}, u32[]{:S(2)}) collective-permute-start(bf16[32,1024]{1,0:T(8,128)(2,1)S(1)} %sum_parts.1.refs_0_), channel_id=1, source_target_pairs={{0,16},{8,24},{16,0},{24,8},{1,17},{9,25},{17,1},{25,9},{2,18},{10... | collective-permute-start | bytes 196616 | tf_op jit(solution)/shard_map/ppermute | solution.py:440
  72.7 4.3 %collective-permute-start.23 = (bf16[32,1024]{1,0:T(8,128)(2,1)S(1)}, bf16[32,1024]{1,0:T(8,128)(2,1)S(1)}, u32[]{:S(2)}, u32[]{:S(2)}) collective-permute-start(bf16[32,1024]{1,0:T(8,128)(2,1)S(1)} %sum_parts.1.refs_0_), channel_id=1, source_target_pairs={{0,8},{8,0},{16,24},{24,16},{1,9},{9,1},{17,25},{25,17},{2,10},{10... | collective-permute-start | bytes 196616 | tf_op jit(solution)/shard_map/ppermute | solution.py:440

commit v5 on v4

--- a/solution.py
+++ b/solution.py
@@ -10,6 +10,8 @@
 HEADS = 8
 MAXLEN = 128
 PASS_COST = 12 * 10**9
+PARTS_COST = 4 * 10**9
+UPDATE_COST = 8 * 10**9
 GATE_COST = 8 * 10**9
 EXTRA = 16
 VMEM = pl.BlockSpec(memory_space=pltpu.VMEM)
@@ -563,17 +565,28 @@
 
     grad = call(sum_first_kernel, "sum_rows", sds((rows, cols)), (sums,))
     grads = [column(grad, m) for m in range(n)]
-    wsum = call(sum_kernel, "sum_parts", sds((part, width)), wparts, after=(grads[1],))
+    there = call(
+        gate_kernel,
+        "gate_parts",
+        sds((8, 128), F32),
+        (),
+        after=tuple(wparts[1:]),
+        cost=PARTS_COST,
+    )
+    wsum = call(sum_kernel, "sum_parts", sds((part, width)), wparts, after=(grad, there))
     wsums = [column(wsum, m) for m in range(n)]
     new_table, new_accum = call(
         update_kernel,
         "update",
         [sds((rows, width), F32), sds((1, rows), F32)],
         (table, accum.reshape(1, rows), *grads),
+        cost=UPDATE_COST,
         placed=True,
         scratch=[pltpu.VMEM((rows, width), F32)],
     )
-    weight_grad = call(place_kernel, "place", sds((n * part, width)), wsums, placed=True)
+    weight_grad = call(
+        place_kernel, "place", sds((n * part, width)), wsums, after=(new_accum,), placed=True
+    )
     return (new_table, new_accum.reshape(rows), weight_grad)
 
 

time: 77.9 us -> 76.5 us (0.982)
  waiting for transfers between devices: 23.5 us -> 19.4 us
  starting transfers between devices: 39.1 us -> 41.7 us
    ppermute x6, waiting for transfers between devices: 9.82 us -> 6.42 us  [along(): lax.ppermute(x, 'shard', [(i, i ^ 2 * m) for i in range(shards)])]
    ppermute x16, starting transfers between devices: 22.1 us -> 23.7 us  [column(): lax.ppermute(x, 'replica', [(i, i ^ m) for i in range(n)])]
    all_to_all x1, waiting for transfers between devices: 2.75 us -> 1.7 us  [swap_along(): lax.all_to_all(x, 'shard', 0, 0, tiled=True, axis_index_groups=groups)]
    ppermute x6, starting transfers between devices: 8 us -> 8.99 us  [along(): lax.ppermute(x, 'shard', [(i, i ^ 2 * m) for i in range(shards)])]
    pallas_call x19 -> x20, Pallas kernels: 13.5 us -> 13.5 us  [call(): pl.pallas_call(run, out_shape=out, in_specs=[SMEM if i < smem else HBM if...]
  transfers between devices with their start and end apart: 28 -> 28, of which waited for: 15 -> 17; matrix products, arithmetic and copies ran while one was open for 0% -> 0% of each run, Pallas kernels for 13% -> 13%
where the time goes in v5:
time: 76.5 us; the launch traced here: 76.2 us
  starting transfers between devices  41.7 us (55%)
  waiting for transfers between devices  19.4 us (25%)
  Pallas kernels  13.5 us (18%)
  between operations  0.89 us (1%)
    ppermute x16, starting transfers between devices, column(): lax.ppermute(x, 'replica', [(i, i ^ m) for i in range(n)])  23.7 us
    pallas_call x20, Pallas kernels, call(): pl.pallas_call(run, out_shape=out, in_specs=[SMEM if i < smem else HBM if...  13.5 us
    ppermute x16, waiting for transfers between devices, column(): lax.ppermute(x, 'replica', [(i, i ^ m) for i in range(n)])  9.01 us
    ppermute x6, starting transfers between devices, along(): lax.ppermute(x, 'shard', [(i, i ^ 2 * m) for i in range(shards)])  8.99 us
    ppermute x6, waiting for transfers between devices, along(): lax.ppermute(x, 'shard', [(i, i ^ 2 * m) for i in range(shards)])  6.42 us
    all_to_all x1, starting transfers between devices, swap_along(): lax.all_to_all(x, 'shard', 0, 0, tiled=True, axis_index_groups=groups)  4.79 us
    all_to_all x1, starting transfers between devices, swap_columns(): return lax.all_to_all(x, 'replica', 0, 0, tiled=True)  3.49 us
    ppermute x4, waiting for transfers between devices, core(): return lax.ppermute(x, 'shard', [(i, i ^ 1) for i in range(shards)])  2.28 us
  transfers between devices with their start and end apart: 28, of which 17 were waited for; matrix products, arithmetic and copies ran while one was open for 0% of the time, Pallas kernels for 13%

profile of v5, /device:TPU:0, one launch (start us, length us, event | category | flops | bytes accessed | tf_op | source)
XLA Modules:
  0.0 76.2 jit_solution(15472498248457566171)
XLA Ops:
  0.7 3.0 %collective-permute-start.8 = (bf16[256,1024]{1,0:T(8,128)(2,1)}, bf16[256,1024]{1,0:T(8,128)(2,1)S(1)}, u32[]{:S(2)}, u32[]{:S(2)}) collective-permute-start(bf16[256,1024]{1,0:T(8,128)(2,1)} %refs_1_.3), channel_id=1, source_target_pairs={{0,16},{8,24},{16,0},{24,8},{1,17},{9,25},{17,1},{25,9},{2,18},{10... | collective-permute-start | bytes 1572872 | tf_op jit(solution)/shard_map/ppermute | solution.py:442
  3.7 1.5 %collective-permute-start.7 = (bf16[256,1024]{1,0:T(8,128)(2,1)}, bf16[256,1024]{1,0:T(8,128)(2,1)S(1)}, u32[]{:S(2)}, u32[]{:S(2)}) collective-permute-start(bf16[256,1024]{1,0:T(8,128)(2,1)} %refs_1_.3), channel_id=1, source_target_pairs={{0,8},{8,0},{16,24},{24,16},{1,9},{9,1},{17,25},{25,17},{2,10},{10... | collective-permute-start | bytes 1572872 | tf_op jit(solution)/shard_map/ppermute | solution.py:442
  5.2 1.8 %carry.1.refs_0_ = bf16[384,256]{1,0:T(8,128)(2,1)} custom-call(bf16[128,1024]{1,0:T(8,128)(2,1)} %refs_0_.4, f32[256,1024]{1,0:T(8,128)} %refs_0_.5), custom_call_target="tpu_custom_call" | custom-call | tf_op jit(solution)/shard_map/carry/pallas_call | solution.py:169
  6.9 3.7 %collective-permute-start.2 = (bf16[384,256]{1,0:T(8,128)(2,1)}, bf16[384,256]{1,0:T(8,128)(2,1)S(1)}, u32[]{:S(2)}, u32[]{:S(2)}) collective-permute-start(bf16[384,256]{1,0:T(8,128)(2,1)} %carry.1.refs_0_), channel_id=1, source_target_pairs={{0,6},{1,7},{2,4},{3,5},{4,2},{5,3},{6,0},{7,1},{8,14},{9,15},{10,... | collective-permute-start | bytes 589832 | tf_op jit(solution)/shard_map/ppermute | solution.py:445
  10.6 0.8 %collective-permute-start = (bf16[384,256]{1,0:T(8,128)(2,1)}, bf16[384,256]{1,0:T(8,128)(2,1)S(1)}, u32[]{:S(2)}, u32[]{:S(2)}) collective-permute-start(bf16[384,256]{1,0:T(8,128)(2,1)} %carry.1.refs_0_), channel_id=1, source_target_pairs={{0,2},{1,3},{2,0},{3,1},{4,6},{5,7},{6,4},{7,5},{8,10},{9,11},{10,... | collective-permute-start | bytes 589832 | tf_op jit(solution)/shard_map/ppermute | solution.py:445
  11.4 0.7 copy-done.6
  12.1 1.4 %pack.1 = bf16[4,544,128]{2,1,0:T(8,128)(2,1)} custom-call(s32[1,4]{1,0:T(1,128)S(1)} %copy-done.8, s32[1,256]{1,0:T(1,128)S(1)} %bitcast.5, s32[1,256]{1,0:T(1,128)S(1)} %bitcast.6, bf16[256,512]{1,0:T(8,128)(2,1)S(1)} %copy-done.3, bf16[256,512]{1,0:T(8,128)(2,1)S(1)} %copy-done.4), custom_call_target="tpu_custom_call" | custom-call | tf_op jit(solution)/shard_map/pack/pallas_call | solution.py:169
  13.5 3.5 %all-to-all-start = ((bf16[4,544,128]{2,1,0:T(8,128)(2,1)}), bf16[4,544,128]{2,1,0:T(8,128)(2,1)S(1)}, u32[]{:S(2)}, u32[]{:S(2)}) async-start(bf16[4,544,128]{2,1,0:T(8,128)(2,1)} %pack.1), calls=%async_computation | async-start | bytes 1114112 | tf_op jit(solution)/shard_map/all_to_all | solution.py:455
  17.0 0.2 collective-permute-done.7.refs_0_.refs_5_.refs_2_
  17.3 1.8 %collective-permute-start.10 = (bf16[128,1024]{1,0:T(8,128)(2,1)S(1)}, bf16[128,1024]{1,0:T(8,128)(2,1)S(1)}, u32[]{:S(2)}, u32[]{:S(2)}) collective-permute-start(bf16[128,1024]{1,0:T(8,128)(2,1)S(1)} %get-tuple-element.28), channel_id=1, source_target_pairs={{0,16},{8,24},{16,0},{24,8},{1,17},{9,25},{17,1},{25,9},{2,18},{10... | collective-permute-start | bytes 786440 | tf_op jit(solution)/shard_map/ppermute | solution.py:442
  19.1 1.5 %collective-permute-start.9 = (bf16[128,1024]{1,0:T(8,128)(2,1)S(1)}, bf16[128,1024]{1,0:T(8,128)(2,1)S(1)}, u32[]{:S(2)}, u32[]{:S(2)}) collective-permute-start(bf16[128,1024]{1,0:T(8,128)(2,1)S(1)} %get-tuple-element.27.refs_1_), channel_id=1, source_target_pairs={{0,8},{8,0},{16,24},{24,16},{1,9},{9,1},{17,25},{25,17},{2,10},{10... | collective-permute-start | bytes 786440 | tf_op jit(solution)/shard_map/ppermute | solution.py:442
  20.6 6.3 %collective-permute-done.1.refs_2_ = bf16[384,256]{1,0:T(8,128)(2,1)S(1)} collective-permute-done((bf16[384,256]{1,0:T(8,128)(2,1)}, bf16[384,256]{1,0:T(8,128)(2,1)S(1)}, u32[]{:S(2)}, u32[]{:S(2)}) %collective-permute-start.1) | collective-permute-done | bytes 196640 | tf_op jit(solution)/shard_map/ppermute | solution.py:445
  27.0 1.4 %collective-permute-start.3 = (bf16[128,256]{1,0:T(8,128)(2,1)S(1)}, bf16[128,256]{1,0:T(8,128)(2,1)S(1)}, u32[]{:S(2)}, u32[]{:S(2)}) collective-permute-start(bf16[128,256]{1,0:T(8,128)(2,1)S(1)} %get-tuple-element.24), channel_id=1, source_target_pairs={{0,8},{8,0},{16,24},{24,16},{1,9},{9,1},{17,25},{25,17},{2,10},{10... | collective-permute-start | bytes 196616 | tf_op jit(solution)/shard_map/ppermute | solution.py:442
  28.4 2.1 %collective-permute-start.5 = (bf16[128,256]{1,0:T(8,128)(2,1)S(1)}, bf16[128,256]{1,0:T(8,128)(2,1)S(1)}, u32[]{:S(2)}, u32[]{:S(2)}) collective-permute-start(bf16[128,256]{1,0:T(8,128)(2,1)S(1)} %get-tuple-element.26), channel_id=1, source_target_pairs={{0,24},{8,16},{16,8},{24,0},{1,25},{9,17},{17,9},{25,1},{2,26},{10... | collective-permute-start | bytes 196616 | tf_op jit(solution)/shard_map/ppermute | solution.py:442
  30.6 1.5 %collective-permute-done.3.refs_1_ = bf16[128,256]{1,0:T(8,128)(2,1)S(1)} collective-permute-done((bf16[128,256]{1,0:T(8,128)(2,1)S(1)}, bf16[128,256]{1,0:T(8,128)(2,1)S(1)}, u32[]{:S(2)}, u32[]{:S(2)}) %collective-permute-start.3) | collective-permute-done | bytes 65568 | tf_op jit(solution)/shard_map/ppermute | solution.py:442
  32.1 0.6 collective-permute-done.4.refs_2_
  32.7 1.0 %collective-permute-done.5.refs_3_ = bf16[128,256]{1,0:T(8,128)(2,1)S(1)} collective-permute-done((bf16[128,256]{1,0:T(8,128)(2,1)S(1)}, bf16[128,256]{1,0:T(8,128)(2,1)S(1)}, u32[]{:S(2)}, u32[]{:S(2)}) %collective-permute-start.5) | collective-permute-done | bytes 65568 | tf_op jit(solution)/shard_map/ppermute | solution.py:442
  33.8 0.8 %weights.1.refs_1_.refs_3_ = bf16[4,2,256,256]{3,2,1,0:T(8,128)(2,1)S(1)} custom-call(bf16[4,544,128]{2,1,0:T(8,128)(2,1)S(1)} %all-to-all-done.refs_4_.refs_0_, bf16[128,1024]{1,0:T(8,128)(2,1)S(1)} %get-tuple-element.27.refs_1_), custom_call_target="tpu_custom_call" | custom-call | tf_op jit(solution)/shard_map/weights/pallas_call | solution.py:169
  34.7 2.8 %mix.1.refs_10_.refs_0_ = bf16[256,1024]{1,0:T(8,128)(2,1)S(1)} custom-call(bf16[4,544,128]{2,1,0:T(8,128)(2,1)S(1)} %all-to-all-done.refs_4_.refs_0_, bf16[4,2,256,256]{3,2,1,0:T(8,128)(2,1)S(1)} %weights.1.refs_1_.refs_3_, bf16[4,256,256]{2,1,0:T(8,128)(2,1)S(1)} %stack.1.refs_2_, bf16[4,256,256]{2,1,0:T(8,128)(2,1)S(1)} %collective-permute-done.11.refs_3_), custom_call_target="tpu_custom_call" | custom-call | tf_op jit(solution)/shard_map/mix/pallas_call | solution.py:169
  37.5 1.8 %back.1 = (bf16[4,256,256]{2,1,0:T(8,128)(2,1)S(1)}, bf16[1024,256]{1,0:T(8,128)(2,1)S(1)}) custom-call(bf16[4,544,128]{2,1,0:T(8,128)(2,1)S(1)} %all-to-all-done.refs_4_.refs_0_, bf16[128,1024]{1,0:T(8,128)(2,1)S(1)} %join.1.refs_1_, bf16[128,1024]{1,0:T(8,128)(2,1)S(1)} %collective-permute-done.6.refs_2_, ...), custom_call_target="tpu_custom_call" | custom-call | tf_op jit(solution)/shard_map/back/pallas_call | solution.py:169
  39.4 0.6 collective-permute-start.12
  39.9 0.7 keep.1.refs_0_
  40.6 0.8 %collective-permute-done.12.refs_1_ = bf16[4,256,256]{2,1,0:T(8,128)(2,1)S(1)} collective-permute-done((bf16[4,256,256]{2,1,0:T(8,128)(2,1)S(1)}, bf16[4,256,256]{2,1,0:T(8,128)(2,1)S(1)}, u32[]{:S(2)}, u32[]{:S(2)}) %collective-permute-start.12) | collective-permute-done | bytes 524320 | tf_op jit(solution)/shard_map/ppermute | solution.py:448
  41.5 0.9 %add.1.refs_6_ = bf16[4,256,256]{2,1,0:T(8,128)(2,1)} custom-call(f32[4,256,256]{2,1,0:T(8,128)S(1)} %keep.1.refs_0_, bf16[4,256,256]{2,1,0:T(8,128)(2,1)S(1)} %collective-permute-done.12.refs_1_), custom_call_target="tpu_custom_call" | custom-call | tf_op jit(solution)/shard_map/add/pallas_call | solution.py:169
  42.3 4.8 %all-to-all-start.1 = ((bf16[4,256,256]{2,1,0:T(8,128)(2,1)}), bf16[4,256,256]{2,1,0:T(8,128)(2,1)S(1)}, u32[]{:S(2)}, u32[]{:S(2)}) async-start(bf16[4,256,256]{2,1,0:T(8,128)(2,1)} %add.1.refs_6_), calls=%async_computation.1 | async-start | bytes 1048576 | tf_op jit(solution)/shard_map/all_to_all | solution.py:452
  47.1 0.8 %wgrad.1 = (f32[128,1024]{1,0:T(8,128)S(1)}, bf16[128,1024]{1,0:T(8,128)(2,1)S(1)}) custom-call(bf16[256,1024]{1,0:T(8,128)(2,1)S(1)} %mix.1.refs_10_.refs_0_, bf16[256,1024]{1,0:T(8,128)(2,1)S(1)} %copy-done, bf16[256,1024]{1,0:T(8,128)(2,1)S(1)} %collective-permute-done.7.refs_0_.refs_5_.refs_2_, ...), custom_call_target="tpu_custom_call" | custom-call | tf_op jit(solution)/shard_map/wgrad/pallas_call | solution.py:169
  48.0 0.1 collective-permute-start.16
  48.1 1.5 %collective-permute-done.16.refs_1_ = bf16[128,1024]{1,0:T(8,128)(2,1)S(1)} collective-permute-done((bf16[128,1024]{1,0:T(8,128)(2,1)S(1)}, bf16[128,1024]{1,0:T(8,128)(2,1)S(1)}, u32[]{:S(2)}, u32[]{:S(2)}) %collective-permute-start.16) | collective-permute-done | bytes 262176 | tf_op jit(solution)/shard_map/ppermute | solution.py:448
  49.6 2.0 %collective-permute-start.17 = (bf16[32,1024]{1,0:T(8,128)(2,1)S(1)}, bf16[32,1024]{1,0:T(8,128)(2,1)S(1)}, u32[]{:S(2)}, u32[]{:S(2)}) collective-permute-start(bf16[32,1024]{1,0:T(8,128)(2,1)S(1)} %get-tuple-element.36), channel_id=1, source_target_pairs={{0,8},{8,0},{16,24},{24,16},{1,9},{9,1},{17,25},{25,17},{2,10},{10... | collective-permute-start | bytes 196616 | tf_op jit(solution)/shard_map/ppermute | solution.py:442
  51.6 0.6 collective-permute-start.18
  52.2 1.0 %collective-permute-start.19 = (bf16[32,1024]{1,0:T(8,128)(2,1)S(1)}, bf16[32,1024]{1,0:T(8,128)(2,1)S(1)}, u32[]{:S(2)}, u32[]{:S(2)}) collective-permute-start(bf16[32,1024]{1,0:T(8,128)(2,1)S(1)} %get-tuple-element.38), channel_id=1, source_target_pairs={{0,24},{8,16},{16,8},{24,0},{1,25},{9,17},{17,9},{25,1},{2,26},{10... | collective-permute-start | bytes 196616 | tf_op jit(solution)/shard_map/ppermute | solution.py:442
  53.2 0.8 %collective-permute-done.17.refs_1_ = bf16[32,1024]{1,0:T(8,128)(2,1)S(1)} collective-permute-done((bf16[32,1024]{1,0:T(8,128)(2,1)S(1)}, bf16[32,1024]{1,0:T(8,128)(2,1)S(1)}, u32[]{:S(2)}, u32[]{:S(2)}) %collective-permute-start.17) | collective-permute-done | bytes 65568 | tf_op jit(solution)/shard_map/ppermute | solution.py:442
  54.0 2.6 %collective-permute-done.18.refs_2_ = bf16[32,1024]{1,0:T(8,128)(2,1)S(1)} collective-permute-done((bf16[32,1024]{1,0:T(8,128)(2,1)S(1)}, bf16[32,1024]{1,0:T(8,128)(2,1)S(1)}, u32[]{:S(2)}, u32[]{:S(2)}) %collective-permute-start.18) | collective-permute-done | bytes 65568 | tf_op jit(solution)/shard_map/ppermute | solution.py:442
  56.6 0.8 collective-permute-done.19.refs_3_
  57.4 2.1 %collective-permute-start.20 = (bf16[32,1024]{1,0:T(8,128)(2,1)S(1)}, bf16[32,1024]{1,0:T(8,128)(2,1)S(1)}, u32[]{:S(2)}, u32[]{:S(2)}) collective-permute-start(bf16[32,1024]{1,0:T(8,128)(2,1)S(1)} %get-tuple-element.40), channel_id=1, source_target_pairs={{0,2},{1,3},{2,0},{3,1},{4,6},{5,7},{6,4},{7,5},{8,10},{9,11},{10,... | collective-permute-start | bytes 196616 | tf_op jit(solution)/shard_map/ppermute | solution.py:445
  59.5 2.4 %collective-permute-start.21 = (bf16[32,1024]{1,0:T(8,128)(2,1)S(1)}, bf16[32,1024]{1,0:T(8,128)(2,1)S(1)}, u32[]{:S(2)}, u32[]{:S(2)}) collective-permute-start(bf16[32,1024]{1,0:T(8,128)(2,1)S(1)} %get-tuple-element.41), channel_id=1, source_target_pairs={{0,4},{1,5},{2,6},{3,7},{4,0},{5,1},{6,2},{7,3},{8,12},{9,13},{10,... | collective-permute-start | bytes 196616 | tf_op jit(solution)/shard_map/ppermute | solution.py:445
  61.9 1.7 %all-to-all-done.1.refs_0_ = bf16[4,256,256]{2,1,0:T(8,128)(2,1)S(1)} async-done(((bf16[4,256,256]{2,1,0:T(8,128)(2,1)}), bf16[4,256,256]{2,1,0:T(8,128)(2,1)S(1)}, u32[]{:S(2)}, u32[]{:S(2)}) %all-to-all-start.1) | async-done | bytes 524320 | tf_op jit(solution)/shard_map/all_to_all | solution.py:452
  63.7 3.5 %collective-permute-start.15 = (bf16[256,256]{1,0:T(8,128)(2,1)S(1)}, bf16[256,256]{1,0:T(8,128)(2,1)S(1)}, u32[]{:S(2)}, u32[]{:S(2)}) collective-permute-start(bf16[256,256]{1,0:T(8,128)(2,1)S(1)} %sum_rows.1.refs_2_.refs_4_), channel_id=1, source_target_pairs={{0,24},{8,16},{16,8},{24,0},{1,25},{9,17},{17,9},{25,1},{2,26},{10... | collective-permute-start | bytes 393224 | tf_op jit(solution)/shard_map/ppermute | solution.py:442
  67.3 0.6 collective-permute-start.13
  68.0 2.8 %collective-permute-start.25 = (bf16[32,1024]{1,0:T(8,128)(2,1)S(1)}, bf16[32,1024]{1,0:T(8,128)(2,1)S(1)}, u32[]{:S(2)}, u32[]{:S(2)}) collective-permute-start(bf16[32,1024]{1,0:T(8,128)(2,1)S(1)} %sum_parts.1.refs_0_), channel_id=1, source_target_pairs={{0,24},{8,16},{16,8},{24,0},{1,25},{9,17},{17,9},{25,1},{2,26},{10... | collective-permute-start | bytes 196616 | tf_op jit(solution)/shard_map/ppermute | solution.py:442
  70.8 0.2 collective-permute-start.24
  71.1 0.1 collective-permute-done.15.refs_5_
  71.2 1.5 %collective-permute-start.23 = (bf16[32,1024]{1,0:T(8,128)(2,1)S(1)}, bf16[32,1024]{1,0:T(8,128)(2,1)S(1)}, u32[]{:S(2)}, u32[]{:S(2)}) collective-permute-start(bf16[32,1024]{1,0:T(8,128)(2,1)S(1)} %sum_parts.1.refs_0_), channel_id=1, source_target_pairs={{0,8},{8,0},{16,24},{24,16},{1,9},{9,1},{17,25},{25,17},{2,10},{10... | collective-permute-start | bytes 196616 | tf_op jit(solution)/shard_map/ppermute | solution.py:442
  72.8 0.2 collective-permute-done.14.refs_4_
  73.0 1.3 %update.1 = (f32[256,1024]{1,0:T(8,128)}, f32[1,256]{1,0:T(1,128)}) custom-call(f32[256,1024]{1,0:T(8,128)S(1)} %copy-done.2, f32[1,256]{1,0:T(1,128)S(1)} %bitcast.7, bf16[256,256]{1,0:T(8,128)(2,1)S(1)} %sum_rows.1.refs_2_.refs_4_, bf16[256,256]{1,0:T(8,128)(2,1)S(1)} %collective-permute-done.13.refs_3_, ...), custom_call_target="tpu_custom_call" | custom-call | flops 8000000000 | tf_op jit(solution)/shard_map/update/pallas_call | solution.py:169
  74.4 0.7 collective-permute-done.24.refs_2_
  75.1 0.4 collective-permute-done.23.refs_1_
  75.5 0.7 place.1
  (48 shorter events, 0.8 us)
Async XLA Ops:
  0.6 10.8 %copy-start.4 = (bf16[256,512]{1,0:T(8,128)(2,1)S(1)}, bf16[256,512]{1,0:T(8,128)(2,1)}, u32[]{:S(2)}) copy-start(bf16[256,512]{1,0:T(8,128)(2,1)} %refs_4_.2) | copy-start | bytes 786436
  0.6 10.8 %copy-start.3 = (bf16[256,512]{1,0:T(8,128)(2,1)S(1)}, bf16[256,512]{1,0:T(8,128)(2,1)}, u32[]{:S(2)}) copy-start(bf16[256,512]{1,0:T(8,128)(2,1)} %refs_3_.1) | copy-start | bytes 786436
  0.7 16.4 %collective-permute-start.8 = (bf16[256,1024]{1,0:T(8,128)(2,1)}, bf16[256,1024]{1,0:T(8,128)(2,1)S(1)}, u32[]{:S(2)}, u32[]{:S(2)}) collective-permute-start(bf16[256,1024]{1,0:T(8,128)(2,1)} %refs_1_.3), channel_id=1, source_target_pairs={{0,16},{8,24},{16,0},{24,8},{1,17},{9,25},{17,1},{25,9},{2,18},{10... | collective-permute-start | bytes 1572872 | tf_op jit(solution)/shard_map/ppermute | solution.py:442
  3.7 13.6 %collective-permute-start.7 = (bf16[256,1024]{1,0:T(8,128)(2,1)}, bf16[256,1024]{1,0:T(8,128)(2,1)S(1)}, u32[]{:S(2)}, u32[]{:S(2)}) collective-permute-start(bf16[256,1024]{1,0:T(8,128)(2,1)} %refs_1_.3), channel_id=1, source_target_pairs={{0,8},{8,0},{16,24},{24,16},{1,9},{9,1},{17,25},{25,17},{2,10},{10... | collective-permute-start | bytes 1572872 | tf_op jit(solution)/shard_map/ppermute | solution.py:442
  5.2 6.2 %copy-start.7 = (s32[256]{0:T(256)S(1)}, s32[256]{0:T(256)}, u32[]{:S(2)}) copy-start(s32[256]{0:T(256)} %param.12) | copy-start | bytes 3076
  6.9 13.7 %collective-permute-start.2 = (bf16[384,256]{1,0:T(8,128)(2,1)}, bf16[384,256]{1,0:T(8,128)(2,1)S(1)}, u32[]{:S(2)}, u32[]{:S(2)}) collective-permute-start(bf16[384,256]{1,0:T(8,128)(2,1)} %carry.1.refs_0_), channel_id=1, source_target_pairs={{0,6},{1,7},{2,4},{3,5},{4,2},{5,3},{6,0},{7,1},{8,14},{9,15},{10,... | collective-permute-start | bytes 589832 | tf_op jit(solution)/shard_map/ppermute | solution.py:445
  10.6 16.3 %collective-permute-start.1 = (bf16[384,256]{1,0:T(8,128)(2,1)}, bf16[384,256]{1,0:T(8,128)(2,1)S(1)}, u32[]{:S(2)}, u32[]{:S(2)}) collective-permute-start(bf16[384,256]{1,0:T(8,128)(2,1)} %carry.1.refs_0_), channel_id=1, source_target_pairs={{0,4},{1,5},{2,6},{3,7},{4,0},{5,1},{6,2},{7,3},{8,12},{9,13},{10,... | collective-permute-start | bytes 589832 | tf_op jit(solution)/shard_map/ppermute | solution.py:445
  10.6 16.3 %collective-permute-start = (bf16[384,256]{1,0:T(8,128)(2,1)}, bf16[384,256]{1,0:T(8,128)(2,1)S(1)}, u32[]{:S(2)}, u32[]{:S(2)}) collective-permute-start(bf16[384,256]{1,0:T(8,128)(2,1)} %carry.1.refs_0_), channel_id=1, source_target_pairs={{0,2},{1,3},{2,0},{3,1},{4,6},{5,7},{6,4},{7,5},{8,10},{9,11},{10,... | collective-permute-start | bytes 589832 | tf_op jit(solution)/shard_map/ppermute | solution.py:445
  11.4 0.7 copy-start.6
  11.4 0.7 copy-start.8
  13.5 13.4 %all-to-all-start = ((bf16[4,544,128]{2,1,0:T(8,128)(2,1)}), bf16[4,544,128]{2,1,0:T(8,128)(2,1)S(1)}, u32[]{:S(2)}, u32[]{:S(2)}) async-start(bf16[4,544,128]{2,1,0:T(8,128)(2,1)} %pack.1), calls=%async_computation | async-start | bytes 1114112 | tf_op jit(solution)/shard_map/all_to_all | solution.py:455
  17.0 9.9 %copy-start.1 = (bf16[384,256]{1,0:T(8,128)(2,1)S(1)}, bf16[384,256]{1,0:T(8,128)(2,1)}, u32[]{:S(2)}) copy-start(bf16[384,256]{1,0:T(8,128)(2,1)} %carry.1.refs_0_) | copy-start | bytes 589828
  17.3 17.3 %collective-permute-start.10 = (bf16[128,1024]{1,0:T(8,128)(2,1)S(1)}, bf16[128,1024]{1,0:T(8,128)(2,1)S(1)}, u32[]{:S(2)}, u32[]{:S(2)}) collective-permute-start(bf16[128,1024]{1,0:T(8,128)(2,1)S(1)} %get-tuple-element.28), channel_id=1, source_target_pairs={{0,16},{8,24},{16,0},{24,8},{1,17},{9,25},{17,1},{25,9},{2,18},{10... | collective-permute-start | bytes 786440 | tf_op jit(solution)/shard_map/ppermute | solution.py:442
  19.1 15.5 %collective-permute-start.9 = (bf16[128,1024]{1,0:T(8,128)(2,1)S(1)}, bf16[128,1024]{1,0:T(8,128)(2,1)S(1)}, u32[]{:S(2)}, u32[]{:S(2)}) collective-permute-start(bf16[128,1024]{1,0:T(8,128)(2,1)S(1)} %get-tuple-element.27.refs_1_), channel_id=1, source_target_pairs={{0,8},{8,0},{16,24},{24,16},{1,9},{9,1},{17,25},{25,17},{2,10},{10... | collective-permute-start | bytes 786440 | tf_op jit(solution)/shard_map/ppermute | solution.py:442
  27.0 5.1 %collective-permute-start.3 = (bf16[128,256]{1,0:T(8,128)(2,1)S(1)}, bf16[128,256]{1,0:T(8,128)(2,1)S(1)}, u32[]{:S(2)}, u32[]{:S(2)}) collective-permute-start(bf16[128,256]{1,0:T(8,128)(2,1)S(1)} %get-tuple-element.24), channel_id=1, source_target_pairs={{0,8},{8,0},{16,24},{24,16},{1,9},{9,1},{17,25},{25,17},{2,10},{10... | collective-permute-start | bytes 196616 | tf_op jit(solution)/shard_map/ppermute | solution.py:442
  28.4 4.3 %collective-permute-start.4 = (bf16[128,256]{1,0:T(8,128)(2,1)S(1)}, bf16[128,256]{1,0:T(8,128)(2,1)S(1)}, u32[]{:S(2)}, u32[]{:S(2)}) collective-permute-start(bf16[128,256]{1,0:T(8,128)(2,1)S(1)} %get-tuple-element.25), channel_id=1, source_target_pairs={{0,16},{8,24},{16,0},{24,8},{1,17},{9,25},{17,1},{25,9},{2,18},{10... | collective-permute-start | bytes 196616 | tf_op jit(solution)/shard_map/ppermute | solution.py:442
  28.4 5.3 %collective-permute-start.5 = (bf16[128,256]{1,0:T(8,128)(2,1)S(1)}, bf16[128,256]{1,0:T(8,128)(2,1)S(1)}, u32[]{:S(2)}, u32[]{:S(2)}) collective-permute-start(bf16[128,256]{1,0:T(8,128)(2,1)S(1)} %get-tuple-element.26), channel_id=1, source_target_pairs={{0,24},{8,16},{16,8},{24,0},{1,25},{9,17},{17,9},{25,1},{2,26},{10... | collective-permute-start | bytes 196616 | tf_op jit(solution)/shard_map/ppermute | solution.py:442
  32.1 2.6 %collective-permute-start.11 = (bf16[4,256,256]{2,1,0:T(8,128)(2,1)S(1)}, bf16[4,256,256]{2,1,0:T(8,128)(2,1)S(1)}, u32[]{:S(2)}, u32[]{:S(2)}) collective-permute-start(bf16[4,256,256]{2,1,0:T(8,128)(2,1)S(1)} %stack.1.refs_2_), channel_id=1, source_target_pairs={{0,1},{1,0},{2,3},{3,2},{4,5},{5,4},{6,7},{7,6},{8,9},{9,8},{10,11... | collective-permute-start | bytes 1572872 | tf_op jit(solution)/shard_map/ppermute | solution.py:448
  33.7 3.8 %collective-permute-start.6 = (bf16[128,1024]{1,0:T(8,128)(2,1)S(1)}, bf16[128,1024]{1,0:T(8,128)(2,1)S(1)}, u32[]{:S(2)}, u32[]{:S(2)}) collective-permute-start(bf16[128,1024]{1,0:T(8,128)(2,1)S(1)} %join.1.refs_1_), channel_id=1, source_target_pairs={{0,1},{1,0},{2,3},{3,2},{4,5},{5,4},{6,7},{7,6},{8,9},{9,8},{10,11... | collective-permute-start | bytes 786440 | tf_op jit(solution)/shard_map/ppermute | solution.py:448
  34.7 2.8 %copy-start = (bf16[256,1024]{1,0:T(8,128)(2,1)S(1)}, bf16[256,1024]{1,0:T(8,128)(2,1)}, u32[]{:S(2)}) copy-start(bf16[256,1024]{1,0:T(8,128)(2,1)} %refs_1_.3) | copy-start | bytes 1572868
  39.4 2.1 %collective-permute-start.12 = (bf16[4,256,256]{2,1,0:T(8,128)(2,1)S(1)}, bf16[4,256,256]{2,1,0:T(8,128)(2,1)S(1)}, u32[]{:S(2)}, u32[]{:S(2)}) collective-permute-start(bf16[4,256,256]{2,1,0:T(8,128)(2,1)S(1)} %get-tuple-element.30), channel_id=1, source_target_pairs={{0,1},{1,0},{2,3},{3,2},{4,5},{5,4},{6,7},{7,6},{8,9},{9,8},{10,11... | collective-permute-start | bytes 1572872 | tf_op jit(solution)/shard_map/ppermute | solution.py:448
  42.3 21.3 %all-to-all-start.1 = ((bf16[4,256,256]{2,1,0:T(8,128)(2,1)}), bf16[4,256,256]{2,1,0:T(8,128)(2,1)S(1)}, u32[]{:S(2)}, u32[]{:S(2)}) async-start(bf16[4,256,256]{2,1,0:T(8,128)(2,1)} %add.1.refs_6_), calls=%async_computation.1 | async-start | bytes 1048576 | tf_op jit(solution)/shard_map/all_to_all | solution.py:452
  48.0 1.6 %collective-permute-start.16 = (bf16[128,1024]{1,0:T(8,128)(2,1)S(1)}, bf16[128,1024]{1,0:T(8,128)(2,1)S(1)}, u32[]{:S(2)}, u32[]{:S(2)}) collective-permute-start(bf16[128,1024]{1,0:T(8,128)(2,1)S(1)} %get-tuple-element.34), channel_id=1, source_target_pairs={{0,1},{1,0},{2,3},{3,2},{4,5},{5,4},{6,7},{7,6},{8,9},{9,8},{10,11... | collective-permute-start | bytes 786440 | tf_op jit(solution)/shard_map/ppermute | solution.py:448
  49.6 4.4 %collective-permute-start.17 = (bf16[32,1024]{1,0:T(8,128)(2,1)S(1)}, bf16[32,1024]{1,0:T(8,128)(2,1)S(1)}, u32[]{:S(2)}, u32[]{:S(2)}) collective-permute-start(bf16[32,1024]{1,0:T(8,128)(2,1)S(1)} %get-tuple-element.36), channel_id=1, source_target_pairs={{0,8},{8,0},{16,24},{24,16},{1,9},{9,1},{17,25},{25,17},{2,10},{10... | collective-permute-start | bytes 196616 | tf_op jit(solution)/shard_map/ppermute | solution.py:442
  51.6 5.0 %collective-permute-start.18 = (bf16[32,1024]{1,0:T(8,128)(2,1)S(1)}, bf16[32,1024]{1,0:T(8,128)(2,1)S(1)}, u32[]{:S(2)}, u32[]{:S(2)}) collective-permute-start(bf16[32,1024]{1,0:T(8,128)(2,1)S(1)} %get-tuple-element.37), channel_id=1, source_target_pairs={{0,16},{8,24},{16,0},{24,8},{1,17},{9,25},{17,1},{25,9},{2,18},{10... | collective-permute-start | bytes 196616 | tf_op jit(solution)/shard_map/ppermute | solution.py:442
  52.2 5.2 %collective-permute-start.19 = (bf16[32,1024]{1,0:T(8,128)(2,1)S(1)}, bf16[32,1024]{1,0:T(8,128)(2,1)S(1)}, u32[]{:S(2)}, u32[]{:S(2)}) collective-permute-start(bf16[32,1024]{1,0:T(8,128)(2,1)S(1)} %get-tuple-element.38), channel_id=1, source_target_pairs={{0,24},{8,16},{16,8},{24,0},{1,25},{9,17},{17,9},{25,1},{2,26},{10... | collective-permute-start | bytes 196616 | tf_op jit(solution)/shard_map/ppermute | solution.py:442
  57.4 9.9 %collective-permute-start.20 = (bf16[32,1024]{1,0:T(8,128)(2,1)S(1)}, bf16[32,1024]{1,0:T(8,128)(2,1)S(1)}, u32[]{:S(2)}, u32[]{:S(2)}) collective-permute-start(bf16[32,1024]{1,0:T(8,128)(2,1)S(1)} %get-tuple-element.40), channel_id=1, source_target_pairs={{0,2},{1,3},{2,0},{3,1},{4,6},{5,7},{6,4},{7,5},{8,10},{9,11},{10,... | collective-permute-start | bytes 196616 | tf_op jit(solution)/shard_map/ppermute | solution.py:445
  59.5 8.4 %collective-permute-start.21 = (bf16[32,1024]{1,0:T(8,128)(2,1)S(1)}, bf16[32,1024]{1,0:T(8,128)(2,1)S(1)}, u32[]{:S(2)}, u32[]{:S(2)}) collective-permute-start(bf16[32,1024]{1,0:T(8,128)(2,1)S(1)} %get-tuple-element.41), channel_id=1, source_target_pairs={{0,4},{1,5},{2,6},{3,7},{4,0},{5,1},{6,2},{7,3},{8,12},{9,13},{10,... | collective-permute-start | bytes 196616 | tf_op jit(solution)/shard_map/ppermute | solution.py:445
  61.9 6.1 %collective-permute-start.22 = (bf16[32,1024]{1,0:T(8,128)(2,1)S(1)}, bf16[32,1024]{1,0:T(8,128)(2,1)S(1)}, u32[]{:S(2)}, u32[]{:S(2)}) collective-permute-start(bf16[32,1024]{1,0:T(8,128)(2,1)S(1)} %get-tuple-element.42), channel_id=1, source_target_pairs={{0,6},{1,7},{2,4},{3,5},{4,2},{5,3},{6,0},{7,1},{8,14},{9,15},{10,... | collective-permute-start | bytes 196616 | tf_op jit(solution)/shard_map/ppermute | solution.py:445
  63.7 9.3 %copy-start.2 = (f32[256,1024]{1,0:T(8,128)S(1)}, f32[256,1024]{1,0:T(8,128)}, u32[]{:S(2)}) copy-start(f32[256,1024]{1,0:T(8,128)} %refs_0_.5) | copy-start | bytes 3145732
  63.7 7.5 %collective-permute-start.15 = (bf16[256,256]{1,0:T(8,128)(2,1)S(1)}, bf16[256,256]{1,0:T(8,128)(2,1)S(1)}, u32[]{:S(2)}, u32[]{:S(2)}) collective-permute-start(bf16[256,256]{1,0:T(8,128)(2,1)S(1)} %sum_rows.1.refs_2_.refs_4_), channel_id=1, source_target_pairs={{0,24},{8,16},{16,8},{24,0},{1,25},{9,17},{17,9},{25,1},{2,26},{10... | collective-permute-start | bytes 393224 | tf_op jit(solution)/shard_map/ppermute | solution.py:442
  67.2 5.8 %collective-permute-start.14 = (bf16[256,256]{1,0:T(8,128)(2,1)S(1)}, bf16[256,256]{1,0:T(8,128)(2,1)S(1)}, u32[]{:S(2)}, u32[]{:S(2)}) collective-permute-start(bf16[256,256]{1,0:T(8,128)(2,1)S(1)} %sum_rows.1.refs_2_.refs_4_), channel_id=1, source_target_pairs={{0,16},{8,24},{16,0},{24,8},{1,17},{9,25},{17,1},{25,9},{2,18},{10... | collective-permute-start | bytes 393224 | tf_op jit(solution)/shard_map/ppermute | solution.py:442
  67.3 5.7 %collective-permute-start.13 = (bf16[256,256]{1,0:T(8,128)(2,1)S(1)}, bf16[256,256]{1,0:T(8,128)(2,1)S(1)}, u32[]{:S(2)}, u32[]{:S(2)}) collective-permute-start(bf16[256,256]{1,0:T(8,128)(2,1)S(1)} %sum_rows.1.refs_2_.refs_4_), channel_id=1, source_target_pairs={{0,8},{8,0},{16,24},{24,16},{1,9},{9,1},{17,25},{25,17},{2,10},{10... | collective-permute-start | bytes 393224 | tf_op jit(solution)/shard_map/ppermute | solution.py:442
  68.0 5.1 %copy-start.9 = (f32[256]{0:T(256)S(1)}, f32[256]{0:T(256)}, u32[]{:S(2)}) copy-start(f32[256]{0:T(256)} %param.10) | copy-start | bytes 3076
  68.0 6.4 %collective-permute-start.25 = (bf16[32,1024]{1,0:T(8,128)(2,1)S(1)}, bf16[32,1024]{1,0:T(8,128)(2,1)S(1)}, u32[]{:S(2)}, u32[]{:S(2)}) collective-permute-start(bf16[32,1024]{1,0:T(8,128)(2,1)S(1)} %sum_parts.1.refs_0_), channel_id=1, source_target_pairs={{0,24},{8,16},{16,8},{24,0},{1,25},{9,17},{17,9},{25,1},{2,26},{10... | collective-permute-start | bytes 196616 | tf_op jit(solution)/shard_map/ppermute | solution.py:442
  70.8 4.3 %collective-permute-start.24 = (bf16[32,1024]{1,0:T(8,128)(2,1)S(1)}, bf16[32,1024]{1,0:T(8,128)(2,1)S(1)}, u32[]{:S(2)}, u32[]{:S(2)}) collective-permute-start(bf16[32,1024]{1,0:T(8,128)(2,1)S(1)} %sum_parts.1.refs_0_), channel_id=1, source_target_pairs={{0,16},{8,24},{16,0},{24,8},{1,17},{9,25},{17,1},{25,9},{2,18},{10... | collective-permute-start | bytes 196616 | tf_op jit(solution)/shard_map/ppermute | solution.py:442
  71.2 4.3 %collective-permute-start.23 = (bf16[32,1024]{1,0:T(8,128)(2,1)S(1)}, bf16[32,1024]{1,0:T(8,128)(2,1)S(1)}, u32[]{:S(2)}, u32[]{:S(2)}) collective-permute-start(bf16[32,1024]{1,0:T(8,128)(2,1)S(1)} %sum_parts.1.refs_0_), channel_id=1, source_target_pairs={{0,8},{8,0},{16,24},{24,16},{1,9},{9,1},{17,25},{25,17},{2,10},{10... | collective-permute-start | bytes 196616 | tf_op jit(solution)/shard_map/ppermute | solution.py:442
  74.4 1.1 %copy-start.5 = (f32[1,256]{1,0:T(1,128)S(1)}, f32[1,256]{1,0:T(1,128)}, u32[]{:S(2)}) copy-start(f32[1,256]{1,0:T(1,128)} %get-tuple-element.32.refs_4_) | copy-start | bytes 3076

commit v6 on v5

--- a/solution.py
+++ b/solution.py
@@ -205,10 +205,10 @@
         sem,
     )
     copies[1].wait()
-    for i in range((out.shape[0] - cols) // part):
-        out[cols + i * part : cols + (i + 1) * part, :] = part_in[:, i * rows : (i + 1) * rows]
+    for i in range((out.shape[0] - rows) // part):
+        out[rows + i * part : rows + (i + 1) * part, :] = part_in[:, i * cols : (i + 1) * cols]
     copies[0].wait()
-    out[0:cols, :] = rows_in[...].T.astype(BF16)
+    out[0:rows, :] = rows_in[...].astype(BF16)
 
 
 def pack_kernel(lens, owner, local, q, k, out, ids, sem):
@@ -257,9 +257,9 @@
 
 def stack_kernel(me, *refs):
     *blocks, out = refs
-    cols = out.shape[1]
+    rows = out.shape[1]
     for m, p in enumerate(blocks):
-        out[me[1] ^ m] = p[0:cols, :]
+        out[me[1] ^ m] = p[0:rows, :]
 
 
 def join_kernel(me, *refs):
@@ -318,28 +318,42 @@
     return jnp.where(at == named, 1.0, 0.0).astype(BF16)
 
 
-def mix_kernel(me, packs, w, mine, other, out):
-    n, cols, rows = mine.shape
+def mix_kernel(me, packs, w, mine, other, out, picks):
+    n, rows, cols = mine.shape
     heads, tok = w.shape[1:3]
     dv = cols // heads
-    blocks = jnp.concatenate([x[z] for z in range(n) for x in (mine, other)], axis=1)
+    same = iota((tok, tok), 0) == iota((tok, tok), 1)
+    at = iota((tok, rows), 1).astype(F32)
     for r in range(n):
-        ids = ids_of(packs, me[0] ^ r, w.shape[2])
-        picks = jnp.concatenate(
-            [one_hot(ids, 2 * z + (me[2] ^ cc), rows) for z in range(n) for cc in range(2)], axis=0
-        )
-        vals = nn(blocks, picks).astype(BF16)
+        ids = ids_of(packs, me[0] ^ r, tok)
+        own = jnp.sum(jnp.where(same, ids[0:1, :], 0.0), axis=1, keepdims=True)
+        loc = jnp.sum(jnp.where(same, ids[1:2, :], 0.0), axis=1, keepdims=True)
+        for z in range(n):
+            for cc in range(2):
+                shard = (2 * z + (me[2] ^ cc)).astype(F32)
+                named = jnp.where(own == shard, loc, -1.0)
+                first = (2 * z + cc) * rows
+                picks[r * tok : (r + 1) * tok, first : first + rows] = jnp.where(
+                    at == named, 1.0, 0.0
+                ).astype(BF16)
+    blocks = jnp.concatenate([x[z] for z in range(n) for x in (mine, other)], axis=0)
+    vals = nn(picks[...], blocks).astype(BF16)
+    for r in range(n):
+        turned = vals[r * tok : (r + 1) * tok, :].T
         for j in range(heads):
             out[j * dv : (j + 1) * dv, r * tok : (r + 1) * tok] = nn(
-                vals[j * dv : (j + 1) * dv, :], w[r, j]
+                turned[j * dv : (j + 1) * dv, :], w[r, j]
             ).astype(BF16)
 
 
-def by_row(me, packs, grad, core, z, rows):
-    n = packs.shape[0]
+def by_row(me, packs, grad, core, out):
+    n, rows, _ = out.shape
     tok = grad.shape[0] // n
     ids = jnp.concatenate([ids_of(packs, me[0] ^ r, tok) for r in range(n)], axis=1)
-    return nn(one_hot(ids, 2 * z + core, rows), grad[...])
+    picks = jnp.concatenate([one_hot(ids, 2 * z + core, rows) for z in range(n)], axis=0)
+    total = nn(picks, grad[...])
+    for z in range(n):
+        out[z] = total[z * rows : (z + 1) * rows, :].astype(out.dtype)
 
 
 def back_kernel(me, packs, ow_mine, ow_other, w, *refs):
@@ -359,13 +373,11 @@
         for j in range(heads):
             at_j = slice(j * head_rows, (j + 1) * head_rows)
             grad[at_r, at_j] = nn(w[r, j], grad[at_r, at_j]).astype(BF16)
-    for z in range(n):
-        send[z] = by_row(me, packs, grad, 1 - me[2], z, send.shape[1]).astype(BF16)
+    by_row(me, packs, grad, 1 - me[2], send)
 
 
 def keep_kernel(me, packs, grad, keep):
-    for z in range(keep.shape[0]):
-        keep[z] = by_row(me, packs, grad, me[2], z, keep.shape[1])
+    by_row(me, packs, grad, me[2], keep)
 
 
 def wgrad_kernel(me, mixed, *refs):
@@ -456,11 +468,11 @@
 
     half = tok // 2
     x, y = column(cotangent, 1), column(cotangent, 2)
-    zrows = cols + part * width // rows
+    zrows = rows + part * width // cols
     zpay = call(
         carry_kernel,
         "carry",
-        sds((zrows, rows)),
+        sds((zrows, cols)),
         (out_weight, table),
         hbm=(0, 1),
         scratch=[
@@ -505,14 +517,14 @@
     owp = call(
         choose_kernel,
         "choose",
-        [sds((zrows - cols, rows))] * n,
+        [sds((zrows - rows, cols))] * n,
         blocks,
         after=(packs,),
-        scratch=[pltpu.VMEM((n, zrows - cols, rows), BF16)],
+        scratch=[pltpu.VMEM((n, zrows - rows, cols), BF16)],
         placed=True,
     )
     mine = call(
-        stack_kernel, "stack", sds((n, cols, rows)), blocks, after=(owp[0],), placed=True
+        stack_kernel, "stack", sds((n, rows, cols)), blocks, after=(owp[0],), placed=True
     )
     other = core(mine)
     owp = [column(p, m) for m, p in enumerate(owp)]
@@ -523,7 +535,12 @@
     here = call(gate_kernel, "gate", sds((8, 128), F32), (), after=(far_x, far_y), cost=GATE_COST)
 
     mixed = call(
-        mix_kernel, "mix", sds((cols, n * tok)), (packs, w, mine, other), placed=True
+        mix_kernel,
+        "mix",
+        sds((cols, n * tok)),
+        (packs, w, mine, other),
+        scratch=[pltpu.VMEM((n * tok, shards * rows), BF16)],
+        placed=True,
     )
     send, grad = call(
         back_kernel,

time: 76.5 us -> 75.3 us (0.984)
  Pallas kernels: 13.5 us -> 12.3 us
    pallas_call x20, Pallas kernels: 13.5 us -> 12.3 us  [call(): pl.pallas_call(run, out_shape=out, in_specs=[SMEM if i < smem else HBM if...]
  transfers between devices with their start and end apart: 28 -> 28, of which waited for: 17 -> 17; matrix products, arithmetic and copies ran while one was open for 0% -> 0% of each run, Pallas kernels for 13% -> 12%
where the time goes in v6:
time: 75.3 us; the launch traced here: 75 us
  starting transfers between devices  41.6 us (55%)
  waiting for transfers between devices  19.5 us (26%)
  Pallas kernels  12.3 us (16%)
  between operations  0.88 us (1%)
    ppermute x16, starting transfers between devices, column(): lax.ppermute(x, 'replica', [(i, i ^ m) for i in range(n)])  23.6 us
    pallas_call x20, Pallas kernels, call(): pl.pallas_call(run, out_shape=out, in_specs=[SMEM if i < smem else HBM if...  12.3 us
    ppermute x16, waiting for transfers between devices, column(): lax.ppermute(x, 'replica', [(i, i ^ m) for i in range(n)])  9.08 us
    ppermute x6, starting transfers between devices, along(): lax.ppermute(x, 'shard', [(i, i ^ 2 * m) for i in range(shards)])  8.98 us
    ppermute x6, waiting for transfers between devices, along(): lax.ppermute(x, 'shard', [(i, i ^ 2 * m) for i in range(shards)])  6.42 us
    all_to_all x1, starting transfers between devices, swap_along(): lax.all_to_all(x, 'shard', 0, 0, tiled=True, axis_index_groups=groups)  4.79 us
    all_to_all x1, starting transfers between devices, swap_columns(): return lax.all_to_all(x, 'replica', 0, 0, tiled=True)  3.49 us
    ppermute x4, waiting for transfers between devices, core(): return lax.ppermute(x, 'shard', [(i, i ^ 1) for i in range(shards)])  2.29 us
  transfers between devices with their start and end apart: 28, of which 17 were waited for; matrix products, arithmetic and copies ran while one was open for 0% of the time, Pallas kernels for 12%

profile of v6, /device:TPU:0, one launch (start us, length us, event | category | flops | bytes accessed | tf_op | source)
XLA Modules:
  0.0 75.0 jit_solution(17097490440434425331)
XLA Ops:
  0.7 3.0 %collective-permute-start.8 = (bf16[256,1024]{1,0:T(8,128)(2,1)}, bf16[256,1024]{1,0:T(8,128)(2,1)S(1)}, u32[]{:S(2)}, u32[]{:S(2)}) collective-permute-start(bf16[256,1024]{1,0:T(8,128)(2,1)} %refs_1_.3), channel_id=1, source_target_pairs={{0,16},{8,24},{16,0},{24,8},{1,17},{9,25},{17,1},{25,9},{2,18},{10... | collective-permute-start | bytes 1572872 | tf_op jit(solution)/shard_map/ppermute | solution.py:454
  3.7 1.5 %collective-permute-start.7 = (bf16[256,1024]{1,0:T(8,128)(2,1)}, bf16[256,1024]{1,0:T(8,128)(2,1)S(1)}, u32[]{:S(2)}, u32[]{:S(2)}) collective-permute-start(bf16[256,1024]{1,0:T(8,128)(2,1)} %refs_1_.3), channel_id=1, source_target_pairs={{0,8},{8,0},{16,24},{24,16},{1,9},{9,1},{17,25},{25,17},{2,10},{10... | collective-permute-start | bytes 1572872 | tf_op jit(solution)/shard_map/ppermute | solution.py:454
  5.2 1.7 %carry.1.refs_0_ = bf16[384,256]{1,0:T(8,128)(2,1)} custom-call(bf16[128,1024]{1,0:T(8,128)(2,1)} %refs_0_.4, f32[256,1024]{1,0:T(8,128)} %refs_0_.5), custom_call_target="tpu_custom_call" | custom-call | tf_op jit(solution)/shard_map/carry/pallas_call | solution.py:169
  6.9 3.7 %collective-permute-start.2 = (bf16[384,256]{1,0:T(8,128)(2,1)}, bf16[384,256]{1,0:T(8,128)(2,1)S(1)}, u32[]{:S(2)}, u32[]{:S(2)}) collective-permute-start(bf16[384,256]{1,0:T(8,128)(2,1)} %carry.1.refs_0_), channel_id=1, source_target_pairs={{0,6},{1,7},{2,4},{3,5},{4,2},{5,3},{6,0},{7,1},{8,14},{9,15},{10,... | collective-permute-start | bytes 589832 | tf_op jit(solution)/shard_map/ppermute | solution.py:457
  10.5 0.8 %collective-permute-start = (bf16[384,256]{1,0:T(8,128)(2,1)}, bf16[384,256]{1,0:T(8,128)(2,1)S(1)}, u32[]{:S(2)}, u32[]{:S(2)}) collective-permute-start(bf16[384,256]{1,0:T(8,128)(2,1)} %carry.1.refs_0_), channel_id=1, source_target_pairs={{0,2},{1,3},{2,0},{3,1},{4,6},{5,7},{6,4},{7,5},{8,10},{9,11},{10,... | collective-permute-start | bytes 589832 | tf_op jit(solution)/shard_map/ppermute | solution.py:457
  11.3 0.7 copy-done.6
  12.0 1.4 %pack.1 = bf16[4,544,128]{2,1,0:T(8,128)(2,1)} custom-call(s32[1,4]{1,0:T(1,128)S(1)} %copy-done.8, s32[1,256]{1,0:T(1,128)S(1)} %bitcast.5, s32[1,256]{1,0:T(1,128)S(1)} %bitcast.6, bf16[256,512]{1,0:T(8,128)(2,1)S(1)} %copy-done.3, bf16[256,512]{1,0:T(8,128)(2,1)S(1)} %copy-done.4), custom_call_target="tpu_custom_call" | custom-call | tf_op jit(solution)/shard_map/pack/pallas_call | solution.py:169
  13.4 3.5 %all-to-all-start = ((bf16[4,544,128]{2,1,0:T(8,128)(2,1)}), bf16[4,544,128]{2,1,0:T(8,128)(2,1)S(1)}, u32[]{:S(2)}, u32[]{:S(2)}) async-start(bf16[4,544,128]{2,1,0:T(8,128)(2,1)} %pack.1), calls=%async_computation | async-start | bytes 1114112 | tf_op jit(solution)/shard_map/all_to_all | solution.py:467
  16.9 0.3 collective-permute-done.7.refs_0_.refs_5_.refs_2_
  17.3 1.7 %collective-permute-start.10 = (bf16[128,1024]{1,0:T(8,128)(2,1)S(1)}, bf16[128,1024]{1,0:T(8,128)(2,1)S(1)}, u32[]{:S(2)}, u32[]{:S(2)}) collective-permute-start(bf16[128,1024]{1,0:T(8,128)(2,1)S(1)} %get-tuple-element.28), channel_id=1, source_target_pairs={{0,16},{8,24},{16,0},{24,8},{1,17},{9,25},{17,1},{25,9},{2,18},{10... | collective-permute-start | bytes 786440 | tf_op jit(solution)/shard_map/ppermute | solution.py:454
  19.1 1.5 %collective-permute-start.9 = (bf16[128,1024]{1,0:T(8,128)(2,1)S(1)}, bf16[128,1024]{1,0:T(8,128)(2,1)S(1)}, u32[]{:S(2)}, u32[]{:S(2)}) collective-permute-start(bf16[128,1024]{1,0:T(8,128)(2,1)S(1)} %get-tuple-element.27.refs_1_), channel_id=1, source_target_pairs={{0,8},{8,0},{16,24},{24,16},{1,9},{9,1},{17,25},{25,17},{2,10},{10... | collective-permute-start | bytes 786440 | tf_op jit(solution)/shard_map/ppermute | solution.py:454
  20.5 6.3 %collective-permute-done.1.refs_2_ = bf16[384,256]{1,0:T(8,128)(2,1)S(1)} collective-permute-done((bf16[384,256]{1,0:T(8,128)(2,1)}, bf16[384,256]{1,0:T(8,128)(2,1)S(1)}, u32[]{:S(2)}, u32[]{:S(2)}) %collective-permute-start.1) | collective-permute-done | bytes 196640 | tf_op jit(solution)/shard_map/ppermute | solution.py:457
  26.9 1.4 %collective-permute-start.3 = (bf16[128,256]{1,0:T(8,128)(2,1)S(1)}, bf16[128,256]{1,0:T(8,128)(2,1)S(1)}, u32[]{:S(2)}, u32[]{:S(2)}) collective-permute-start(bf16[128,256]{1,0:T(8,128)(2,1)S(1)} %get-tuple-element.24), channel_id=1, source_target_pairs={{0,8},{8,0},{16,24},{24,16},{1,9},{9,1},{17,25},{25,17},{2,10},{10... | collective-permute-start | bytes 196616 | tf_op jit(solution)/shard_map/ppermute | solution.py:454
  28.3 2.1 %collective-permute-start.5 = (bf16[128,256]{1,0:T(8,128)(2,1)S(1)}, bf16[128,256]{1,0:T(8,128)(2,1)S(1)}, u32[]{:S(2)}, u32[]{:S(2)}) collective-permute-start(bf16[128,256]{1,0:T(8,128)(2,1)S(1)} %get-tuple-element.26), channel_id=1, source_target_pairs={{0,24},{8,16},{16,8},{24,0},{1,25},{9,17},{17,9},{25,1},{2,26},{10... | collective-permute-start | bytes 196616 | tf_op jit(solution)/shard_map/ppermute | solution.py:454
  30.5 1.5 %collective-permute-done.3.refs_1_ = bf16[128,256]{1,0:T(8,128)(2,1)S(1)} collective-permute-done((bf16[128,256]{1,0:T(8,128)(2,1)S(1)}, bf16[128,256]{1,0:T(8,128)(2,1)S(1)}, u32[]{:S(2)}, u32[]{:S(2)}) %collective-permute-start.3) | collective-permute-done | bytes 65568 | tf_op jit(solution)/shard_map/ppermute | solution.py:454
  32.0 0.6 collective-permute-done.4.refs_2_
  32.6 1.0 %collective-permute-done.5.refs_3_ = bf16[128,256]{1,0:T(8,128)(2,1)S(1)} collective-permute-done((bf16[128,256]{1,0:T(8,128)(2,1)S(1)}, bf16[128,256]{1,0:T(8,128)(2,1)S(1)}, u32[]{:S(2)}, u32[]{:S(2)}) %collective-permute-start.5) | collective-permute-done | bytes 65568 | tf_op jit(solution)/shard_map/ppermute | solution.py:454
  33.7 0.8 %weights.1.refs_1_.refs_3_ = bf16[4,2,256,256]{3,2,1,0:T(8,128)(2,1)S(1)} custom-call(bf16[4,544,128]{2,1,0:T(8,128)(2,1)S(1)} %all-to-all-done.refs_4_.refs_0_, bf16[128,1024]{1,0:T(8,128)(2,1)S(1)} %get-tuple-element.27.refs_1_), custom_call_target="tpu_custom_call" | custom-call | tf_op jit(solution)/shard_map/weights/pallas_call | solution.py:169
  34.6 1.7 %mix.1.refs_10_.refs_0_ = bf16[256,1024]{1,0:T(8,128)(2,1)S(1)} custom-call(bf16[4,544,128]{2,1,0:T(8,128)(2,1)S(1)} %all-to-all-done.refs_4_.refs_0_, bf16[4,2,256,256]{3,2,1,0:T(8,128)(2,1)S(1)} %weights.1.refs_1_.refs_3_, bf16[4,256,256]{2,1,0:T(8,128)(2,1)S(1)} %stack.1.refs_2_, bf16[4,256,256]{2,1,0:T(8,128)(2,1)S(1)} %collective-permute-done.11.refs_3_), custom_call_target="tpu_custom_call" | custom-call | tf_op jit(solution)/shard_map/mix/pallas_call | solution.py:169
  36.3 1.8 %back.1 = (bf16[4,256,256]{2,1,0:T(8,128)(2,1)S(1)}, bf16[1024,256]{1,0:T(8,128)(2,1)S(1)}) custom-call(bf16[4,544,128]{2,1,0:T(8,128)(2,1)S(1)} %all-to-all-done.refs_4_.refs_0_, bf16[128,1024]{1,0:T(8,128)(2,1)S(1)} %join.1.refs_1_, bf16[128,1024]{1,0:T(8,128)(2,1)S(1)} %collective-permute-done.6.refs_2_, ...), custom_call_target="tpu_custom_call" | custom-call | tf_op jit(solution)/shard_map/back/pallas_call | solution.py:169
  38.2 0.6 collective-permute-start.12
  38.7 0.7 keep.1.refs_0_
  39.5 0.8 %collective-permute-done.12.refs_1_ = bf16[4,256,256]{2,1,0:T(8,128)(2,1)S(1)} collective-permute-done((bf16[4,256,256]{2,1,0:T(8,128)(2,1)S(1)}, bf16[4,256,256]{2,1,0:T(8,128)(2,1)S(1)}, u32[]{:S(2)}, u32[]{:S(2)}) %collective-permute-start.12) | collective-permute-done | bytes 524320 | tf_op jit(solution)/shard_map/ppermute | solution.py:460
  40.3 0.9 %add.1.refs_6_ = bf16[4,256,256]{2,1,0:T(8,128)(2,1)} custom-call(f32[4,256,256]{2,1,0:T(8,128)S(1)} %keep.1.refs_0_, bf16[4,256,256]{2,1,0:T(8,128)(2,1)S(1)} %collective-permute-done.12.refs_1_), custom_call_target="tpu_custom_call" | custom-call | tf_op jit(solution)/shard_map/add/pallas_call | solution.py:169
  41.2 4.8 %all-to-all-start.1 = ((bf16[4,256,256]{2,1,0:T(8,128)(2,1)}), bf16[4,256,256]{2,1,0:T(8,128)(2,1)S(1)}, u32[]{:S(2)}, u32[]{:S(2)}) async-start(bf16[4,256,256]{2,1,0:T(8,128)(2,1)} %add.1.refs_6_), calls=%async_computation.1 | async-start | bytes 1048576 | tf_op jit(solution)/shard_map/all_to_all | solution.py:464
  45.9 0.9 %wgrad.1 = (f32[128,1024]{1,0:T(8,128)S(1)}, bf16[128,1024]{1,0:T(8,128)(2,1)S(1)}) custom-call(bf16[256,1024]{1,0:T(8,128)(2,1)S(1)} %mix.1.refs_10_.refs_0_, bf16[256,1024]{1,0:T(8,128)(2,1)S(1)} %copy-done, bf16[256,1024]{1,0:T(8,128)(2,1)S(1)} %collective-permute-done.7.refs_0_.refs_5_.refs_2_, ...), custom_call_target="tpu_custom_call" | custom-call | tf_op jit(solution)/shard_map/wgrad/pallas_call | solution.py:169
  46.8 0.1 collective-permute-start.16
  46.9 1.5 %collective-permute-done.16.refs_1_ = bf16[128,1024]{1,0:T(8,128)(2,1)S(1)} collective-permute-done((bf16[128,1024]{1,0:T(8,128)(2,1)S(1)}, bf16[128,1024]{1,0:T(8,128)(2,1)S(1)}, u32[]{:S(2)}, u32[]{:S(2)}) %collective-permute-start.16) | collective-permute-done | bytes 262176 | tf_op jit(solution)/shard_map/ppermute | solution.py:460
  48.5 2.0 %collective-permute-start.17 = (bf16[32,1024]{1,0:T(8,128)(2,1)S(1)}, bf16[32,1024]{1,0:T(8,128)(2,1)S(1)}, u32[]{:S(2)}, u32[]{:S(2)}) collective-permute-start(bf16[32,1024]{1,0:T(8,128)(2,1)S(1)} %get-tuple-element.36), channel_id=1, source_target_pairs={{0,8},{8,0},{16,24},{24,16},{1,9},{9,1},{17,25},{25,17},{2,10},{10... | collective-permute-start | bytes 196616 | tf_op jit(solution)/shard_map/ppermute | solution.py:454
  50.5 0.6 collective-permute-start.18
  51.0 1.0 %collective-permute-start.19 = (bf16[32,1024]{1,0:T(8,128)(2,1)S(1)}, bf16[32,1024]{1,0:T(8,128)(2,1)S(1)}, u32[]{:S(2)}, u32[]{:S(2)}) collective-permute-start(bf16[32,1024]{1,0:T(8,128)(2,1)S(1)} %get-tuple-element.38), channel_id=1, source_target_pairs={{0,24},{8,16},{16,8},{24,0},{1,25},{9,17},{17,9},{25,1},{2,26},{10... | collective-permute-start | bytes 196616 | tf_op jit(solution)/shard_map/ppermute | solution.py:454
  52.0 0.8 %collective-permute-done.17.refs_1_ = bf16[32,1024]{1,0:T(8,128)(2,1)S(1)} collective-permute-done((bf16[32,1024]{1,0:T(8,128)(2,1)S(1)}, bf16[32,1024]{1,0:T(8,128)(2,1)S(1)}, u32[]{:S(2)}, u32[]{:S(2)}) %collective-permute-start.17) | collective-permute-done | bytes 65568 | tf_op jit(solution)/shard_map/ppermute | solution.py:454
  52.9 2.6 %collective-permute-done.18.refs_2_ = bf16[32,1024]{1,0:T(8,128)(2,1)S(1)} collective-permute-done((bf16[32,1024]{1,0:T(8,128)(2,1)S(1)}, bf16[32,1024]{1,0:T(8,128)(2,1)S(1)}, u32[]{:S(2)}, u32[]{:S(2)}) %collective-permute-start.18) | collective-permute-done | bytes 65568 | tf_op jit(solution)/shard_map/ppermute | solution.py:454
  55.4 0.8 %collective-permute-done.19.refs_3_ = bf16[32,1024]{1,0:T(8,128)(2,1)S(1)} collective-permute-done((bf16[32,1024]{1,0:T(8,128)(2,1)S(1)}, bf16[32,1024]{1,0:T(8,128)(2,1)S(1)}, u32[]{:S(2)}, u32[]{:S(2)}) %collective-permute-start.19) | collective-permute-done | bytes 65568 | tf_op jit(solution)/shard_map/ppermute | solution.py:454
  56.2 2.1 %collective-permute-start.20 = (bf16[32,1024]{1,0:T(8,128)(2,1)S(1)}, bf16[32,1024]{1,0:T(8,128)(2,1)S(1)}, u32[]{:S(2)}, u32[]{:S(2)}) collective-permute-start(bf16[32,1024]{1,0:T(8,128)(2,1)S(1)} %get-tuple-element.40), channel_id=1, source_target_pairs={{0,2},{1,3},{2,0},{3,1},{4,6},{5,7},{6,4},{7,5},{8,10},{9,11},{10,... | collective-permute-start | bytes 196616 | tf_op jit(solution)/shard_map/ppermute | solution.py:457
  58.3 2.4 %collective-permute-start.21 = (bf16[32,1024]{1,0:T(8,128)(2,1)S(1)}, bf16[32,1024]{1,0:T(8,128)(2,1)S(1)}, u32[]{:S(2)}, u32[]{:S(2)}) collective-permute-start(bf16[32,1024]{1,0:T(8,128)(2,1)S(1)} %get-tuple-element.41), channel_id=1, source_target_pairs={{0,4},{1,5},{2,6},{3,7},{4,0},{5,1},{6,2},{7,3},{8,12},{9,13},{10,... | collective-permute-start | bytes 196616 | tf_op jit(solution)/shard_map/ppermute | solution.py:457
  60.8 1.7 %all-to-all-done.1.refs_0_ = bf16[4,256,256]{2,1,0:T(8,128)(2,1)S(1)} async-done(((bf16[4,256,256]{2,1,0:T(8,128)(2,1)}), bf16[4,256,256]{2,1,0:T(8,128)(2,1)S(1)}, u32[]{:S(2)}, u32[]{:S(2)}) %all-to-all-start.1) | async-done | bytes 524320 | tf_op jit(solution)/shard_map/all_to_all | solution.py:464
  62.6 3.5 %collective-permute-start.15 = (bf16[256,256]{1,0:T(8,128)(2,1)S(1)}, bf16[256,256]{1,0:T(8,128)(2,1)S(1)}, u32[]{:S(2)}, u32[]{:S(2)}) collective-permute-start(bf16[256,256]{1,0:T(8,128)(2,1)S(1)} %sum_rows.1.refs_2_.refs_4_), channel_id=1, source_target_pairs={{0,24},{8,16},{16,8},{24,0},{1,25},{9,17},{17,9},{25,1},{2,26},{10... | collective-permute-start | bytes 393224 | tf_op jit(solution)/shard_map/ppermute | solution.py:454
  66.1 0.6 collective-permute-start.13
  66.8 2.9 %collective-permute-start.25 = (bf16[32,1024]{1,0:T(8,128)(2,1)S(1)}, bf16[32,1024]{1,0:T(8,128)(2,1)S(1)}, u32[]{:S(2)}, u32[]{:S(2)}) collective-permute-start(bf16[32,1024]{1,0:T(8,128)(2,1)S(1)} %sum_parts.1.refs_0_), channel_id=1, source_target_pairs={{0,24},{8,16},{16,8},{24,0},{1,25},{9,17},{17,9},{25,1},{2,26},{10... | collective-permute-start | bytes 196616 | tf_op jit(solution)/shard_map/ppermute | solution.py:454
  69.7 0.3 collective-permute-start.24
  69.9 0.1 collective-permute-done.15.refs_5_
  70.0 1.6 %collective-permute-start.23 = (bf16[32,1024]{1,0:T(8,128)(2,1)S(1)}, bf16[32,1024]{1,0:T(8,128)(2,1)S(1)}, u32[]{:S(2)}, u32[]{:S(2)}) collective-permute-start(bf16[32,1024]{1,0:T(8,128)(2,1)S(1)} %sum_parts.1.refs_0_), channel_id=1, source_target_pairs={{0,8},{8,0},{16,24},{24,16},{1,9},{9,1},{17,25},{25,17},{2,10},{10... | collective-permute-start | bytes 196616 | tf_op jit(solution)/shard_map/ppermute | solution.py:454
  71.6 0.2 collective-permute-done.14.refs_4_
  71.9 1.3 %update.1 = (f32[256,1024]{1,0:T(8,128)}, f32[1,256]{1,0:T(1,128)}) custom-call(f32[256,1024]{1,0:T(8,128)S(1)} %copy-done.2, f32[1,256]{1,0:T(1,128)S(1)} %bitcast.7, bf16[256,256]{1,0:T(8,128)(2,1)S(1)} %sum_rows.1.refs_2_.refs_4_, bf16[256,256]{1,0:T(8,128)(2,1)S(1)} %collective-permute-done.13.refs_3_, ...), custom_call_target="tpu_custom_call" | custom-call | flops 8000000000 | tf_op jit(solution)/shard_map/update/pallas_call | solution.py:169
  73.2 0.7 collective-permute-done.24.refs_2_
  73.9 0.4 collective-permute-done.23.refs_1_
  74.3 0.7 place.1
  (48 shorter events, 0.8 us)
Async XLA Ops:
  0.6 10.7 %copy-start.4 = (bf16[256,512]{1,0:T(8,128)(2,1)S(1)}, bf16[256,512]{1,0:T(8,128)(2,1)}, u32[]{:S(2)}) copy-start(bf16[256,512]{1,0:T(8,128)(2,1)} %refs_4_.2) | copy-start | bytes 786436
  0.6 10.7 %copy-start.3 = (bf16[256,512]{1,0:T(8,128)(2,1)S(1)}, bf16[256,512]{1,0:T(8,128)(2,1)}, u32[]{:S(2)}) copy-start(bf16[256,512]{1,0:T(8,128)(2,1)} %refs_3_.1) | copy-start | bytes 786436
  0.7 16.3 %collective-permute-start.8 = (bf16[256,1024]{1,0:T(8,128)(2,1)}, bf16[256,1024]{1,0:T(8,128)(2,1)S(1)}, u32[]{:S(2)}, u32[]{:S(2)}) collective-permute-start(bf16[256,1024]{1,0:T(8,128)(2,1)} %refs_1_.3), channel_id=1, source_target_pairs={{0,16},{8,24},{16,0},{24,8},{1,17},{9,25},{17,1},{25,9},{2,18},{10... | collective-permute-start | bytes 1572872 | tf_op jit(solution)/shard_map/ppermute | solution.py:454
  3.7 13.6 %collective-permute-start.7 = (bf16[256,1024]{1,0:T(8,128)(2,1)}, bf16[256,1024]{1,0:T(8,128)(2,1)S(1)}, u32[]{:S(2)}, u32[]{:S(2)}) collective-permute-start(bf16[256,1024]{1,0:T(8,128)(2,1)} %refs_1_.3), channel_id=1, source_target_pairs={{0,8},{8,0},{16,24},{24,16},{1,9},{9,1},{17,25},{25,17},{2,10},{10... | collective-permute-start | bytes 1572872 | tf_op jit(solution)/shard_map/ppermute | solution.py:454
  5.2 6.1 %copy-start.7 = (s32[256]{0:T(256)S(1)}, s32[256]{0:T(256)}, u32[]{:S(2)}) copy-start(s32[256]{0:T(256)} %param.12) | copy-start | bytes 3076
  6.9 13.7 %collective-permute-start.2 = (bf16[384,256]{1,0:T(8,128)(2,1)}, bf16[384,256]{1,0:T(8,128)(2,1)S(1)}, u32[]{:S(2)}, u32[]{:S(2)}) collective-permute-start(bf16[384,256]{1,0:T(8,128)(2,1)} %carry.1.refs_0_), channel_id=1, source_target_pairs={{0,6},{1,7},{2,4},{3,5},{4,2},{5,3},{6,0},{7,1},{8,14},{9,15},{10,... | collective-permute-start | bytes 589832 | tf_op jit(solution)/shard_map/ppermute | solution.py:457
  10.5 16.3 %collective-permute-start.1 = (bf16[384,256]{1,0:T(8,128)(2,1)}, bf16[384,256]{1,0:T(8,128)(2,1)S(1)}, u32[]{:S(2)}, u32[]{:S(2)}) collective-permute-start(bf16[384,256]{1,0:T(8,128)(2,1)} %carry.1.refs_0_), channel_id=1, source_target_pairs={{0,4},{1,5},{2,6},{3,7},{4,0},{5,1},{6,2},{7,3},{8,12},{9,13},{10,... | collective-permute-start | bytes 589832 | tf_op jit(solution)/shard_map/ppermute | solution.py:457
  10.5 16.3 %collective-permute-start = (bf16[384,256]{1,0:T(8,128)(2,1)}, bf16[384,256]{1,0:T(8,128)(2,1)S(1)}, u32[]{:S(2)}, u32[]{:S(2)}) collective-permute-start(bf16[384,256]{1,0:T(8,128)(2,1)} %carry.1.refs_0_), channel_id=1, source_target_pairs={{0,2},{1,3},{2,0},{3,1},{4,6},{5,7},{6,4},{7,5},{8,10},{9,11},{10,... | collective-permute-start | bytes 589832 | tf_op jit(solution)/shard_map/ppermute | solution.py:457
  11.3 0.7 copy-start.6
  11.3 0.7 copy-start.8
  13.4 13.4 %all-to-all-start = ((bf16[4,544,128]{2,1,0:T(8,128)(2,1)}), bf16[4,544,128]{2,1,0:T(8,128)(2,1)S(1)}, u32[]{:S(2)}, u32[]{:S(2)}) async-start(bf16[4,544,128]{2,1,0:T(8,128)(2,1)} %pack.1), calls=%async_computation | async-start | bytes 1114112 | tf_op jit(solution)/shard_map/all_to_all | solution.py:467
  16.9 9.9 %copy-start.1 = (bf16[384,256]{1,0:T(8,128)(2,1)S(1)}, bf16[384,256]{1,0:T(8,128)(2,1)}, u32[]{:S(2)}) copy-start(bf16[384,256]{1,0:T(8,128)(2,1)} %carry.1.refs_0_) | copy-start | bytes 589828
  17.3 17.2 %collective-permute-start.10 = (bf16[128,1024]{1,0:T(8,128)(2,1)S(1)}, bf16[128,1024]{1,0:T(8,128)(2,1)S(1)}, u32[]{:S(2)}, u32[]{:S(2)}) collective-permute-start(bf16[128,1024]{1,0:T(8,128)(2,1)S(1)} %get-tuple-element.28), channel_id=1, source_target_pairs={{0,16},{8,24},{16,0},{24,8},{1,17},{9,25},{17,1},{25,9},{2,18},{10... | collective-permute-start | bytes 786440 | tf_op jit(solution)/shard_map/ppermute | solution.py:454
  19.1 15.5 %collective-permute-start.9 = (bf16[128,1024]{1,0:T(8,128)(2,1)S(1)}, bf16[128,1024]{1,0:T(8,128)(2,1)S(1)}, u32[]{:S(2)}, u32[]{:S(2)}) collective-permute-start(bf16[128,1024]{1,0:T(8,128)(2,1)S(1)} %get-tuple-element.27.refs_1_), channel_id=1, source_target_pairs={{0,8},{8,0},{16,24},{24,16},{1,9},{9,1},{17,25},{25,17},{2,10},{10... | collective-permute-start | bytes 786440 | tf_op jit(solution)/shard_map/ppermute | solution.py:454
  26.9 5.1 %collective-permute-start.3 = (bf16[128,256]{1,0:T(8,128)(2,1)S(1)}, bf16[128,256]{1,0:T(8,128)(2,1)S(1)}, u32[]{:S(2)}, u32[]{:S(2)}) collective-permute-start(bf16[128,256]{1,0:T(8,128)(2,1)S(1)} %get-tuple-element.24), channel_id=1, source_target_pairs={{0,8},{8,0},{16,24},{24,16},{1,9},{9,1},{17,25},{25,17},{2,10},{10... | collective-permute-start | bytes 196616 | tf_op jit(solution)/shard_map/ppermute | solution.py:454
  28.3 4.3 %collective-permute-start.4 = (bf16[128,256]{1,0:T(8,128)(2,1)S(1)}, bf16[128,256]{1,0:T(8,128)(2,1)S(1)}, u32[]{:S(2)}, u32[]{:S(2)}) collective-permute-start(bf16[128,256]{1,0:T(8,128)(2,1)S(1)} %get-tuple-element.25), channel_id=1, source_target_pairs={{0,16},{8,24},{16,0},{24,8},{1,17},{9,25},{17,1},{25,9},{2,18},{10... | collective-permute-start | bytes 196616 | tf_op jit(solution)/shard_map/ppermute | solution.py:454
  28.3 5.3 %collective-permute-start.5 = (bf16[128,256]{1,0:T(8,128)(2,1)S(1)}, bf16[128,256]{1,0:T(8,128)(2,1)S(1)}, u32[]{:S(2)}, u32[]{:S(2)}) collective-permute-start(bf16[128,256]{1,0:T(8,128)(2,1)S(1)} %get-tuple-element.26), channel_id=1, source_target_pairs={{0,24},{8,16},{16,8},{24,0},{1,25},{9,17},{17,9},{25,1},{2,26},{10... | collective-permute-start | bytes 196616 | tf_op jit(solution)/shard_map/ppermute | solution.py:454
  32.0 2.6 %collective-permute-start.11 = (bf16[4,256,256]{2,1,0:T(8,128)(2,1)S(1)}, bf16[4,256,256]{2,1,0:T(8,128)(2,1)S(1)}, u32[]{:S(2)}, u32[]{:S(2)}) collective-permute-start(bf16[4,256,256]{2,1,0:T(8,128)(2,1)S(1)} %stack.1.refs_2_), channel_id=1, source_target_pairs={{0,1},{1,0},{2,3},{3,2},{4,5},{5,4},{6,7},{7,6},{8,9},{9,8},{10,11... | collective-permute-start | bytes 1572872 | tf_op jit(solution)/shard_map/ppermute | solution.py:460
  33.6 2.7 %collective-permute-start.6 = (bf16[128,1024]{1,0:T(8,128)(2,1)S(1)}, bf16[128,1024]{1,0:T(8,128)(2,1)S(1)}, u32[]{:S(2)}, u32[]{:S(2)}) collective-permute-start(bf16[128,1024]{1,0:T(8,128)(2,1)S(1)} %join.1.refs_1_), channel_id=1, source_target_pairs={{0,1},{1,0},{2,3},{3,2},{4,5},{5,4},{6,7},{7,6},{8,9},{9,8},{10,11... | collective-permute-start | bytes 786440 | tf_op jit(solution)/shard_map/ppermute | solution.py:460
  34.6 1.7 %copy-start = (bf16[256,1024]{1,0:T(8,128)(2,1)S(1)}, bf16[256,1024]{1,0:T(8,128)(2,1)}, u32[]{:S(2)}) copy-start(bf16[256,1024]{1,0:T(8,128)(2,1)} %refs_1_.3) | copy-start | bytes 1572868
  38.2 2.1 %collective-permute-start.12 = (bf16[4,256,256]{2,1,0:T(8,128)(2,1)S(1)}, bf16[4,256,256]{2,1,0:T(8,128)(2,1)S(1)}, u32[]{:S(2)}, u32[]{:S(2)}) collective-permute-start(bf16[4,256,256]{2,1,0:T(8,128)(2,1)S(1)} %get-tuple-element.30), channel_id=1, source_target_pairs={{0,1},{1,0},{2,3},{3,2},{4,5},{5,4},{6,7},{7,6},{8,9},{9,8},{10,11... | collective-permute-start | bytes 1572872 | tf_op jit(solution)/shard_map/ppermute | solution.py:460
  41.2 21.3 %all-to-all-start.1 = ((bf16[4,256,256]{2,1,0:T(8,128)(2,1)}), bf16[4,256,256]{2,1,0:T(8,128)(2,1)S(1)}, u32[]{:S(2)}, u32[]{:S(2)}) async-start(bf16[4,256,256]{2,1,0:T(8,128)(2,1)} %add.1.refs_6_), calls=%async_computation.1 | async-start | bytes 1048576 | tf_op jit(solution)/shard_map/all_to_all | solution.py:464
  46.8 1.6 %collective-permute-start.16 = (bf16[128,1024]{1,0:T(8,128)(2,1)S(1)}, bf16[128,1024]{1,0:T(8,128)(2,1)S(1)}, u32[]{:S(2)}, u32[]{:S(2)}) collective-permute-start(bf16[128,1024]{1,0:T(8,128)(2,1)S(1)} %get-tuple-element.34), channel_id=1, source_target_pairs={{0,1},{1,0},{2,3},{3,2},{4,5},{5,4},{6,7},{7,6},{8,9},{9,8},{10,11... | collective-permute-start | bytes 786440 | tf_op jit(solution)/shard_map/ppermute | solution.py:460
  48.5 4.4 %collective-permute-start.17 = (bf16[32,1024]{1,0:T(8,128)(2,1)S(1)}, bf16[32,1024]{1,0:T(8,128)(2,1)S(1)}, u32[]{:S(2)}, u32[]{:S(2)}) collective-permute-start(bf16[32,1024]{1,0:T(8,128)(2,1)S(1)} %get-tuple-element.36), channel_id=1, source_target_pairs={{0,8},{8,0},{16,24},{24,16},{1,9},{9,1},{17,25},{25,17},{2,10},{10... | collective-permute-start | bytes 196616 | tf_op jit(solution)/shard_map/ppermute | solution.py:454
  50.5 5.0 %collective-permute-start.18 = (bf16[32,1024]{1,0:T(8,128)(2,1)S(1)}, bf16[32,1024]{1,0:T(8,128)(2,1)S(1)}, u32[]{:S(2)}, u32[]{:S(2)}) collective-permute-start(bf16[32,1024]{1,0:T(8,128)(2,1)S(1)} %get-tuple-element.37), channel_id=1, source_target_pairs={{0,16},{8,24},{16,0},{24,8},{1,17},{9,25},{17,1},{25,9},{2,18},{10... | collective-permute-start | bytes 196616 | tf_op jit(solution)/shard_map/ppermute | solution.py:454
  51.0 5.2 %collective-permute-start.19 = (bf16[32,1024]{1,0:T(8,128)(2,1)S(1)}, bf16[32,1024]{1,0:T(8,128)(2,1)S(1)}, u32[]{:S(2)}, u32[]{:S(2)}) collective-permute-start(bf16[32,1024]{1,0:T(8,128)(2,1)S(1)} %get-tuple-element.38), channel_id=1, source_target_pairs={{0,24},{8,16},{16,8},{24,0},{1,25},{9,17},{17,9},{25,1},{2,26},{10... | collective-permute-start | bytes 196616 | tf_op jit(solution)/shard_map/ppermute | solution.py:454
  56.2 9.9 %collective-permute-start.20 = (bf16[32,1024]{1,0:T(8,128)(2,1)S(1)}, bf16[32,1024]{1,0:T(8,128)(2,1)S(1)}, u32[]{:S(2)}, u32[]{:S(2)}) collective-permute-start(bf16[32,1024]{1,0:T(8,128)(2,1)S(1)} %get-tuple-element.40), channel_id=1, source_target_pairs={{0,2},{1,3},{2,0},{3,1},{4,6},{5,7},{6,4},{7,5},{8,10},{9,11},{10,... | collective-permute-start | bytes 196616 | tf_op jit(solution)/shard_map/ppermute | solution.py:457
  58.3 8.4 %collective-permute-start.21 = (bf16[32,1024]{1,0:T(8,128)(2,1)S(1)}, bf16[32,1024]{1,0:T(8,128)(2,1)S(1)}, u32[]{:S(2)}, u32[]{:S(2)}) collective-permute-start(bf16[32,1024]{1,0:T(8,128)(2,1)S(1)} %get-tuple-element.41), channel_id=1, source_target_pairs={{0,4},{1,5},{2,6},{3,7},{4,0},{5,1},{6,2},{7,3},{8,12},{9,13},{10,... | collective-permute-start | bytes 196616 | tf_op jit(solution)/shard_map/ppermute | solution.py:457
  60.7 6.1 %collective-permute-start.22 = (bf16[32,1024]{1,0:T(8,128)(2,1)S(1)}, bf16[32,1024]{1,0:T(8,128)(2,1)S(1)}, u32[]{:S(2)}, u32[]{:S(2)}) collective-permute-start(bf16[32,1024]{1,0:T(8,128)(2,1)S(1)} %get-tuple-element.42), channel_id=1, source_target_pairs={{0,6},{1,7},{2,4},{3,5},{4,2},{5,3},{6,0},{7,1},{8,14},{9,15},{10,... | collective-permute-start | bytes 196616 | tf_op jit(solution)/shard_map/ppermute | solution.py:457
  62.5 9.3 %copy-start.2 = (f32[256,1024]{1,0:T(8,128)S(1)}, f32[256,1024]{1,0:T(8,128)}, u32[]{:S(2)}) copy-start(f32[256,1024]{1,0:T(8,128)} %refs_0_.5) | copy-start | bytes 3145732
  62.6 7.5 %collective-permute-start.15 = (bf16[256,256]{1,0:T(8,128)(2,1)S(1)}, bf16[256,256]{1,0:T(8,128)(2,1)S(1)}, u32[]{:S(2)}, u32[]{:S(2)}) collective-permute-start(bf16[256,256]{1,0:T(8,128)(2,1)S(1)} %sum_rows.1.refs_2_.refs_4_), channel_id=1, source_target_pairs={{0,24},{8,16},{16,8},{24,0},{1,25},{9,17},{17,9},{25,1},{2,26},{10... | collective-permute-start | bytes 393224 | tf_op jit(solution)/shard_map/ppermute | solution.py:454
  66.0 5.8 %collective-permute-start.14 = (bf16[256,256]{1,0:T(8,128)(2,1)S(1)}, bf16[256,256]{1,0:T(8,128)(2,1)S(1)}, u32[]{:S(2)}, u32[]{:S(2)}) collective-permute-start(bf16[256,256]{1,0:T(8,128)(2,1)S(1)} %sum_rows.1.refs_2_.refs_4_), channel_id=1, source_target_pairs={{0,16},{8,24},{16,0},{24,8},{1,17},{9,25},{17,1},{25,9},{2,18},{10... | collective-permute-start | bytes 393224 | tf_op jit(solution)/shard_map/ppermute | solution.py:454
  66.1 5.8 %collective-permute-start.13 = (bf16[256,256]{1,0:T(8,128)(2,1)S(1)}, bf16[256,256]{1,0:T(8,128)(2,1)S(1)}, u32[]{:S(2)}, u32[]{:S(2)}) collective-permute-start(bf16[256,256]{1,0:T(8,128)(2,1)S(1)} %sum_rows.1.refs_2_.refs_4_), channel_id=1, source_target_pairs={{0,8},{8,0},{16,24},{24,16},{1,9},{9,1},{17,25},{25,17},{2,10},{10... | collective-permute-start | bytes 393224 | tf_op jit(solution)/shard_map/ppermute | solution.py:454
  66.8 5.1 %copy-start.9 = (f32[256]{0:T(256)S(1)}, f32[256]{0:T(256)}, u32[]{:S(2)}) copy-start(f32[256]{0:T(256)} %param.10) | copy-start | bytes 3076
  66.8 6.4 %collective-permute-start.25 = (bf16[32,1024]{1,0:T(8,128)(2,1)S(1)}, bf16[32,1024]{1,0:T(8,128)(2,1)S(1)}, u32[]{:S(2)}, u32[]{:S(2)}) collective-permute-start(bf16[32,1024]{1,0:T(8,128)(2,1)S(1)} %sum_parts.1.refs_0_), channel_id=1, source_target_pairs={{0,24},{8,16},{16,8},{24,0},{1,25},{9,17},{17,9},{25,1},{2,26},{10... | collective-permute-start | bytes 196616 | tf_op jit(solution)/shard_map/ppermute | solution.py:454
  69.7 4.3 %collective-permute-start.24 = (bf16[32,1024]{1,0:T(8,128)(2,1)S(1)}, bf16[32,1024]{1,0:T(8,128)(2,1)S(1)}, u32[]{:S(2)}, u32[]{:S(2)}) collective-permute-start(bf16[32,1024]{1,0:T(8,128)(2,1)S(1)} %sum_parts.1.refs_0_), channel_id=1, source_target_pairs={{0,16},{8,24},{16,0},{24,8},{1,17},{9,25},{17,1},{25,9},{2,18},{10... | collective-permute-start | bytes 196616 | tf_op jit(solution)/shard_map/ppermute | solution.py:454
  70.0 4.3 %collective-permute-start.23 = (bf16[32,1024]{1,0:T(8,128)(2,1)S(1)}, bf16[32,1024]{1,0:T(8,128)(2,1)S(1)}, u32[]{:S(2)}, u32[]{:S(2)}) collective-permute-start(bf16[32,1024]{1,0:T(8,128)(2,1)S(1)} %sum_parts.1.refs_0_), channel_id=1, source_target_pairs={{0,8},{8,0},{16,24},{24,16},{1,9},{9,1},{17,25},{25,17},{2,10},{10... | collective-permute-start | bytes 196616 | tf_op jit(solution)/shard_map/ppermute | solution.py:454
  73.2 1.1 %copy-start.5 = (f32[1,256]{1,0:T(1,128)S(1)}, f32[1,256]{1,0:T(1,128)}, u32[]{:S(2)}) copy-start(f32[1,256]{1,0:T(1,128)} %get-tuple-element.32.refs_4_) | copy-start | bytes 3076

commit v7 on v6

--- a/solution.py
+++ b/solution.py
@@ -432,13 +432,14 @@
     rows, width = table.shape
     cols = width // len(parts)
     for m, p in enumerate(parts):
-        grad[:, aligned(me[0] ^ m, cols)] = p[...].astype(F32)
-    mean = jnp.sum(grad[...] * grad[...], axis=1, keepdims=True) * (1.0 / width)
+        grad[:, aligned(me[0] ^ m, cols)] = p[...]
+    g = grad[...].astype(F32)
+    mean = jnp.sum(g * g, axis=1, keepdims=True) * (1.0 / width)
     same = iota((rows, rows), 0) == iota((rows, rows), 1)
     old = jnp.sum(jnp.where(same, accum[...], 0.0), axis=1, keepdims=True)
     fresh = old + mean
     new_accum[...] = jnp.sum(jnp.where(same, fresh, 0.0), axis=0, keepdims=True)
-    new_table[...] = table[...] - grad[...] / (jnp.sqrt(fresh) + 1e-08)
+    new_table[...] = table[...] - g / (jnp.sqrt(fresh) + 1e-08)
 
 
 def body(table, accum, owner, local_row, lengths, queries, keys, cotangent, out_weight):
@@ -599,7 +600,7 @@
         (table, accum.reshape(1, rows), *grads),
         cost=UPDATE_COST,
         placed=True,
-        scratch=[pltpu.VMEM((rows, width), F32)],
+        scratch=[pltpu.VMEM((rows, width), BF16)],
     )
     weight_grad = call(
         place_kernel, "place", sds((n * part, width)), wsums, after=(new_accum,), placed=True

time: 75.3 us -> 75.3 us (level)
  no operation moved by 1% of the time
where the time goes in v7:
time: 75.3 us; the launch traced here: 75 us
  starting transfers between devices  41.6 us (55%)
  waiting for transfers between devices  19.5 us (26%)
  Pallas kernels  12.3 us (16%)
  between operations  0.88 us (1%)
    ppermute x16, starting transfers between devices, column(): lax.ppermute(x, 'replica', [(i, i ^ m) for i in range(n)])  23.6 us
    pallas_call x20, Pallas kernels, call(): pl.pallas_call(run, out_shape=out, in_specs=[SMEM if i < smem else HBM if...  12.3 us
    ppermute x16, waiting for transfers between devices, column(): lax.ppermute(x, 'replica', [(i, i ^ m) for i in range(n)])  9.05 us
    ppermute x6, starting transfers between devices, along(): lax.ppermute(x, 'shard', [(i, i ^ 2 * m) for i in range(shards)])  8.98 us
    ppermute x6, waiting for transfers between devices, along(): lax.ppermute(x, 'shard', [(i, i ^ 2 * m) for i in range(shards)])  6.42 us
    all_to_all x1, starting transfers between devices, swap_along(): lax.all_to_all(x, 'shard', 0, 0, tiled=True, axis_index_groups=groups)  4.79 us
    all_to_all x1, starting transfers between devices, swap_columns(): return lax.all_to_all(x, 'replica', 0, 0, tiled=True)  3.49 us
    ppermute x4, waiting for transfers between devices, core(): return lax.ppermute(x, 'shard', [(i, i ^ 1) for i in range(shards)])  2.29 us
  transfers between devices with their start and end apart: 28, of which 17 were waited for; matrix products, arithmetic and copies ran while one was open for 0% of the time, Pallas kernels for 12%

profile of v7, /device:TPU:0, one launch (start us, length us, event | category | flops | bytes accessed | tf_op | source)
XLA Modules:
  0.0 75.0 jit_solution(11138046325149798121)
XLA Ops:
  0.7 3.0 %collective-permute-start.8 = (bf16[256,1024]{1,0:T(8,128)(2,1)}, bf16[256,1024]{1,0:T(8,128)(2,1)S(1)}, u32[]{:S(2)}, u32[]{:S(2)}) collective-permute-start(bf16[256,1024]{1,0:T(8,128)(2,1)} %refs_1_.3), channel_id=1, source_target_pairs={{0,16},{8,24},{16,0},{24,8},{1,17},{9,25},{17,1},{25,9},{2,18},{10... | collective-permute-start | bytes 1572872 | tf_op jit(solution)/shard_map/ppermute | solution.py:455
  3.7 1.5 %collective-permute-start.7 = (bf16[256,1024]{1,0:T(8,128)(2,1)}, bf16[256,1024]{1,0:T(8,128)(2,1)S(1)}, u32[]{:S(2)}, u32[]{:S(2)}) collective-permute-start(bf16[256,1024]{1,0:T(8,128)(2,1)} %refs_1_.3), channel_id=1, source_target_pairs={{0,8},{8,0},{16,24},{24,16},{1,9},{9,1},{17,25},{25,17},{2,10},{10... | collective-permute-start | bytes 1572872 | tf_op jit(solution)/shard_map/ppermute | solution.py:455
  5.2 1.7 %carry.1.refs_0_ = bf16[384,256]{1,0:T(8,128)(2,1)} custom-call(bf16[128,1024]{1,0:T(8,128)(2,1)} %refs_0_.4, f32[256,1024]{1,0:T(8,128)} %refs_0_.5), custom_call_target="tpu_custom_call" | custom-call | tf_op jit(solution)/shard_map/carry/pallas_call | solution.py:169
  6.9 3.7 %collective-permute-start.2 = (bf16[384,256]{1,0:T(8,128)(2,1)}, bf16[384,256]{1,0:T(8,128)(2,1)S(1)}, u32[]{:S(2)}, u32[]{:S(2)}) collective-permute-start(bf16[384,256]{1,0:T(8,128)(2,1)} %carry.1.refs_0_), channel_id=1, source_target_pairs={{0,6},{1,7},{2,4},{3,5},{4,2},{5,3},{6,0},{7,1},{8,14},{9,15},{10,... | collective-permute-start | bytes 589832 | tf_op jit(solution)/shard_map/ppermute | solution.py:458
  10.5 0.8 %collective-permute-start = (bf16[384,256]{1,0:T(8,128)(2,1)}, bf16[384,256]{1,0:T(8,128)(2,1)S(1)}, u32[]{:S(2)}, u32[]{:S(2)}) collective-permute-start(bf16[384,256]{1,0:T(8,128)(2,1)} %carry.1.refs_0_), channel_id=1, source_target_pairs={{0,2},{1,3},{2,0},{3,1},{4,6},{5,7},{6,4},{7,5},{8,10},{9,11},{10,... | collective-permute-start | bytes 589832 | tf_op jit(solution)/shard_map/ppermute | solution.py:458
  11.3 0.7 copy-done.6
  12.0 1.4 %pack.1 = bf16[4,544,128]{2,1,0:T(8,128)(2,1)} custom-call(s32[1,4]{1,0:T(1,128)S(1)} %copy-done.8, s32[1,256]{1,0:T(1,128)S(1)} %bitcast.5, s32[1,256]{1,0:T(1,128)S(1)} %bitcast.6, bf16[256,512]{1,0:T(8,128)(2,1)S(1)} %copy-done.3, bf16[256,512]{1,0:T(8,128)(2,1)S(1)} %copy-done.4), custom_call_target="tpu_custom_call" | custom-call | tf_op jit(solution)/shard_map/pack/pallas_call | solution.py:169
  13.4 3.5 %all-to-all-start = ((bf16[4,544,128]{2,1,0:T(8,128)(2,1)}), bf16[4,544,128]{2,1,0:T(8,128)(2,1)S(1)}, u32[]{:S(2)}, u32[]{:S(2)}) async-start(bf16[4,544,128]{2,1,0:T(8,128)(2,1)} %pack.1), calls=%async_computation | async-start | bytes 1114112 | tf_op jit(solution)/shard_map/all_to_all | solution.py:468
  16.9 0.3 collective-permute-done.7.refs_0_.refs_5_.refs_2_
  17.3 1.7 %collective-permute-start.10 = (bf16[128,1024]{1,0:T(8,128)(2,1)S(1)}, bf16[128,1024]{1,0:T(8,128)(2,1)S(1)}, u32[]{:S(2)}, u32[]{:S(2)}) collective-permute-start(bf16[128,1024]{1,0:T(8,128)(2,1)S(1)} %get-tuple-element.28), channel_id=1, source_target_pairs={{0,16},{8,24},{16,0},{24,8},{1,17},{9,25},{17,1},{25,9},{2,18},{10... | collective-permute-start | bytes 786440 | tf_op jit(solution)/shard_map/ppermute | solution.py:455
  19.1 1.5 %collective-permute-start.9 = (bf16[128,1024]{1,0:T(8,128)(2,1)S(1)}, bf16[128,1024]{1,0:T(8,128)(2,1)S(1)}, u32[]{:S(2)}, u32[]{:S(2)}) collective-permute-start(bf16[128,1024]{1,0:T(8,128)(2,1)S(1)} %get-tuple-element.27.refs_1_), channel_id=1, source_target_pairs={{0,8},{8,0},{16,24},{24,16},{1,9},{9,1},{17,25},{25,17},{2,10},{10... | collective-permute-start | bytes 786440 | tf_op jit(solution)/shard_map/ppermute | solution.py:455
  20.5 6.3 %collective-permute-done.1.refs_2_ = bf16[384,256]{1,0:T(8,128)(2,1)S(1)} collective-permute-done((bf16[384,256]{1,0:T(8,128)(2,1)}, bf16[384,256]{1,0:T(8,128)(2,1)S(1)}, u32[]{:S(2)}, u32[]{:S(2)}) %collective-permute-start.1) | collective-permute-done | bytes 196640 | tf_op jit(solution)/shard_map/ppermute | solution.py:458
  26.9 1.4 %collective-permute-start.3 = (bf16[128,256]{1,0:T(8,128)(2,1)S(1)}, bf16[128,256]{1,0:T(8,128)(2,1)S(1)}, u32[]{:S(2)}, u32[]{:S(2)}) collective-permute-start(bf16[128,256]{1,0:T(8,128)(2,1)S(1)} %get-tuple-element.24), channel_id=1, source_target_pairs={{0,8},{8,0},{16,24},{24,16},{1,9},{9,1},{17,25},{25,17},{2,10},{10... | collective-permute-start | bytes 196616 | tf_op jit(solution)/shard_map/ppermute | solution.py:455
  28.3 2.1 %collective-permute-start.5 = (bf16[128,256]{1,0:T(8,128)(2,1)S(1)}, bf16[128,256]{1,0:T(8,128)(2,1)S(1)}, u32[]{:S(2)}, u32[]{:S(2)}) collective-permute-start(bf16[128,256]{1,0:T(8,128)(2,1)S(1)} %get-tuple-element.26), channel_id=1, source_target_pairs={{0,24},{8,16},{16,8},{24,0},{1,25},{9,17},{17,9},{25,1},{2,26},{10... | collective-permute-start | bytes 196616 | tf_op jit(solution)/shard_map/ppermute | solution.py:455
  30.5 1.5 %collective-permute-done.3.refs_1_ = bf16[128,256]{1,0:T(8,128)(2,1)S(1)} collective-permute-done((bf16[128,256]{1,0:T(8,128)(2,1)S(1)}, bf16[128,256]{1,0:T(8,128)(2,1)S(1)}, u32[]{:S(2)}, u32[]{:S(2)}) %collective-permute-start.3) | collective-permute-done | bytes 65568 | tf_op jit(solution)/shard_map/ppermute | solution.py:455
  32.0 0.6 collective-permute-done.4.refs_2_
  32.6 1.0 %collective-permute-done.5.refs_3_ = bf16[128,256]{1,0:T(8,128)(2,1)S(1)} collective-permute-done((bf16[128,256]{1,0:T(8,128)(2,1)S(1)}, bf16[128,256]{1,0:T(8,128)(2,1)S(1)}, u32[]{:S(2)}, u32[]{:S(2)}) %collective-permute-start.5) | collective-permute-done | bytes 65568 | tf_op jit(solution)/shard_map/ppermute | solution.py:455
  33.7 0.8 %weights.1.refs_1_.refs_3_ = bf16[4,2,256,256]{3,2,1,0:T(8,128)(2,1)S(1)} custom-call(bf16[4,544,128]{2,1,0:T(8,128)(2,1)S(1)} %all-to-all-done.refs_4_.refs_0_, bf16[128,1024]{1,0:T(8,128)(2,1)S(1)} %get-tuple-element.27.refs_1_), custom_call_target="tpu_custom_call" | custom-call | tf_op jit(solution)/shard_map/weights/pallas_call | solution.py:169
  34.6 1.7 %mix.1.refs_10_.refs_0_ = bf16[256,1024]{1,0:T(8,128)(2,1)S(1)} custom-call(bf16[4,544,128]{2,1,0:T(8,128)(2,1)S(1)} %all-to-all-done.refs_4_.refs_0_, bf16[4,2,256,256]{3,2,1,0:T(8,128)(2,1)S(1)} %weights.1.refs_1_.refs_3_, bf16[4,256,256]{2,1,0:T(8,128)(2,1)S(1)} %stack.1.refs_2_, bf16[4,256,256]{2,1,0:T(8,128)(2,1)S(1)} %collective-permute-done.11.refs_3_), custom_call_target="tpu_custom_call" | custom-call | tf_op jit(solution)/shard_map/mix/pallas_call | solution.py:169
  36.3 1.8 %back.1 = (bf16[4,256,256]{2,1,0:T(8,128)(2,1)S(1)}, bf16[1024,256]{1,0:T(8,128)(2,1)S(1)}) custom-call(bf16[4,544,128]{2,1,0:T(8,128)(2,1)S(1)} %all-to-all-done.refs_4_.refs_0_, bf16[128,1024]{1,0:T(8,128)(2,1)S(1)} %join.1.refs_1_, bf16[128,1024]{1,0:T(8,128)(2,1)S(1)} %collective-permute-done.6.refs_2_, ...), custom_call_target="tpu_custom_call" | custom-call | tf_op jit(solution)/shard_map/back/pallas_call | solution.py:169
  38.2 0.6 collective-permute-start.12
  38.7 0.7 keep.1.refs_0_
  39.5 0.8 %collective-permute-done.12.refs_1_ = bf16[4,256,256]{2,1,0:T(8,128)(2,1)S(1)} collective-permute-done((bf16[4,256,256]{2,1,0:T(8,128)(2,1)S(1)}, bf16[4,256,256]{2,1,0:T(8,128)(2,1)S(1)}, u32[]{:S(2)}, u32[]{:S(2)}) %collective-permute-start.12) | collective-permute-done | bytes 524320 | tf_op jit(solution)/shard_map/ppermute | solution.py:461
  40.3 0.9 %add.1.refs_6_ = bf16[4,256,256]{2,1,0:T(8,128)(2,1)} custom-call(f32[4,256,256]{2,1,0:T(8,128)S(1)} %keep.1.refs_0_, bf16[4,256,256]{2,1,0:T(8,128)(2,1)S(1)} %collective-permute-done.12.refs_1_), custom_call_target="tpu_custom_call" | custom-call | tf_op jit(solution)/shard_map/add/pallas_call | solution.py:169
  41.2 4.8 %all-to-all-start.1 = ((bf16[4,256,256]{2,1,0:T(8,128)(2,1)}), bf16[4,256,256]{2,1,0:T(8,128)(2,1)S(1)}, u32[]{:S(2)}, u32[]{:S(2)}) async-start(bf16[4,256,256]{2,1,0:T(8,128)(2,1)} %add.1.refs_6_), calls=%async_computation.1 | async-start | bytes 1048576 | tf_op jit(solution)/shard_map/all_to_all | solution.py:465
  45.9 0.9 %wgrad.1 = (f32[128,1024]{1,0:T(8,128)S(1)}, bf16[128,1024]{1,0:T(8,128)(2,1)S(1)}) custom-call(bf16[256,1024]{1,0:T(8,128)(2,1)S(1)} %mix.1.refs_10_.refs_0_, bf16[256,1024]{1,0:T(8,128)(2,1)S(1)} %copy-done, bf16[256,1024]{1,0:T(8,128)(2,1)S(1)} %collective-permute-done.7.refs_0_.refs_5_.refs_2_, ...), custom_call_target="tpu_custom_call" | custom-call | tf_op jit(solution)/shard_map/wgrad/pallas_call | solution.py:169
  46.8 0.1 collective-permute-start.16
  46.9 1.5 %collective-permute-done.16.refs_1_ = bf16[128,1024]{1,0:T(8,128)(2,1)S(1)} collective-permute-done((bf16[128,1024]{1,0:T(8,128)(2,1)S(1)}, bf16[128,1024]{1,0:T(8,128)(2,1)S(1)}, u32[]{:S(2)}, u32[]{:S(2)}) %collective-permute-start.16) | collective-permute-done | bytes 262176 | tf_op jit(solution)/shard_map/ppermute | solution.py:461
  48.5 2.0 %collective-permute-start.17 = (bf16[32,1024]{1,0:T(8,128)(2,1)S(1)}, bf16[32,1024]{1,0:T(8,128)(2,1)S(1)}, u32[]{:S(2)}, u32[]{:S(2)}) collective-permute-start(bf16[32,1024]{1,0:T(8,128)(2,1)S(1)} %get-tuple-element.36), channel_id=1, source_target_pairs={{0,8},{8,0},{16,24},{24,16},{1,9},{9,1},{17,25},{25,17},{2,10},{10... | collective-permute-start | bytes 196616 | tf_op jit(solution)/shard_map/ppermute | solution.py:455
  50.5 0.6 collective-permute-start.18
  51.0 1.0 %collective-permute-start.19 = (bf16[32,1024]{1,0:T(8,128)(2,1)S(1)}, bf16[32,1024]{1,0:T(8,128)(2,1)S(1)}, u32[]{:S(2)}, u32[]{:S(2)}) collective-permute-start(bf16[32,1024]{1,0:T(8,128)(2,1)S(1)} %get-tuple-element.38), channel_id=1, source_target_pairs={{0,24},{8,16},{16,8},{24,0},{1,25},{9,17},{17,9},{25,1},{2,26},{10... | collective-permute-start | bytes 196616 | tf_op jit(solution)/shard_map/ppermute | solution.py:455
  52.0 0.8 %collective-permute-done.17.refs_1_ = bf16[32,1024]{1,0:T(8,128)(2,1)S(1)} collective-permute-done((bf16[32,1024]{1,0:T(8,128)(2,1)S(1)}, bf16[32,1024]{1,0:T(8,128)(2,1)S(1)}, u32[]{:S(2)}, u32[]{:S(2)}) %collective-permute-start.17) | collective-permute-done | bytes 65568 | tf_op jit(solution)/shard_map/ppermute | solution.py:455
  52.9 2.6 %collective-permute-done.18.refs_2_ = bf16[32,1024]{1,0:T(8,128)(2,1)S(1)} collective-permute-done((bf16[32,1024]{1,0:T(8,128)(2,1)S(1)}, bf16[32,1024]{1,0:T(8,128)(2,1)S(1)}, u32[]{:S(2)}, u32[]{:S(2)}) %collective-permute-start.18) | collective-permute-done | bytes 65568 | tf_op jit(solution)/shard_map/ppermute | solution.py:455
  55.4 0.8 %collective-permute-done.19.refs_3_ = bf16[32,1024]{1,0:T(8,128)(2,1)S(1)} collective-permute-done((bf16[32,1024]{1,0:T(8,128)(2,1)S(1)}, bf16[32,1024]{1,0:T(8,128)(2,1)S(1)}, u32[]{:S(2)}, u32[]{:S(2)}) %collective-permute-start.19) | collective-permute-done | bytes 65568 | tf_op jit(solution)/shard_map/ppermute | solution.py:455
  56.2 2.1 %collective-permute-start.20 = (bf16[32,1024]{1,0:T(8,128)(2,1)S(1)}, bf16[32,1024]{1,0:T(8,128)(2,1)S(1)}, u32[]{:S(2)}, u32[]{:S(2)}) collective-permute-start(bf16[32,1024]{1,0:T(8,128)(2,1)S(1)} %get-tuple-element.40), channel_id=1, source_target_pairs={{0,2},{1,3},{2,0},{3,1},{4,6},{5,7},{6,4},{7,5},{8,10},{9,11},{10,... | collective-permute-start | bytes 196616 | tf_op jit(solution)/shard_map/ppermute | solution.py:458
  58.3 2.4 %collective-permute-start.21 = (bf16[32,1024]{1,0:T(8,128)(2,1)S(1)}, bf16[32,1024]{1,0:T(8,128)(2,1)S(1)}, u32[]{:S(2)}, u32[]{:S(2)}) collective-permute-start(bf16[32,1024]{1,0:T(8,128)(2,1)S(1)} %get-tuple-element.41), channel_id=1, source_target_pairs={{0,4},{1,5},{2,6},{3,7},{4,0},{5,1},{6,2},{7,3},{8,12},{9,13},{10,... | collective-permute-start | bytes 196616 | tf_op jit(solution)/shard_map/ppermute | solution.py:458
  60.8 1.7 %all-to-all-done.1.refs_0_ = bf16[4,256,256]{2,1,0:T(8,128)(2,1)S(1)} async-done(((bf16[4,256,256]{2,1,0:T(8,128)(2,1)}), bf16[4,256,256]{2,1,0:T(8,128)(2,1)S(1)}, u32[]{:S(2)}, u32[]{:S(2)}) %all-to-all-start.1) | async-done | bytes 524320 | tf_op jit(solution)/shard_map/all_to_all | solution.py:465
  62.6 3.5 %collective-permute-start.15 = (bf16[256,256]{1,0:T(8,128)(2,1)S(1)}, bf16[256,256]{1,0:T(8,128)(2,1)S(1)}, u32[]{:S(2)}, u32[]{:S(2)}) collective-permute-start(bf16[256,256]{1,0:T(8,128)(2,1)S(1)} %sum_rows.1.refs_2_.refs_4_), channel_id=1, source_target_pairs={{0,24},{8,16},{16,8},{24,0},{1,25},{9,17},{17,9},{25,1},{2,26},{10... | collective-permute-start | bytes 393224 | tf_op jit(solution)/shard_map/ppermute | solution.py:455
  66.1 0.6 collective-permute-start.13
  66.8 2.9 %collective-permute-start.25 = (bf16[32,1024]{1,0:T(8,128)(2,1)S(1)}, bf16[32,1024]{1,0:T(8,128)(2,1)S(1)}, u32[]{:S(2)}, u32[]{:S(2)}) collective-permute-start(bf16[32,1024]{1,0:T(8,128)(2,1)S(1)} %sum_parts.1.refs_0_), channel_id=1, source_target_pairs={{0,24},{8,16},{16,8},{24,0},{1,25},{9,17},{17,9},{25,1},{2,26},{10... | collective-permute-start | bytes 196616 | tf_op jit(solution)/shard_map/ppermute | solution.py:455
  69.7 0.3 collective-permute-start.24
  69.9 0.1 collective-permute-done.15.refs_5_
  70.0 1.6 %collective-permute-start.23 = (bf16[32,1024]{1,0:T(8,128)(2,1)S(1)}, bf16[32,1024]{1,0:T(8,128)(2,1)S(1)}, u32[]{:S(2)}, u32[]{:S(2)}) collective-permute-start(bf16[32,1024]{1,0:T(8,128)(2,1)S(1)} %sum_parts.1.refs_0_), channel_id=1, source_target_pairs={{0,8},{8,0},{16,24},{24,16},{1,9},{9,1},{17,25},{25,17},{2,10},{10... | collective-permute-start | bytes 196616 | tf_op jit(solution)/shard_map/ppermute | solution.py:455
  71.6 0.2 collective-permute-done.14.refs_4_
  71.9 1.3 %update.1 = (f32[256,1024]{1,0:T(8,128)}, f32[1,256]{1,0:T(1,128)}) custom-call(f32[256,1024]{1,0:T(8,128)S(1)} %copy-done.2, f32[1,256]{1,0:T(1,128)S(1)} %bitcast.7, bf16[256,256]{1,0:T(8,128)(2,1)S(1)} %sum_rows.1.refs_2_.refs_4_, bf16[256,256]{1,0:T(8,128)(2,1)S(1)} %collective-permute-done.13.refs_3_, ...), custom_call_target="tpu_custom_call" | custom-call | flops 8000000000 | tf_op jit(solution)/shard_map/update/pallas_call | solution.py:169
  73.2 0.7 collective-permute-done.24.refs_2_
  73.9 0.4 collective-permute-done.23.refs_1_
  74.3 0.7 place.1
  (48 shorter events, 0.8 us)
Async XLA Ops:
  0.6 10.7 %copy-start.4 = (bf16[256,512]{1,0:T(8,128)(2,1)S(1)}, bf16[256,512]{1,0:T(8,128)(2,1)}, u32[]{:S(2)}) copy-start(bf16[256,512]{1,0:T(8,128)(2,1)} %refs_4_.2) | copy-start | bytes 786436
  0.6 10.7 %copy-start.3 = (bf16[256,512]{1,0:T(8,128)(2,1)S(1)}, bf16[256,512]{1,0:T(8,128)(2,1)}, u32[]{:S(2)}) copy-start(bf16[256,512]{1,0:T(8,128)(2,1)} %refs_3_.1) | copy-start | bytes 786436
  0.7 16.3 %collective-permute-start.8 = (bf16[256,1024]{1,0:T(8,128)(2,1)}, bf16[256,1024]{1,0:T(8,128)(2,1)S(1)}, u32[]{:S(2)}, u32[]{:S(2)}) collective-permute-start(bf16[256,1024]{1,0:T(8,128)(2,1)} %refs_1_.3), channel_id=1, source_target_pairs={{0,16},{8,24},{16,0},{24,8},{1,17},{9,25},{17,1},{25,9},{2,18},{10... | collective-permute-start | bytes 1572872 | tf_op jit(solution)/shard_map/ppermute | solution.py:455
  3.7 13.6 %collective-permute-start.7 = (bf16[256,1024]{1,0:T(8,128)(2,1)}, bf16[256,1024]{1,0:T(8,128)(2,1)S(1)}, u32[]{:S(2)}, u32[]{:S(2)}) collective-permute-start(bf16[256,1024]{1,0:T(8,128)(2,1)} %refs_1_.3), channel_id=1, source_target_pairs={{0,8},{8,0},{16,24},{24,16},{1,9},{9,1},{17,25},{25,17},{2,10},{10... | collective-permute-start | bytes 1572872 | tf_op jit(solution)/shard_map/ppermute | solution.py:455
  5.2 6.1 %copy-start.7 = (s32[256]{0:T(256)S(1)}, s32[256]{0:T(256)}, u32[]{:S(2)}) copy-start(s32[256]{0:T(256)} %param.12) | copy-start | bytes 3076
  6.9 13.7 %collective-permute-start.2 = (bf16[384,256]{1,0:T(8,128)(2,1)}, bf16[384,256]{1,0:T(8,128)(2,1)S(1)}, u32[]{:S(2)}, u32[]{:S(2)}) collective-permute-start(bf16[384,256]{1,0:T(8,128)(2,1)} %carry.1.refs_0_), channel_id=1, source_target_pairs={{0,6},{1,7},{2,4},{3,5},{4,2},{5,3},{6,0},{7,1},{8,14},{9,15},{10,... | collective-permute-start | bytes 589832 | tf_op jit(solution)/shard_map/ppermute | solution.py:458
  10.5 16.3 %collective-permute-start.1 = (bf16[384,256]{1,0:T(8,128)(2,1)}, bf16[384,256]{1,0:T(8,128)(2,1)S(1)}, u32[]{:S(2)}, u32[]{:S(2)}) collective-permute-start(bf16[384,256]{1,0:T(8,128)(2,1)} %carry.1.refs_0_), channel_id=1, source_target_pairs={{0,4},{1,5},{2,6},{3,7},{4,0},{5,1},{6,2},{7,3},{8,12},{9,13},{10,... | collective-permute-start | bytes 589832 | tf_op jit(solution)/shard_map/ppermute | solution.py:458
  10.5 16.3 %collective-permute-start = (bf16[384,256]{1,0:T(8,128)(2,1)}, bf16[384,256]{1,0:T(8,128)(2,1)S(1)}, u32[]{:S(2)}, u32[]{:S(2)}) collective-permute-start(bf16[384,256]{1,0:T(8,128)(2,1)} %carry.1.refs_0_), channel_id=1, source_target_pairs={{0,2},{1,3},{2,0},{3,1},{4,6},{5,7},{6,4},{7,5},{8,10},{9,11},{10,... | collective-permute-start | bytes 589832 | tf_op jit(solution)/shard_map/ppermute | solution.py:458
  11.3 0.7 copy-start.6
  11.3 0.7 copy-start.8
  13.4 13.4 %all-to-all-start = ((bf16[4,544,128]{2,1,0:T(8,128)(2,1)}), bf16[4,544,128]{2,1,0:T(8,128)(2,1)S(1)}, u32[]{:S(2)}, u32[]{:S(2)}) async-start(bf16[4,544,128]{2,1,0:T(8,128)(2,1)} %pack.1), calls=%async_computation | async-start | bytes 1114112 | tf_op jit(solution)/shard_map/all_to_all | solution.py:468
  16.9 9.9 %copy-start.1 = (bf16[384,256]{1,0:T(8,128)(2,1)S(1)}, bf16[384,256]{1,0:T(8,128)(2,1)}, u32[]{:S(2)}) copy-start(bf16[384,256]{1,0:T(8,128)(2,1)} %carry.1.refs_0_) | copy-start | bytes 589828
  17.3 17.2 %collective-permute-start.10 = (bf16[128,1024]{1,0:T(8,128)(2,1)S(1)}, bf16[128,1024]{1,0:T(8,128)(2,1)S(1)}, u32[]{:S(2)}, u32[]{:S(2)}) collective-permute-start(bf16[128,1024]{1,0:T(8,128)(2,1)S(1)} %get-tuple-element.28), channel_id=1, source_target_pairs={{0,16},{8,24},{16,0},{24,8},{1,17},{9,25},{17,1},{25,9},{2,18},{10... | collective-permute-start | bytes 786440 | tf_op jit(solution)/shard_map/ppermute | solution.py:455
  19.1 15.5 %collective-permute-start.9 = (bf16[128,1024]{1,0:T(8,128)(2,1)S(1)}, bf16[128,1024]{1,0:T(8,128)(2,1)S(1)}, u32[]{:S(2)}, u32[]{:S(2)}) collective-permute-start(bf16[128,1024]{1,0:T(8,128)(2,1)S(1)} %get-tuple-element.27.refs_1_), channel_id=1, source_target_pairs={{0,8},{8,0},{16,24},{24,16},{1,9},{9,1},{17,25},{25,17},{2,10},{10... | collective-permute-start | bytes 786440 | tf_op jit(solution)/shard_map/ppermute | solution.py:455
  26.9 5.1 %collective-permute-start.3 = (bf16[128,256]{1,0:T(8,128)(2,1)S(1)}, bf16[128,256]{1,0:T(8,128)(2,1)S(1)}, u32[]{:S(2)}, u32[]{:S(2)}) collective-permute-start(bf16[128,256]{1,0:T(8,128)(2,1)S(1)} %get-tuple-element.24), channel_id=1, source_target_pairs={{0,8},{8,0},{16,24},{24,16},{1,9},{9,1},{17,25},{25,17},{2,10},{10... | collective-permute-start | bytes 196616 | tf_op jit(solution)/shard_map/ppermute | solution.py:455
  28.3 4.3 %collective-permute-start.4 = (bf16[128,256]{1,0:T(8,128)(2,1)S(1)}, bf16[128,256]{1,0:T(8,128)(2,1)S(1)}, u32[]{:S(2)}, u32[]{:S(2)}) collective-permute-start(bf16[128,256]{1,0:T(8,128)(2,1)S(1)} %get-tuple-element.25), channel_id=1, source_target_pairs={{0,16},{8,24},{16,0},{24,8},{1,17},{9,25},{17,1},{25,9},{2,18},{10... | collective-permute-start | bytes 196616 | tf_op jit(solution)/shard_map/ppermute | solution.py:455
  28.3 5.3 %collective-permute-start.5 = (bf16[128,256]{1,0:T(8,128)(2,1)S(1)}, bf16[128,256]{1,0:T(8,128)(2,1)S(1)}, u32[]{:S(2)}, u32[]{:S(2)}) collective-permute-start(bf16[128,256]{1,0:T(8,128)(2,1)S(1)} %get-tuple-element.26), channel_id=1, source_target_pairs={{0,24},{8,16},{16,8},{24,0},{1,25},{9,17},{17,9},{25,1},{2,26},{10... | collective-permute-start | bytes 196616 | tf_op jit(solution)/shard_map/ppermute | solution.py:455
  32.0 2.6 %collective-permute-start.11 = (bf16[4,256,256]{2,1,0:T(8,128)(2,1)S(1)}, bf16[4,256,256]{2,1,0:T(8,128)(2,1)S(1)}, u32[]{:S(2)}, u32[]{:S(2)}) collective-permute-start(bf16[4,256,256]{2,1,0:T(8,128)(2,1)S(1)} %stack.1.refs_2_), channel_id=1, source_target_pairs={{0,1},{1,0},{2,3},{3,2},{4,5},{5,4},{6,7},{7,6},{8,9},{9,8},{10,11... | collective-permute-start | bytes 1572872 | tf_op jit(solution)/shard_map/ppermute | solution.py:461
  33.6 2.7 %collective-permute-start.6 = (bf16[128,1024]{1,0:T(8,128)(2,1)S(1)}, bf16[128,1024]{1,0:T(8,128)(2,1)S(1)}, u32[]{:S(2)}, u32[]{:S(2)}) collective-permute-start(bf16[128,1024]{1,0:T(8,128)(2,1)S(1)} %join.1.refs_1_), channel_id=1, source_target_pairs={{0,1},{1,0},{2,3},{3,2},{4,5},{5,4},{6,7},{7,6},{8,9},{9,8},{10,11... | collective-permute-start | bytes 786440 | tf_op jit(solution)/shard_map/ppermute | solution.py:461
  34.6 1.7 %copy-start = (bf16[256,1024]{1,0:T(8,128)(2,1)S(1)}, bf16[256,1024]{1,0:T(8,128)(2,1)}, u32[]{:S(2)}) copy-start(bf16[256,1024]{1,0:T(8,128)(2,1)} %refs_1_.3) | copy-start | bytes 1572868
  38.2 2.1 %collective-permute-start.12 = (bf16[4,256,256]{2,1,0:T(8,128)(2,1)S(1)}, bf16[4,256,256]{2,1,0:T(8,128)(2,1)S(1)}, u32[]{:S(2)}, u32[]{:S(2)}) collective-permute-start(bf16[4,256,256]{2,1,0:T(8,128)(2,1)S(1)} %get-tuple-element.30), channel_id=1, source_target_pairs={{0,1},{1,0},{2,3},{3,2},{4,5},{5,4},{6,7},{7,6},{8,9},{9,8},{10,11... | collective-permute-start | bytes 1572872 | tf_op jit(solution)/shard_map/ppermute | solution.py:461
  41.2 21.3 %all-to-all-start.1 = ((bf16[4,256,256]{2,1,0:T(8,128)(2,1)}), bf16[4,256,256]{2,1,0:T(8,128)(2,1)S(1)}, u32[]{:S(2)}, u32[]{:S(2)}) async-start(bf16[4,256,256]{2,1,0:T(8,128)(2,1)} %add.1.refs_6_), calls=%async_computation.1 | async-start | bytes 1048576 | tf_op jit(solution)/shard_map/all_to_all | solution.py:465
  46.8 1.6 %collective-permute-start.16 = (bf16[128,1024]{1,0:T(8,128)(2,1)S(1)}, bf16[128,1024]{1,0:T(8,128)(2,1)S(1)}, u32[]{:S(2)}, u32[]{:S(2)}) collective-permute-start(bf16[128,1024]{1,0:T(8,128)(2,1)S(1)} %get-tuple-element.34), channel_id=1, source_target_pairs={{0,1},{1,0},{2,3},{3,2},{4,5},{5,4},{6,7},{7,6},{8,9},{9,8},{10,11... | collective-permute-start | bytes 786440 | tf_op jit(solution)/shard_map/ppermute | solution.py:461
  48.5 4.4 %collective-permute-start.17 = (bf16[32,1024]{1,0:T(8,128)(2,1)S(1)}, bf16[32,1024]{1,0:T(8,128)(2,1)S(1)}, u32[]{:S(2)}, u32[]{:S(2)}) collective-permute-start(bf16[32,1024]{1,0:T(8,128)(2,1)S(1)} %get-tuple-element.36), channel_id=1, source_target_pairs={{0,8},{8,0},{16,24},{24,16},{1,9},{9,1},{17,25},{25,17},{2,10},{10... | collective-permute-start | bytes 196616 | tf_op jit(solution)/shard_map/ppermute | solution.py:455
  50.5 5.0 %collective-permute-start.18 = (bf16[32,1024]{1,0:T(8,128)(2,1)S(1)}, bf16[32,1024]{1,0:T(8,128)(2,1)S(1)}, u32[]{:S(2)}, u32[]{:S(2)}) collective-permute-start(bf16[32,1024]{1,0:T(8,128)(2,1)S(1)} %get-tuple-element.37), channel_id=1, source_target_pairs={{0,16},{8,24},{16,0},{24,8},{1,17},{9,25},{17,1},{25,9},{2,18},{10... | collective-permute-start | bytes 196616 | tf_op jit(solution)/shard_map/ppermute | solution.py:455
  51.0 5.2 %collective-permute-start.19 = (bf16[32,1024]{1,0:T(8,128)(2,1)S(1)}, bf16[32,1024]{1,0:T(8,128)(2,1)S(1)}, u32[]{:S(2)}, u32[]{:S(2)}) collective-permute-start(bf16[32,1024]{1,0:T(8,128)(2,1)S(1)} %get-tuple-element.38), channel_id=1, source_target_pairs={{0,24},{8,16},{16,8},{24,0},{1,25},{9,17},{17,9},{25,1},{2,26},{10... | collective-permute-start | bytes 196616 | tf_op jit(solution)/shard_map/ppermute | solution.py:455
  56.2 9.9 %collective-permute-start.20 = (bf16[32,1024]{1,0:T(8,128)(2,1)S(1)}, bf16[32,1024]{1,0:T(8,128)(2,1)S(1)}, u32[]{:S(2)}, u32[]{:S(2)}) collective-permute-start(bf16[32,1024]{1,0:T(8,128)(2,1)S(1)} %get-tuple-element.40), channel_id=1, source_target_pairs={{0,2},{1,3},{2,0},{3,1},{4,6},{5,7},{6,4},{7,5},{8,10},{9,11},{10,... | collective-permute-start | bytes 196616 | tf_op jit(solution)/shard_map/ppermute | solution.py:458
  58.3 8.4 %collective-permute-start.21 = (bf16[32,1024]{1,0:T(8,128)(2,1)S(1)}, bf16[32,1024]{1,0:T(8,128)(2,1)S(1)}, u32[]{:S(2)}, u32[]{:S(2)}) collective-permute-start(bf16[32,1024]{1,0:T(8,128)(2,1)S(1)} %get-tuple-element.41), channel_id=1, source_target_pairs={{0,4},{1,5},{2,6},{3,7},{4,0},{5,1},{6,2},{7,3},{8,12},{9,13},{10,... | collective-permute-start | bytes 196616 | tf_op jit(solution)/shard_map/ppermute | solution.py:458
  60.7 6.1 %collective-permute-start.22 = (bf16[32,1024]{1,0:T(8,128)(2,1)S(1)}, bf16[32,1024]{1,0:T(8,128)(2,1)S(1)}, u32[]{:S(2)}, u32[]{:S(2)}) collective-permute-start(bf16[32,1024]{1,0:T(8,128)(2,1)S(1)} %get-tuple-element.42), channel_id=1, source_target_pairs={{0,6},{1,7},{2,4},{3,5},{4,2},{5,3},{6,0},{7,1},{8,14},{9,15},{10,... | collective-permute-start | bytes 196616 | tf_op jit(solution)/shard_map/ppermute | solution.py:458
  62.5 9.3 %copy-start.2 = (f32[256,1024]{1,0:T(8,128)S(1)}, f32[256,1024]{1,0:T(8,128)}, u32[]{:S(2)}) copy-start(f32[256,1024]{1,0:T(8,128)} %refs_0_.5) | copy-start | bytes 3145732
  62.6 7.5 %collective-permute-start.15 = (bf16[256,256]{1,0:T(8,128)(2,1)S(1)}, bf16[256,256]{1,0:T(8,128)(2,1)S(1)}, u32[]{:S(2)}, u32[]{:S(2)}) collective-permute-start(bf16[256,256]{1,0:T(8,128)(2,1)S(1)} %sum_rows.1.refs_2_.refs_4_), channel_id=1, source_target_pairs={{0,24},{8,16},{16,8},{24,0},{1,25},{9,17},{17,9},{25,1},{2,26},{10... | collective-permute-start | bytes 393224 | tf_op jit(solution)/shard_map/ppermute | solution.py:455
  66.0 5.8 %collective-permute-start.14 = (bf16[256,256]{1,0:T(8,128)(2,1)S(1)}, bf16[256,256]{1,0:T(8,128)(2,1)S(1)}, u32[]{:S(2)}, u32[]{:S(2)}) collective-permute-start(bf16[256,256]{1,0:T(8,128)(2,1)S(1)} %sum_rows.1.refs_2_.refs_4_), channel_id=1, source_target_pairs={{0,16},{8,24},{16,0},{24,8},{1,17},{9,25},{17,1},{25,9},{2,18},{10... | collective-permute-start | bytes 393224 | tf_op jit(solution)/shard_map/ppermute | solution.py:455
  66.1 5.8 %collective-permute-start.13 = (bf16[256,256]{1,0:T(8,128)(2,1)S(1)}, bf16[256,256]{1,0:T(8,128)(2,1)S(1)}, u32[]{:S(2)}, u32[]{:S(2)}) collective-permute-start(bf16[256,256]{1,0:T(8,128)(2,1)S(1)} %sum_rows.1.refs_2_.refs_4_), channel_id=1, source_target_pairs={{0,8},{8,0},{16,24},{24,16},{1,9},{9,1},{17,25},{25,17},{2,10},{10... | collective-permute-start | bytes 393224 | tf_op jit(solution)/shard_map/ppermute | solution.py:455
  66.8 5.1 %copy-start.9 = (f32[256]{0:T(256)S(1)}, f32[256]{0:T(256)}, u32[]{:S(2)}) copy-start(f32[256]{0:T(256)} %param.10) | copy-start | bytes 3076
  66.8 6.4 %collective-permute-start.25 = (bf16[32,1024]{1,0:T(8,128)(2,1)S(1)}, bf16[32,1024]{1,0:T(8,128)(2,1)S(1)}, u32[]{:S(2)}, u32[]{:S(2)}) collective-permute-start(bf16[32,1024]{1,0:T(8,128)(2,1)S(1)} %sum_parts.1.refs_0_), channel_id=1, source_target_pairs={{0,24},{8,16},{16,8},{24,0},{1,25},{9,17},{17,9},{25,1},{2,26},{10... | collective-permute-start | bytes 196616 | tf_op jit(solution)/shard_map/ppermute | solution.py:455
  69.7 4.3 %collective-permute-start.24 = (bf16[32,1024]{1,0:T(8,128)(2,1)S(1)}, bf16[32,1024]{1,0:T(8,128)(2,1)S(1)}, u32[]{:S(2)}, u32[]{:S(2)}) collective-permute-start(bf16[32,1024]{1,0:T(8,128)(2,1)S(1)} %sum_parts.1.refs_0_), channel_id=1, source_target_pairs={{0,16},{8,24},{16,0},{24,8},{1,17},{9,25},{17,1},{25,9},{2,18},{10... | collective-permute-start | bytes 196616 | tf_op jit(solution)/shard_map/ppermute | solution.py:455
  70.0 4.3 %collective-permute-start.23 = (bf16[32,1024]{1,0:T(8,128)(2,1)S(1)}, bf16[32,1024]{1,0:T(8,128)(2,1)S(1)}, u32[]{:S(2)}, u32[]{:S(2)}) collective-permute-start(bf16[32,1024]{1,0:T(8,128)(2,1)S(1)} %sum_parts.1.refs_0_), channel_id=1, source_target_pairs={{0,8},{8,0},{16,24},{24,16},{1,9},{9,1},{17,25},{25,17},{2,10},{10... | collective-permute-start | bytes 196616 | tf_op jit(solution)/shard_map/ppermute | solution.py:455
  73.2 1.1 %copy-start.5 = (f32[1,256]{1,0:T(1,128)S(1)}, f32[1,256]{1,0:T(1,128)}, u32[]{:S(2)}) copy-start(f32[1,256]{1,0:T(1,128)} %get-tuple-element.32.refs_4_) | copy-start | bytes 3076
